TPU v7x, 32 devices: a whole 2x2x4 slice. The times are simulated.
32 devices in a mesh: dp: 4 (over y, x), ctx: 8 (over z, core).
Axes of the slice: x: 2, y: 2, z: 4, core: 2. Of those that a mesh axis runs over, the one named last changes fastest.
Arguments:
- inputs: bfloat16 [4, 1024, 2048], P('dp', 'ctx'), may hold values from -6 to 6
- attn_gain: bfloat16 [2048], P('dp'), may hold values from 0.25 to 1.75
- w_query: bfloat16 [2048, 2048], P('dp'), may hold values from -0.125 to 0.125
- w_key: bfloat16 [2048, 512], P('dp'), may hold values from -0.125 to 0.125
- w_value: bfloat16 [2048, 512], P('dp'), may hold values from -0.125 to 0.125
- q_gain: bfloat16 [64], replicated, may hold values from 0.25 to 1.75
- key_norm_gain: bfloat16 [64], replicated, may hold values from 0.25 to 1.75
- w_out: bfloat16 [2048, 2048], P('dp'), may hold values from -1.75 to 1.75
- ffn_gain: bfloat16 [2048], P('dp'), may hold values from 0.25 to 1.75
- w_gate: bfloat16 [2048, 8192], P('dp'), may hold values from -0.125 to 0.125
- w_up: bfloat16 [2048, 8192], P('dp'), may hold values from -0.125 to 0.125
- w_down: bfloat16 [8192, 2048], P('dp'), may hold values from -0.109375 to 0.109375
- stretch_map: int32 [16], replicated, may hold values from 0 to 15, as said below
- pos_ids: int32 [4, 1024], P('dp', 'ctx'), may hold values from 0 to 1791, as said below
- cotangent: bfloat16 [4, 1024, 2048], P('dp', 'ctx'), may hold values from -6 to 6
Outputs:
- output: bfloat16 [4, 1024, 2048], P('dp', 'ctx')
- input_grad: bfloat16 [4, 1024, 2048], P('dp', 'ctx')
- attn_gain_grad: float32 [2048], P('dp')
- w_query_grad: float32 [2048, 2048], P('dp')
- w_key_grad: float32 [2048, 512], P('dp')
- w_value_grad: float32 [2048, 512], P('dp')
- q_gain_grad: float32 [64], replicated
- k_gain_grad: float32 [64], replicated
- w_out_grad: float32 [2048, 2048], P('dp')
- ffn_gain_grad: float32 [2048], P('dp')
- w_gate_grad: float32 [2048, 8192], P('dp')
- w_up_grad: float32 [2048, 8192], P('dp')
- w_down_grad: float32 [8192, 2048], P('dp')
Inputs may be any that keep to these rules, and one draw needn't show every extreme that they name: Stored block b of 64 rows holds stretch stretch_map[b]; the map is a permutation, and blocks 2 i and 2 i + 1 hold stretches that add up to 15. pos_ids[s, r] is stretch_map[r // 64] * 64 + r % 64 plus an offset of sequence s; the offsets are distinct multiples of 256.
All inputs are finite; a program needn't handle non-finite values.
Results may differ from a plain program's by a relative error of at most 0.025.
Values may be sent and summed in bfloat16 or wider, within the bound.
A program may use at most 1 GiB of HBM per device.

v0:
```python
from functools import partial

import jax
import jax.numpy as jnp
from jax import lax
from jax.sharding import PartitionSpec as P

NORM_EPSILON = 1e-05
ROPE_BASE = 1000000.0
MASKED_SCORE = -1e30


def contract_rows(left, right):
    return lax.dot_general(
        left, right, (((0,), (0,)), ((), ())), preferred_element_type=jnp.float32
    )


def contract_cols(left, right):
    return lax.dot_general(
        left, right, (((1,), (1,)), ((), ())), preferred_element_type=jnp.float32
    )


def normalize(values):
    inverse = lax.rsqrt(jnp.mean(values * values, axis=-1, keepdims=True) + NORM_EPSILON)
    return (values * inverse, inverse)


def normalize_back(grad_hat, scaled, inverse):
    return inverse * (grad_hat - scaled * jnp.mean(grad_hat * scaled, axis=-1, keepdims=True))


def apply_rotary(values, cosine, sine_table):
    middle = values.shape[-1] // 2
    first_half = values[..., :middle]
    second_half = values[..., middle:]
    return jnp.concatenate(
        [
            first_half * cosine - second_half * sine_table,
            second_half * cosine + first_half * sine_table,
        ],
        axis=-1,
    )


def rotate_back(grad_values, cosine, sine_table):
    middle = grad_values.shape[-1] // 2
    first_half = grad_values[..., :middle]
    second_half = grad_values[..., middle:]
    return jnp.concatenate(
        [
            first_half * cosine + second_half * sine_table,
            second_half * cosine - first_half * sine_table,
        ],
        axis=-1,
    )


def round_keep(values):
    return lax.optimization_barrier(values.astype(jnp.bfloat16)).astype(jnp.float32)


def masked_scores(query_rows, key_rows, query_places, key_places, score_scale):
    scores = contract_cols(query_rows, key_rows) * score_scale
    allowed = key_places[None, :] <= query_places[:, None]
    return jnp.where(allowed, scores, MASKED_SCORE)


def attend_head(operands, query_places, key_places, score_scale):
    query_rows, key_rows, value_rows = operands
    scores = masked_scores(query_rows, key_rows, query_places, key_places, score_scale)
    top_score = jnp.max(scores, axis=-1, keepdims=True)
    weights = jnp.exp(scores - top_score)
    weight_sum = jnp.sum(weights, axis=-1, keepdims=True)
    softmax_probs = (weights / weight_sum).astype(jnp.bfloat16)
    mixed_rows = jnp.dot(softmax_probs, value_rows, preferred_element_type=jnp.float32)
    return (mixed_rows, (top_score + jnp.log(weight_sum))[:, 0])


def attend_back(operands, query_places, key_places, score_scale):
    query_rows, key_rows, value_rows, grad_rows, log_total = operands
    scores = masked_scores(query_rows, key_rows, query_places, key_places, score_scale)
    softmax_probs = jnp.exp(scores - log_total[:, None])
    grad_probs = contract_cols(grad_rows, value_rows)
    inner_sum = jnp.sum(softmax_probs * grad_probs, axis=-1, keepdims=True)
    grad_scores = (softmax_probs * (grad_probs - inner_sum)).astype(jnp.bfloat16)
    grad_query = jnp.dot(grad_scores, key_rows, preferred_element_type=jnp.float32) * score_scale
    grad_key = contract_rows(grad_scores, query_rows) * score_scale
    grad_value = contract_rows(softmax_probs.astype(jnp.bfloat16), grad_rows)
    return (grad_query, grad_key, grad_value)


def local(
    inputs,
    attn_gain,
    w_query,
    w_key,
    w_value,
    q_gain,
    key_norm_gain,
    w_out,
    ffn_gain,
    w_gate,
    w_up,
    w_down,
    stretch_map,
    pos_ids,
    cotangent,
):
    row_count = inputs.shape[1]
    model_width = inputs.shape[2]
    head_dim = q_gain.shape[0]
    query_width = w_query.shape[1]
    key_width = w_key.shape[1]
    hidden_units = w_gate.shape[1]
    query_heads = query_width // head_dim
    key_heads = key_width // head_dim
    heads_per_group = query_heads // key_heads
    ratio_down = hidden_units // model_width
    half_rows = row_count // 2
    stretch_count = stretch_map.shape[0]
    ctx_count = lax.axis_size("ctx")
    key_length = row_count * ctx_count
    score_scale = head_dim ** (-0.5)
    local_index = jnp.arange(row_count, dtype=jnp.int32)
    own_blocks = 2 * lax.axis_index("ctx") + local_index // half_rows
    block_ids = jnp.arange(stretch_count, dtype=jnp.int32)
    picked = jnp.where(block_ids[None, :] == own_blocks[:, None], stretch_map[None, :], 0)
    query_places = jnp.sum(picked, axis=1) * half_rows + local_index % half_rows
    key_places = jnp.repeat(
        stretch_map, half_rows, total_repeat_length=key_length
    ) * half_rows + jnp.tile(jnp.arange(half_rows, dtype=jnp.int32), stretch_count)
    group_places = jnp.tile(query_places, heads_per_group)
    steps_half = jnp.arange(head_dim // 2, dtype=jnp.float32)
    frequency = jnp.power(jnp.float32(ROPE_BASE), -2.0 * steps_half / head_dim)
    rotary_angles = pos_ids[0].astype(jnp.float32)[:, None] * frequency[None, :]
    cosine = jnp.cos(rotary_angles)[:, None, :]
    sine_table = jnp.sin(rotary_angles)[:, None, :]
    inputs_f = inputs[0].astype(jnp.float32)
    hat_one, inverse_one = normalize(inputs_f)
    gain_piece = lax.all_gather(attn_gain, "dp", axis=0, tiled=True)
    piece_query = lax.all_gather(w_query, "dp", axis=0, tiled=True)
    piece_key = lax.all_gather(w_key, "dp", axis=0, tiled=True)
    piece_value = lax.all_gather(w_value, "dp", axis=0, tiled=True)
    columns = (hat_one * gain_piece.astype(jnp.float32)[None, :]).astype(jnp.bfloat16)
    gain_full = gain_piece
    query_pre = jnp.dot(columns, piece_query, preferred_element_type=jnp.float32)
    key_before_norm = jnp.dot(columns, piece_key, preferred_element_type=jnp.float32)
    value_pre = jnp.dot(columns, piece_value, preferred_element_type=jnp.float32)
    gain_one = gain_full
    gain_one_f = gain_one.astype(jnp.float32)
    normed_one = (hat_one * gain_one_f).astype(jnp.bfloat16)
    q_gain_f = q_gain.astype(jnp.float32)
    k_gain_f = key_norm_gain.astype(jnp.float32)
    query_hat, query_inverse = normalize(query_pre.reshape(row_count, query_heads, head_dim))
    query_rot = apply_rotary(query_hat * q_gain_f, cosine, sine_table).astype(jnp.bfloat16)
    key_hat, key_inverse = normalize(key_before_norm.reshape(row_count, key_heads, head_dim))
    key_rot = apply_rotary(key_hat * k_gain_f, cosine, sine_table).astype(jnp.bfloat16)
    value_low = value_pre.astype(jnp.bfloat16)
    key_all, value_all = (
        lax.all_gather(key_rot.reshape(row_count, key_width), "ctx", axis=0, tiled=True),
        lax.all_gather(value_low, "ctx", axis=0, tiled=True),
    )
    query_grouped = (
        query_rot.reshape(row_count, key_heads, heads_per_group, head_dim)
        .transpose(1, 2, 0, 3)
        .reshape(key_heads, heads_per_group * row_count, head_dim)
    )
    key_grouped = key_all.reshape(key_length, key_heads, head_dim).transpose(1, 0, 2)
    value_grouped = value_all.reshape(key_length, key_heads, head_dim).transpose(1, 0, 2)
    head_mixed, log_total = lax.map(
        partial(
            attend_head, query_places=group_places, key_places=key_places, score_scale=score_scale
        ),
        (query_grouped, key_grouped, value_grouped),
    )
    mixed_rows = (
        head_mixed.reshape(key_heads, heads_per_group, row_count, head_dim)
        .transpose(2, 0, 1, 3)
        .reshape(row_count, query_width)
    )
    mixed_low = mixed_rows.astype(jnp.bfloat16)
    piece = lax.all_gather(w_out, "dp", axis=0, tiled=True)
    span = piece.shape[0]
    attention_out = jnp.zeros((row_count, model_width), jnp.float32) + jnp.dot(
        lax.slice_in_dim(mixed_low, 0, span, axis=1), piece, preferred_element_type=jnp.float32
    )
    hidden_in = inputs_f + attention_out
    hat_two, inverse_two = normalize(hidden_in)
    sum_gate = jnp.zeros((row_count, hidden_units), jnp.float32)
    sum_up = jnp.zeros((row_count, hidden_units), jnp.float32)
    gain_piece = lax.all_gather(ffn_gain, "dp", axis=0, tiled=True)
    piece_gate = lax.all_gather(w_gate, "dp", axis=0, tiled=True)
    piece_up = lax.all_gather(w_up, "dp", axis=0, tiled=True)
    span = piece_gate.shape[0]
    columns = (
        lax.slice_in_dim(hat_two, 0, span, axis=1) * gain_piece.astype(jnp.float32)[None, :]
    ).astype(jnp.bfloat16)
    gain_full = gain_piece
    gate_pre = sum_gate + jnp.dot(columns, piece_gate, preferred_element_type=jnp.float32)
    up_pre = sum_up + jnp.dot(columns, piece_up, preferred_element_type=jnp.float32)
    gain_two_f = gain_full.astype(jnp.float32)
    normed_two = (hat_two * gain_two_f).astype(jnp.bfloat16)
    gate_sig = jax.nn.sigmoid(gate_pre)
    gate_act = gate_pre * gate_sig
    act_low = (gate_act * up_pre).astype(jnp.bfloat16)
    piece = lax.all_gather(w_down, "dp", axis=0, tiled=True)
    span = piece.shape[0]
    ffn_out = jnp.zeros((row_count, model_width), jnp.float32) + jnp.dot(
        lax.slice_in_dim(act_low, 0, span, axis=1), piece, preferred_element_type=jnp.float32
    )
    output = (hidden_in + ffn_out).astype(jnp.bfloat16)[None]
    cot_low = cotangent[0]
    grad_act = contract_cols(cot_low, lax.all_gather(w_down, "dp", axis=0, tiled=True))
    grad_gate = (grad_act * up_pre * gate_sig * (1.0 + gate_pre * (1.0 - gate_sig))).astype(
        jnp.bfloat16
    )
    grad_up = (grad_act * gate_act).astype(jnp.bfloat16)
    piece_gate = lax.all_gather(w_gate, "dp", axis=0, tiled=True)
    piece_up = lax.all_gather(w_up, "dp", axis=0, tiled=True)
    column_part = contract_cols(grad_gate, piece_gate) + contract_cols(grad_up, piece_up)
    grad_normed_two = lax.dynamic_update_slice_in_dim(
        jnp.zeros((row_count, model_width), jnp.float32), column_part, jnp.int32(0), 1
    )
    gain_grad_two = jnp.sum(grad_normed_two * hat_two, axis=0)
    grad_hidden = cot_low.astype(jnp.float32) + normalize_back(
        grad_normed_two * gain_two_f, hat_two, inverse_two
    )
    grad_hidden_low = grad_hidden.astype(jnp.bfloat16)
    grad_mixed = contract_cols(grad_hidden_low, lax.all_gather(w_out, "dp", axis=0, tiled=True))
    grad_mixed_low = grad_mixed.astype(jnp.bfloat16)
    grad_grouped = (
        grad_mixed_low.reshape(row_count, key_heads, heads_per_group, head_dim)
        .transpose(1, 2, 0, 3)
        .reshape(key_heads, heads_per_group * row_count, head_dim)
    )
    grad_q_heads, grad_k_heads, grad_v_heads = lax.map(
        partial(
            attend_back, query_places=group_places, key_places=key_places, score_scale=score_scale
        ),
        (query_grouped, key_grouped, value_grouped, grad_grouped, log_total),
    )
    grad_query_rot = round_keep(
        grad_q_heads.reshape(key_heads, heads_per_group, row_count, head_dim)
        .transpose(2, 0, 1, 3)
        .reshape(row_count, query_heads, head_dim)
    )
    key_grad_all = grad_k_heads.transpose(1, 0, 2).reshape(key_length, key_width)
    value_grad_all = grad_v_heads.transpose(1, 0, 2).reshape(key_length, key_width)
    key_grad, value_grad = (
        lax.psum_scatter(
            key_grad_all.astype(jnp.bfloat16), "ctx", scatter_dimension=0, tiled=True
        ).astype(jnp.float32),
        lax.psum_scatter(
            value_grad_all.astype(jnp.bfloat16), "ctx", scatter_dimension=0, tiled=True
        ).astype(jnp.float32),
    )
    grad_value_low = value_grad.astype(jnp.bfloat16)
    grad_key_rot = round_keep(key_grad.reshape(row_count, key_heads, head_dim))
    grad_query_gained = rotate_back(grad_query_rot, cosine, sine_table)
    q_gain_grad = jnp.sum(grad_query_gained * query_hat, axis=(0, 1))
    grad_query_pre = (
        normalize_back(grad_query_gained * q_gain_f, query_hat, query_inverse)
        .reshape(row_count, query_width)
        .astype(jnp.bfloat16)
    )
    grad_key_gained = rotate_back(grad_key_rot, cosine, sine_table)
    k_gain_grad = jnp.sum(grad_key_gained * key_hat, axis=(0, 1))
    grad_key_pre = (
        normalize_back(grad_key_gained * k_gain_f, key_hat, key_inverse)
        .reshape(row_count, key_width)
        .astype(jnp.bfloat16)
    )
    piece_query = lax.all_gather(w_query, "dp", axis=0, tiled=True)
    piece_key = lax.all_gather(w_key, "dp", axis=0, tiled=True)
    piece_value = lax.all_gather(w_value, "dp", axis=0, tiled=True)
    column_part = (
        contract_cols(grad_query_pre, piece_query)
        + contract_cols(grad_key_pre, piece_key)
        + contract_cols(grad_value_low, piece_value)
    )
    grad_normed_one = lax.dynamic_update_slice_in_dim(
        jnp.zeros((row_count, model_width), jnp.float32), column_part, jnp.int32(0), 1
    )
    gain_grad_one = jnp.sum(grad_normed_one * hat_one, axis=0)
    grad_inputs = grad_hidden + normalize_back(grad_normed_one * gain_one_f, hat_one, inverse_one)
    input_grad = grad_inputs.astype(jnp.bfloat16)[None]
    repeats = model_width // head_dim
    gain_columns = jnp.stack(
        [
            gain_grad_one,
            gain_grad_two,
            jnp.tile(q_gain_grad, repeats),
            jnp.tile(k_gain_grad, repeats),
        ],
        axis=1,
    )
    gain_table = jnp.concatenate([gain_columns, jnp.zeros((model_width, 124), jnp.float32)], axis=1)
    grad_qkv = jnp.concatenate([grad_query_pre, grad_key_pre, grad_value_low], axis=1)
    grad_ffn = jnp.concatenate([grad_gate, grad_up], axis=1)
    start = jnp.int32(0)
    count = model_width // lax.axis_size("dp") * lax.axis_size("dp")
    mixed_part = lax.dynamic_slice_in_dim(mixed_low, start, count, 1)
    second_part = lax.dynamic_slice_in_dim(normed_two, start, count, 1)
    act_part = lax.dynamic_slice_in_dim(act_low, start * ratio_down, count * ratio_down, 1)
    gains_part = lax.dynamic_slice_in_dim(gain_table, start, count, 0)
    down_part = contract_rows(act_part, cot_low).reshape(count, ratio_down * model_width)
    shard = lax.psum_scatter(
        jnp.concatenate(
            [
                contract_rows(normed_one, grad_qkv),
                contract_rows(mixed_part, grad_hidden_low),
                contract_rows(second_part, grad_ffn),
                down_part,
                gains_part,
            ],
            axis=1,
        ).astype(jnp.bfloat16),
        "dp",
        scatter_dimension=0,
        tiled=True,
    ).astype(jnp.float32)
    shard = lax.psum(shard.astype(jnp.bfloat16), "ctx").astype(jnp.float32)
    shard_rows = shard.shape[0]
    edge_key = query_width + key_width
    edge_value = edge_key + key_width
    edge_out = edge_value + model_width
    edge_gate = edge_out + hidden_units
    edge_up = edge_gate + hidden_units
    edge_down = edge_up + ratio_down * model_width
    w_query_grad = shard[:, :query_width]
    w_key_grad = shard[:, query_width:edge_key]
    w_value_grad = shard[:, edge_key:edge_value]
    w_out_grad = shard[:, edge_value:edge_out]
    w_gate_grad = shard[:, edge_out:edge_gate]
    w_up_grad = shard[:, edge_gate:edge_up]
    w_down_grad = shard[:, edge_up:edge_down].reshape(shard_rows * ratio_down, model_width)
    attn_gain_grad = shard[:, edge_down]
    ffn_gain_grad = shard[:, edge_down + 1]
    q_gain_out = shard[:head_dim, edge_down + 2]
    k_gain_out = shard[:head_dim, edge_down + 3]
    return (
        output,
        input_grad,
        attn_gain_grad,
        w_query_grad,
        w_key_grad,
        w_value_grad,
        q_gain_out,
        k_gain_out,
        w_out_grad,
        ffn_gain_grad,
        w_gate_grad,
        w_up_grad,
        w_down_grad,
    )


def solution(mesh):
    in_specs = (
        P("dp", "ctx", None),
        P("dp"),
        P("dp", None),
        P("dp", None),
        P("dp", None),
        P(),
        P(),
        P("dp", None),
        P("dp"),
        P("dp", None),
        P("dp", None),
        P("dp", None),
        P(),
        P("dp", "ctx"),
        P("dp", "ctx", None),
    )
    out_specs = (
        P("dp", "ctx", None),
        P("dp", "ctx", None),
        P("dp"),
        P("dp", None),
        P("dp", None),
        P("dp", None),
        P(),
        P(),
        P("dp", None),
        P("dp"),
        P("dp", None),
        P("dp", None),
        P("dp", None),
    )
    return jax.shard_map(local, mesh=mesh, in_specs=in_specs, out_specs=out_specs, check_vma=False)
```

profile of v0, /device:TPU:0, one launch (start us, length us, event | category | flops | bytes accessed | tf_op | source)
XLA Modules:
  0.0 3446.4 jit_solution(8006155186594751028)
XLA Ops:
  9.4 9.5 all-gather
  20.2 27.7 all-gather.18.cloned.1.call-done
  51.1 34.0 all-gather.14.cloned.1.call-done
  96.5 8.0 all-gather.1
  112.7 22.4 all-gather.16.cloned.1.call-done
  137.8 85.2 %all-gather.12.cloned.1.call-done = bf16[2048,2048]{1,0:T(8,128)(2,1)} async-done(((bf16[512,2048]{1,0:T(8,128)(2,1)}), bf16[2048,2048]{1,0:T(8,128)(2,1)}) %all-gather.12.cloned.1.call-update) | async-done | bytes 8388624 | tf_op jit(solution)/shard_map/all_gather | solution.py:143
  223.0 12.3 copy.86
  242.6 114.4 %while.29 = (s32[]{:T(128)}, bf16[8,512,64]{1,2,0:T(8,128)(2,1)S(1)}, f32[8,512]{1,0:T(8,128)S(1)}, bf16[8,512,64]{2,1,0:T(8,128)(2,1)S(1)}, bf16[8,1024,64]{2,1...) while((s32[]{:T(128)}, ...), condition=%wide.region_7.8_spmd.clone, body=%wide.region_4.7_spmd.clone.sunk | while | flops 138982912 | bytes 7189369 | solution.py:172
  364.2 247.3 %all-gather.26.cloned.1.call-done = bf16[2048,8192]{1,0:T(8,128)(2,1)} async-done(((bf16[512,8192]{1,0:T(8,128)(2,1)}), bf16[2048,8192]{1,0:T(8,128)(2,1)}) %all-gather.26.cloned.1.call-update) | async-done | bytes 33554448 | tf_op jit(solution)/shard_map/all_gather | solution.py:195
  611.4 19.9 fusion.94
  631.3 279.2 %all-gather.24.cloned.1.call-done = bf16[2048,8192]{1,0:T(8,128)(2,1)} async-done(((bf16[512,8192]{1,0:T(8,128)(2,1)}), bf16[2048,8192]{1,0:T(8,128)(2,1)}) %all-gather.24.cloned.1.call-update) | async-done | bytes 33554448 | tf_op jit(solution)/shard_map/all_gather | solution.py:194
  910.5 19.9 fusion.93
  930.4 279.2 %all-gather.28.cloned.1.call-done = bf16[8192,2048]{1,0:T(8,128)(2,1)} async-done(((bf16[2048,2048]{1,0:T(8,128)(2,1)}), bf16[8192,2048]{1,0:T(8,128)(2,1)}) %all-gather.28.cloned.1.call-update) | async-done | bytes 33554448 | tf_op jit(solution)/shard_map/all_gather | solution.py:208
  1209.6 21.4 multiply_convert_fusion.1
  1231.0 27.4 convolution_convert_fusion
  1258.4 16.3 fusion.95
  1274.7 17.9 multiply_reduce_fusion.2
  1303.8 147.0 %while.30 = (s32[]{:T(128)}, bf16[8,512,64]{1,2,0:T(8,128)(2,1)S(1)}, bf16[8,1024,64]{1,2,0:T(8,128)(2,1)}, bf16[8,1024,64]{1,2,0:T(8,128)(2,1)}, bf16[8,512,64]...) while((s32[]{:T(128)}, ...), condition=%wide.region_12.13_spmd.clone, body=%wide.region_10.12_spmd.clone.sunk | while | flops 340932096 | bytes 17799048 | solution.py:238
  1458.6 12.4 copy.99
  1471.0 15.5 convolution_convert_fusion.1
  1486.5 55.1 %reshape.362 = bf16[2048,8192]{1,0:T(8,128)(2,1)} reshape(bf16[8192,2048]{1,0:T(8,128)(2,1)} %convolution_convert_fusion.1) | data formatting | bytes 67108864 | tf_op jit(solution)/shard_map/reshape | solution.py:308
  1542.0 6.3 fusion.96
  1555.2 18.9 reduce-scatter.12.cloned.1.call-done
  1578.2 7.8 convolution_convert_fusion.2
  1586.1 174.0 %concatenate.41 = bf16[2048,29824]{1,0:T(8,128)(2,1)} concatenate(bf16[2048,3072]{1,0:T(8,128)(2,1)} %convolution_convert_fusion.2, bf16[2048,2048]{1,0:T(8,128)(2,1)} %copy.99, bf16[2048,16384]{1,0:T(8,128)(2,1)} %convolution_convert_fusion, bf16[2048,8192]{1,0:T(8,128)(2,1)} %reshape.362, bf16[2048,1]{1,0:T(8,128)(2,1)} %stack.10, bf16[2048,1]{1,0:T(8,128)(2,1)S(1)} %stack.11, ...), dimensions={1} | concatenate | bytes 244318208 | tf_op jit(solution)/shard_map/concatenate | solution.py:310
  1760.4 999.8 %reduce-scatter.8.cloned.1.call-done = bf16[512,29824]{1,0:T(8,128)(2,1)} async-done(((bf16[2048,29824]{1,0:T(8,128)(2,1)}), bf16[512,29824]{1,0:T(8,128)(2,1)}) %reduce-scatter.8.cloned.1.call-update) | async-done | bytes 30539792 | tf_op jit(solution)/shard_map/reduce_scatter | solution.py:309
  2761.4 18.0 fusion.49
  2780.5 573.8 %all-reduce.2.cloned.1.call-done = bf16[512,29824]{1,0:T(8,128)(2,1)} async-done(((bf16[512,29824]{1,0:T(8,128)(2,1)}), bf16[512,29824]{1,0:T(8,128)(2,1)}) %all-reduce.2.cloned.1.call-update) | async-done | bytes 30539792 | tf_op jit(solution)/shard_map/psum | solution.py:324
  3354.3 29.7 convert_element_type.208
  3387.5 23.4 fusion.89
  3410.9 19.0 reshape.363
  3432.8 6.7 fusion.90
  (373 shorter events, 342.5 us)
Async XLA Ops:
  7.2 43.7 %copy-start.24 = (bf16[64]{0:T(256)(128)(2,1)S(1)}, bf16[64]{0:T(256)(128)(2,1)}, u32[]{:S(2)}) copy-start(bf16[64]{0:T(256)(128)(2,1)} %param.27) | copy-start | bytes 388
  7.2 43.8 %copy-start.25 = (s32[1,128]{1,0:T(1,128)S(1)}, s32[1,128]{1,0:T(1,128)}, u32[]{:S(2)}) copy-start(s32[1,128]{1,0:T(1,128)} %param.34) | copy-start | bytes 1540
  7.2 40.7 %all-gather.18.cloned.1.call-start = ((), (), s32[]{:S(2)}) async-start(), calls=%async_computation.6 | async-start | bytes 2621440 | tf_op jit(solution)/shard_map/all_gather | solution.py:145
  7.9 81.1 %copy-start.2 = (bf16[1,128,2048]{2,1,0:T(8,128)(2,1)S(1)}, bf16[1,128,2048]{2,1,0:T(8,128)(2,1)}, u32[]{:S(2)}) copy-start(bf16[1,128,2048]{2,1,0:T(8,128)(2,1)} %param.21) | copy-start | bytes 1572868
  7.9 77.2 %all-gather.14.cloned.1.call-start = ((), (), s32[]{:S(2)}) async-start(), calls=%async_computation.4 | async-start | bytes 2621440 | tf_op jit(solution)/shard_map/all_gather | solution.py:144
  8.7 100.7 %all-gather.20.cloned.1.call-start = ((), (), s32[]{:S(2)}) async-start(), calls=%async_computation.7 | async-start | bytes 1179648 | tf_op jit(solution)/shard_map/all_gather | solution.py:163
  18.9 216.4 %copy-start.14 = (f32[4,1,512]{2,1,0:T(1,128)}, f32[4,1,512]{2,1,0:T(1,128)S(1)}, u32[]{:S(2)}) copy-start(f32[4,1,512]{2,1,0:T(1,128)S(1)} %convert_element_type.210) | copy-start | bytes 24580
  20.2 215.1 %copy-start.19 = (f32[128]{0:T(128)}, f32[128]{0:T(128)S(1)}, u32[]{:S(2)}) copy-start(f32[128]{0:T(128)S(1)} %add_rsqrt_fusion.3) | copy-start | bytes 1540
  50.9 84.2 %all-gather.16.cloned.1.call-start = ((), (), s32[]{:S(2)}) async-start(), calls=%async_computation.5 | async-start | bytes 1179648 | tf_op jit(solution)/shard_map/all_gather | solution.py:162
  50.9 42.0 %copy-start.21 = (f32[64]{0:T(128)}, f32[64]{0:T(128)S(1)}, u32[]{:S(2)}) copy-start(f32[64]{0:T(128)S(1)} %convert_element_type.173) | copy-start | bytes 772
  93.0 130.1 %all-gather.12.cloned.1.call-start = ((), (), s32[]{:S(2)}) async-start(), calls=%async_computation.3 | async-start | bytes 10485760 | tf_op jit(solution)/shard_map/all_gather | solution.py:143
  93.5 265.7 %all-gather.22.cloned.1.call-start = ((), (), s32[]{:S(2)}) async-start(), calls=%async_computation.8 | async-start | bytes 10485760 | tf_op jit(solution)/shard_map/all_gather | solution.py:184
  94.1 517.3 %all-gather.26.cloned.1.call-start = ((), (), s32[]{:S(2)}) async-start(), calls=%async_computation.10 | async-start | bytes 41943040 | tf_op jit(solution)/shard_map/all_gather | solution.py:195
  94.9 815.7 %all-gather.24.cloned.1.call-start = ((), (), s32[]{:S(2)}) async-start(), calls=%async_computation.9 | async-start | bytes 41943040 | tf_op jit(solution)/shard_map/all_gather | solution.py:194
  95.6 8.9 copy-start.16
  95.7 1114.0 %all-gather.28.cloned.1.call-start = ((), (), s32[]{:S(2)}) async-start(), calls=%async_computation.11 | async-start | bytes 41943040 | tf_op jit(solution)/shard_map/all_gather | solution.py:208
  96.4 1452.0 %reduce-scatter.10.cloned.1.call-start = ((), (), s32[]{:S(2)}) async-start(), calls=%async_computation.14 | async-start | bytes 1179648
  364.0 928.6 %copy-start = (f32[128,2048]{1,0:T(8,128)}, f32[128,2048]{1,0:T(8,128)S(1)}, u32[]{:S(2)}) copy-start(f32[128,2048]{1,0:T(8,128)S(1)} %get-tuple-element.665) | copy-start | bytes 3145732
  1274.7 17.9 copy-start.10
  1292.6 7.5 slice-start
  1453.5 120.6 %reduce-scatter.12.cloned.1.call-start = ((), (), s32[]{:S(2)}) async-start(), calls=%async_computation.15 | async-start | bytes 1179648
  1458.6 12.4 copy-start.11
  1541.6 1218.5 %reduce-scatter.8.cloned.1.call-start = ((), (), s32[]{:S(2)}) async-start(), calls=%async_computation.12 | async-start | bytes 152698880 | tf_op jit(solution)/shard_map/reduce_scatter | solution.py:309
  1542.0 7.6 copy-start.8
  1542.0 7.6 copy-start.18
  1542.0 7.6 copy-start.22
  1548.4 25.7 copy-start.3
  1548.4 25.7 copy-start.15
  1548.4 25.7 copy-start.20
  1578.2 7.8 copy-start.9
  1760.1 1594.3 %all-reduce.2.cloned.1.call-start = ((), (), s32[]{:S(2)}) async-start(), calls=%async_computation.13 | async-start | bytes 61079552 | tf_op jit(solution)/shard_map/psum | solution.py:324
  2761.4 18.0 copy-start.5
  (10 other events, 23.3 us)
Sparse Core Ops, SparseCore 0:
  9.9 38.0 all-gather.17
  49.8 35.2 all-gather.13
  87.3 22.0 all-gather.19
  111.4 23.5 all-gather.15
  136.8 86.2 all-gather.11
  224.7 87.5 all-gather.21
  314.2 297.2 all-gather.25
  613.3 297.2 all-gather.23
  912.4 297.2 all-gather.27
  1453.6 32.4 reduce-scatter.9
  1541.7 32.2 reduce-scatter.11
  1760.2 999.9 reduce-scatter.7
  2762.8 591.4 all-reduce.1
where the time goes:
time: 3460 us; the launch traced here: 3450 us
  waiting for transfers between devices  2580 us (75%)
  local copies, waits for them, and re-layouts  339 us (10%)
  matrix products  287 us (8%)
  other arithmetic  210 us (6%)
    reduce_scatter x1, waiting for transfers between devices, local(): lax.psum_scatter(jnp.concatenate([contract_rows(normed_one, grad_qkv), co...  1000 us
    psum x1, waiting for transfers between devices, local(): shard = lax.psum(shard.astype(jnp.bfloat16), 'ctx').astype(jnp.float32)  574 us
    all_gather x1, waiting for transfers between devices, local(): piece = lax.all_gather(w_down, 'dp', axis=0, tiled=True)  279 us
    all_gather x1, waiting for transfers between devices, local(): piece_gate = lax.all_gather(w_gate, 'dp', axis=0, tiled=True)  279 us
    all_gather x1, waiting for transfers between devices, local(): piece_up = lax.all_gather(w_up, 'dp', axis=0, tiled=True)  247 us
    concatenate x1, local copies, waits for them, and re-layouts, local(): jnp.concatenate([contract_rows(normed_one, grad_qkv), contract_rows(mixed...  174 us
    dot_general x31, matrix products, contract_cols(): lax.dot_general(left, right, (((1,), (1,)), ((), ())), preferred_element_...  109 us
    add x16, other arithmetic, local(): jnp.repeat(stretch_map, half_rows, total_repeat_length=key_length)  94.6 us
  transfers between devices with their start and end apart: 13, of which 11 were waited for; matrix products, arithmetic and copies ran while one was open for 9% of the time, Pallas kernels for 0%

commit v1 on v0

v1 whole, which is shorter than its diff:
```python
from functools import partial

import jax
import jax.numpy as jnp
from jax import lax
from jax.sharding import Mesh, PartitionSpec as P

NORM_EPSILON = 1e-05
ROPE_BASE = 1000000.0
MASKED_SCORE = -1e30
BF16 = jnp.bfloat16
F32 = jnp.float32


def dot(left, right):
    return jnp.dot(left, right, preferred_element_type=F32)


def contract_rows(left, right):
    return lax.dot_general(left, right, (((0,), (0,)), ((), ())), preferred_element_type=F32)


def contract_cols(left, right):
    return lax.dot_general(left, right, (((1,), (1,)), ((), ())), preferred_element_type=F32)


def normalize(values):
    inverse = lax.rsqrt(jnp.mean(values * values, axis=-1, keepdims=True) + NORM_EPSILON)
    return (values * inverse, inverse)


def normalize_back(grad_hat, scaled, inverse):
    return inverse * (grad_hat - scaled * jnp.mean(grad_hat * scaled, axis=-1, keepdims=True))


def apply_rotary(values, cosine, sine):
    middle = values.shape[-1] // 2
    first, second = values[..., :middle], values[..., middle:]
    return jnp.concatenate([first * cosine - second * sine, second * cosine + first * sine], axis=-1)


def rotate_back(values, cosine, sine):
    middle = values.shape[-1] // 2
    first, second = values[..., :middle], values[..., middle:]
    return jnp.concatenate([first * cosine + second * sine, second * cosine - first * sine], axis=-1)


def masked_scores(query_rows, key_rows, query_places, key_places, score_scale):
    scores = contract_cols(query_rows, key_rows) * score_scale
    allowed = key_places[None, :] <= query_places[:, None]
    return jnp.where(allowed, scores, MASKED_SCORE)


def attend_head(operands, query_places, key_places, score_scale):
    query_rows, key_rows, value_rows = operands
    scores = masked_scores(query_rows, key_rows, query_places, key_places, score_scale)
    top_score = jnp.max(scores, axis=-1, keepdims=True)
    weights = jnp.exp(scores - top_score)
    weight_sum = jnp.sum(weights, axis=-1, keepdims=True)
    probs = (weights / weight_sum).astype(BF16)
    return (dot(probs, value_rows), (top_score + jnp.log(weight_sum))[:, 0])


def attend_back(operands, query_places, key_places, score_scale):
    query_rows, key_rows, value_rows, grad_rows, log_total = operands
    scores = masked_scores(query_rows, key_rows, query_places, key_places, score_scale)
    probs = jnp.exp(scores - log_total[:, None])
    grad_probs = contract_cols(grad_rows, value_rows)
    inner = jnp.sum(probs * grad_probs, axis=-1, keepdims=True)
    grad_scores = (probs * (grad_probs - inner)).astype(BF16)
    grad_query = dot(grad_scores, key_rows) * score_scale
    grad_key = contract_rows(grad_scores, query_rows) * score_scale
    grad_value = contract_rows(probs.astype(BF16), grad_rows)
    return (grad_query, grad_key, grad_value)


def columns_to_owner(weight, dp, parts, part):
    rows, cols = weight.shape
    width = cols // (dp * parts)
    cut = weight.reshape(rows, dp, parts, width)
    mine = lax.dynamic_index_in_dim(cut, part, 2, keepdims=False) if parts > 1 else cut[:, :, 0]
    out = lax.all_to_all(mine.transpose(1, 0, 2), "dp", 0, 0)
    return out.reshape(dp * rows, width)


def rows_to_owner(grad, dp):
    rows, width = grad.shape
    return lax.all_to_all(grad.reshape(dp, rows // dp, width), "dp", 0, 0)


def local(
    inputs, attn_gain, w_query, w_key, w_value, q_gain, key_norm_gain, w_out, ffn_gain,
    w_gate, w_up, w_down, stretch_map, pos_ids, cotangent,
):
    dp, lines, cores = lax.axis_size("dp"), lax.axis_size("z"), lax.axis_size("core")
    core = lax.axis_index("core")
    rows, width = inputs.shape[1], inputs.shape[2]
    head = q_gain.shape[0]
    query_width, key_width, hidden = w_query.shape[1], w_key.shape[1], w_gate.shape[1]
    half = rows // 2
    stretches = stretch_map.shape[0]
    length = stretches * half
    group = query_width // key_width
    kv_heads = key_width // head // dp
    q_heads = kv_heads * group
    tokens = dp * rows
    scale = head ** (-0.5)
    ctx = lax.axis_index("z") * cores + core

    index = jnp.arange(rows, dtype=jnp.int32)
    blocks = jnp.arange(stretches, dtype=jnp.int32)
    own = 2 * ctx + index // half
    query_places = jnp.sum(jnp.where(blocks[None, :] == own[:, None], stretch_map[None, :], 0), axis=1) * half + index % half
    key_places = jnp.repeat(stretch_map, half, total_repeat_length=length) * half + jnp.tile(
        jnp.arange(half, dtype=jnp.int32), stretches
    )
    group_places = jnp.tile(query_places, group)
    frequency = jnp.power(F32(ROPE_BASE), -2.0 * jnp.arange(head // 2, dtype=F32) / head)
    positions = lax.all_gather(pos_ids[0], "dp").reshape(tokens)
    angles = positions.astype(F32)[:, None] * frequency[None, :]
    cosine, sine = jnp.cos(angles)[:, None, :], jnp.sin(angles)[:, None, :]

    gain_one = lax.all_gather(attn_gain, "dp", axis=0, tiled=True).astype(F32)
    gain_two = lax.all_gather(ffn_gain, "dp", axis=0, tiled=True).astype(F32)
    wq = columns_to_owner(w_query, dp, 1, 0)
    wk = columns_to_owner(w_key, dp, 1, 0)
    wv = columns_to_owner(w_value, dp, 1, 0)
    wg = columns_to_owner(w_gate, dp, cores, core)
    wu = columns_to_owner(w_up, dp, cores, core)
    slice_rows = hidden // dp // cores
    wd = lax.dynamic_slice_in_dim(w_down, core * slice_rows, slice_rows, 0)
    own_x = inputs[0].astype(F32)
    hat_one, inverse_one = normalize(own_x)
    x_all = lax.all_gather(inputs[0], "dp", axis=0, tiled=True)
    normed_one = (normalize(x_all.astype(F32))[0] * gain_one).astype(BF16)
    q_gain_f, k_gain_f = q_gain.astype(F32), key_norm_gain.astype(F32)
    query_hat, query_inverse = normalize(dot(normed_one, wq).reshape(tokens, q_heads, head))
    query_rot = apply_rotary(query_hat * q_gain_f, cosine, sine).astype(BF16)
    key_hat, key_inverse = normalize(dot(normed_one, wk).reshape(tokens, kv_heads, head))
    key_rot = apply_rotary(key_hat * k_gain_f, cosine, sine).astype(BF16)
    value_low = dot(normed_one, wv).astype(BF16)
    keys_values = jnp.concatenate([key_rot.reshape(dp, rows, kv_heads * head), value_low.reshape(dp, rows, kv_heads * head)], axis=2)
    kv_all = lax.all_gather(keys_values, ("z", "core"), axis=1, tiled=True)
    kv_all = kv_all.reshape(dp, length, 2, kv_heads, head).transpose(2, 0, 3, 1, 4).reshape(2, dp * kv_heads, length, head)
    key_heads, value_heads = kv_all[0], kv_all[1]

    def to_heads(values):
        return (
            values.reshape(dp, rows, kv_heads, group, head).transpose(0, 2, 3, 1, 4).reshape(dp * kv_heads, group * rows, head)
        )

    def from_heads(values):
        return (
            values.reshape(dp, kv_heads, group, rows, head).transpose(0, 3, 1, 2, 4).reshape(tokens, q_heads * head)
        )

    query_grouped = to_heads(query_rot)
    mixed, log_total = lax.map(
        partial(attend_head, query_places=group_places, key_places=key_places, score_scale=scale),
        (query_grouped, key_heads, value_heads),
    )
    mixed_low = from_heads(mixed).astype(BF16)
    attn_part = dot(mixed_low, w_out)
    attn_out = jnp.sum(lax.all_to_all(attn_part.astype(BF16).reshape(dp, rows, width), "dp", 0, 0).astype(F32), axis=0)
    hidden_in = own_x + attn_out
    hat_two, inverse_two = normalize(hidden_in)

    normed_two = (hat_two * gain_two).astype(BF16)
    plane = tokens * cores

    def plane_gather(values):
        return lax.all_gather(values, ("dp", "core")).reshape(plane, width)

    def plane_sum(values):
        parts = lax.all_to_all(values.reshape(dp * cores, rows, width).astype(BF16), ("dp", "core"), 0, 0)
        return jnp.sum(parts.astype(F32), axis=0)

    normed_two_all = plane_gather(normed_two)
    cot_all = plane_gather(cotangent[0])
    gate = dot(normed_two_all, wg)
    up = dot(normed_two_all, wu)
    sig = jax.nn.sigmoid(gate)
    act = gate * sig
    act_low = (act * up).astype(BF16)
    output = (hidden_in + plane_sum(dot(act_low, wd))).astype(BF16)[None]
    grad_act = contract_cols(cot_all, wd)
    grad_gate = (grad_act * up * sig * (1.0 + gate * (1.0 - sig))).astype(BF16)
    grad_up = (grad_act * act).astype(BF16)
    grad_normed_two = plane_sum(contract_cols(grad_gate, wg) + contract_cols(grad_up, wu))
    gain_grad_two = jnp.sum(grad_normed_two * hat_two, axis=0)
    grad_hidden = cotangent[0].astype(F32) + normalize_back(grad_normed_two * gain_two, hat_two, inverse_two)

    grad_hidden_all = lax.all_gather(grad_hidden.astype(BF16), "dp", axis=0, tiled=True)
    grad_mixed = contract_cols(grad_hidden_all, w_out).astype(BF16)
    grad_q, grad_k, grad_v = lax.map(
        partial(attend_back, query_places=group_places, key_places=key_places, score_scale=scale),
        (query_grouped, key_heads, value_heads, to_heads(grad_mixed), log_total),
    )
    grad_query_rot = from_heads(grad_q).astype(BF16).astype(F32).reshape(tokens, q_heads, head)
    kv_grad = jnp.stack([grad_k, grad_v]).reshape(2, dp, kv_heads, length, head).transpose(3, 1, 0, 2, 4).astype(BF16)
    kv_grad = lax.psum_scatter(kv_grad, ("z", "core"), scatter_dimension=0, tiled=True).transpose(1, 0, 2, 3, 4).reshape(tokens, 2, kv_heads, head)
    grad_key_rot = kv_grad[:, 0].astype(F32)
    grad_value_low = kv_grad[:, 1].reshape(tokens, kv_heads * head)
    grad_query_gained = rotate_back(grad_query_rot, cosine, sine)
    q_gain_grad = jnp.sum(grad_query_gained * query_hat, axis=(0, 1))
    grad_query_pre = normalize_back(grad_query_gained * q_gain_f, query_hat, query_inverse).reshape(tokens, -1).astype(BF16)
    grad_key_gained = rotate_back(grad_key_rot, cosine, sine)
    k_gain_grad = jnp.sum(grad_key_gained * key_hat, axis=(0, 1))
    grad_key_pre = normalize_back(grad_key_gained * k_gain_f, key_hat, key_inverse).reshape(tokens, -1).astype(BF16)
    normed_part = contract_cols(grad_query_pre, wq) + contract_cols(grad_key_pre, wk) + contract_cols(grad_value_low, wv)
    grad_normed_one = jnp.sum(
        lax.all_to_all(normed_part.astype(BF16).reshape(dp, rows, width), "dp", 0, 0).astype(F32), axis=0
    )
    gain_grad_one = jnp.sum(grad_normed_one * hat_one, axis=0)
    input_grad = (grad_hidden + normalize_back(grad_normed_one * gain_one, hat_one, inverse_one)).astype(BF16)[None]

    def finish_columns(grad):
        return rows_to_owner(lax.psum(grad.astype(BF16), "z"), dp)

    down = lax.all_gather(lax.psum(contract_rows(act_low, cot_all).astype(BF16), "z"), "core", axis=0, tiled=True)

    def finish_hidden(grad):
        mine = lax.all_gather(finish_columns(grad), "core")
        return mine.transpose(2, 1, 0, 3).reshape(width // dp, hidden).astype(F32)

    gate_grad = finish_hidden(contract_rows(normed_two_all, grad_gate))
    up_grad = finish_hidden(contract_rows(normed_two_all, grad_up))
    out_grad = lax.psum(contract_rows(mixed_low, grad_hidden_all).astype(BF16), ("z", "core")).astype(F32)

    def finish_heads(grad):
        mine = rows_to_owner(lax.psum(grad.astype(BF16), ("z", "core")), dp)
        return mine.transpose(1, 0, 2).reshape(width // dp, -1).astype(F32)

    query_grad = finish_heads(contract_rows(normed_one, grad_query_pre))
    key_grad = finish_heads(contract_rows(normed_one, grad_key_pre))
    value_grad = finish_heads(contract_rows(normed_one, grad_value_low))
    gains = jnp.concatenate([gain_grad_one, gain_grad_two, q_gain_grad, k_gain_grad])
    gains = lax.psum(gains, ("dp", "z", "core"))
    place = lax.axis_index("dp")
    piece = width // dp
    attn_gain_grad = lax.dynamic_slice_in_dim(gains, place * piece, piece, 0)
    ffn_gain_grad = lax.dynamic_slice_in_dim(gains, width + place * piece, piece, 0)
    return (
        output, input_grad, attn_gain_grad, query_grad, key_grad, value_grad,
        gains[2 * width : 2 * width + head], gains[2 * width + head :], out_grad, ffn_gain_grad,
        gate_grad, up_grad, down.astype(F32),
    )


def solution(mesh):
    dp, ctx = mesh.shape["dp"], mesh.shape["ctx"]
    fine = Mesh(mesh.devices.reshape(dp, ctx // 2, 2), ("dp", "z", "core"))
    tokens = P("dp", ("z", "core"), None)
    rows = P("dp", None)
    in_specs = (
        tokens, P("dp"), rows, rows, rows, P(), P(), rows, P("dp"), rows, rows, rows, P(), P("dp", ("z", "core")), tokens,
    )
    out_specs = (tokens, tokens, P("dp"), rows, rows, rows, P(), P(), rows, P("dp"), rows, rows, rows)
    return jax.shard_map(local, mesh=fine, in_specs=in_specs, out_specs=out_specs, check_vma=False)
```

time: 3460 us -> 1880 us (0.54)
  waiting for transfers between devices: 2580 us -> 669 us
  blocking collectives: 17.5 us -> 189 us
  local copies, waits for them, and re-layouts: 339 us -> 467 us
  matrix products: 287 us -> 222 us
  starting transfers between devices: 0.77 us -> 54.7 us
    reduce_scatter x1 -> x0, waiting for transfers between devices: 1000 us -> none  [local(): lax.psum_scatter(jnp.concatenate([contract_rows(normed_one, grad_qkv), co...]
    all_gather x9 -> x8, waiting for transfers between devices: 979 us -> 35.1 us  [the longest x1 34.3 us: local(): lax.all_gather(grad_hidden.astype(BF16), 'dp', axis=0, tiled=True)]
    unnamed x67 -> x124, local copies, waits for them, and re-layouts: 13.6 us -> 302 us
    all_to_all x0 -> x12, waiting for transfers between devices: none -> 240 us  [the longest x5 120 us: columns_to_owner(): out = lax.all_to_all(mine.transpose(1, 0, 2), 'dp', 0, 0)]
    psum x1 -> x2, waiting for transfers between devices: 574 us -> 391 us  [the longest x1 391 us: finish_columns(): return rows_to_owner(lax.psum(grad.astype(BF16), 'z'), dp)]
    concatenate x1 -> x3, local copies, waits for them, and re-layouts: 174 us -> 0.21 us  [the longest x2 0.13 us: apply_rotary(): jnp.concatenate([first * cosine - second * sine, second * cosine + first...]
    convert_element_type x4 -> x12, local copies, waits for them, and re-layouts: 2.58 us -> 115 us  [the longest x4 102 us: finish_hidden(): return mine.transpose(2, 1, 0, 3).reshape(width // dp, hidden).astype(F32)]
    all_to_all x0 -> x2, blocking collectives: none -> 105 us  [the longest x1 53.8 us: rows_to_owner(): return lax.all_to_all(grad.reshape(dp, rows // dp, width), 'dp', 0, 0)]
  transfers between devices with their start and end apart: 13 -> 23, of which waited for: 11 -> 13; matrix products, arithmetic and copies ran while one was open for 9% -> 15% of each run, Pallas kernels for 0% -> 0%
where the time goes in v1:
time: 1880 us; the launch traced here: 1860 us
  waiting for transfers between devices  669 us (36%)
  local copies, waits for them, and re-layouts  467 us (25%)
  other arithmetic  241 us (13%)
  matrix products  222 us (12%)
  blocking collectives  189 us (10%)
  starting transfers between devices  54.7 us (3%)
    psum x1, waiting for transfers between devices, finish_columns(): return rows_to_owner(lax.psum(grad.astype(BF16), 'z'), dp)  391 us
    unnamed x124, local copies, waits for them, and re-layouts  302 us
    all_to_all x5, waiting for transfers between devices, columns_to_owner(): out = lax.all_to_all(mine.transpose(1, 0, 2), 'dp', 0, 0)  120 us
    convert_element_type x4, local copies, waits for them, and re-layouts, finish_hidden(): return mine.transpose(2, 1, 0, 3).reshape(width // dp, hidden).astype(F32)  102 us
    add x16, other arithmetic, local(): jnp.repeat(stretch_map, half, total_repeat_length=length) * half  89.2 us
    dot_general x31, matrix products, contract_cols(): lax.dot_general(left, right, (((1,), (1,)), ((), ())), preferred_element_...  83.8 us
    dot_general x23, matrix products, dot(): return jnp.dot(left, right, preferred_element_type=F32)  74.6 us
    gather x32, other arithmetic, local(): jnp.repeat(stretch_map, half, total_repeat_length=length) * half  72.6 us
  transfers between devices with their start and end apart: 23, of which 13 were waited for; matrix products, arithmetic and copies ran while one was open for 15% of the time, Pallas kernels for 0%

profile of v1, /device:TPU:0, one launch (start us, length us, event | category | flops | bytes accessed | tf_op | source)
XLA Modules:
  0.0 1859.8 jit_solution(8825054890819679538)
XLA Ops:
  71.2 24.3 %all-to-all-done = bf16[4,512,512]{2,1,0:T(8,128)(2,1)} async-done(((bf16[4,512,512]{2,1,0:T(8,128)(2,1)}), bf16[4,512,512]{2,1,0:T(8,128)(2,1)}, u32[]{:S(2)}, u32[]{:S(2)}) %all-to-all-start) | async-done | bytes 2097184 | tf_op jit(solution)/shard_map/all_to_all | solution.py:82
  118.9 116.6 %while.29 = (s32[]{:T(128)}, bf16[8,512,64]{1,2,0:T(8,128)(2,1)}, f32[8,512]{1,0:T(8,128)S(1)}, bf16[8,512,64]{2,1,0:T(8,128)(2,1)S(1)}, bf16[8,1024,64]{2,1,0:T...) while((s32[]{:T(128)}, bf16[8,512,64]{1,2,0:T(8,128)(2,1)}, ...), condition=%wide.region_7.8_spmd.clone, body=%wide.region_4.7_spmd.clone.sunk | while | flops 138982912 | bytes 7189369 | solution.py:158
  247.5 27.5 %all-gather.5 = bf16[4,1,512]{2,1,0:T(2,128)(2,1)S(1)} all-gather(bf16[1,1,512]{2,1,0:T(2,128)(2,1)S(1)} %reshape.631), channel_id=1, replica_groups=mesh['dp'=4,'z'=4,'core'=2] {'dp'}, dimensions={0}, use_global_device_ids=true | all-gather | bytes 5120 | tf_op jit(solution)/shard_map/all_gather | solution.py:124
  280.3 12.0 copy.146
  292.3 12.0 copy.144
  329.7 55.7 %all-to-all-done.4 = bf16[4,512,1024]{2,1,0:T(8,128)(2,1)} async-done(((bf16[4,512,1024]{2,1,0:T(8,128)(2,1)}), bf16[4,512,1024]{2,1,0:T(8,128)(2,1)}, u32[]{:S(2)}, u32[]{:S(2)}) %all-to-all-start.4) | async-done | bytes 4194336 | tf_op jit(solution)/shard_map/all_to_all | solution.py:82
  390.3 10.0 fusion.98
  400.3 33.5 %all-to-all-done.5 = bf16[4,512,1024]{2,1,0:T(8,128)(2,1)} async-done(((bf16[4,512,1024]{2,1,0:T(8,128)(2,1)}), bf16[4,512,1024]{2,1,0:T(8,128)(2,1)}, u32[]{:S(2)}, u32[]{:S(2)}) %all-to-all-start.5) | async-done | bytes 4194336 | tf_op jit(solution)/shard_map/all_to_all | solution.py:82
  433.8 10.0 fusion.99
  443.8 13.3 fusion.50
  457.0 15.7 fusion.100
  479.8 51.6 %all_to_all.70 = bf16[8,128,2048]{2,1,0:T(8,128)(2,1)S(1)} all-to-all(bf16[8,128,2048]{2,1,0:T(8,128)(2,1)S(1)} %bitcast.521), channel_id=1, replica_groups=mesh['dp'=4,'z'=4,'core'=2] {'dp','core'}, dimensions={0} | all-to-all | bytes 8388608 | tf_op jit(solution)/shard_map/all_to_all | solution.py:175
  534.8 34.3 %all-gather.21.cloned.1.call-done = bf16[512,2048]{1,0:T(8,128)(2,1)} async-done(((bf16[128,2048]{1,0:T(8,128)(2,1)}), bf16[512,2048]{1,0:T(8,128)(2,1)}) %all-gather.21.cloned.1.call-update) | async-done | bytes 2097168 | tf_op jit(solution)/shard_map/all_gather | solution.py:193
  576.3 159.1 %while.30 = (s32[]{:T(128)}, bf16[8,512,64]{1,2,0:T(8,128)(2,1)}, bf16[8,1024,64]{1,2,0:T(8,128)(2,1)}, bf16[8,1024,64]{1,2,0:T(8,128)(2,1)}, bf16[8,512,64]{2,1...) while((s32[]{:T(128)}, bf16[8,512,64]{1,2,0:T(8,128)(2,1)}, ...), condition=%wide.region_16.17_spmd.clone, body=%wide.region_14.16_spmd.clone.sunk | while | flops 340932096 | bytes 17799048 | solution.py:195
  737.1 104.5 %copy.161 = bf16[1024,4,2,2,64]{1,4,3,2,0:T(8,128)(2,1)} copy(bf16[1024,4,2,2,64]{0,4,3,1,2:T(8,128)(2,1)S(1)} %maximum_bitcast_fusion) | data formatting | bytes 4194304
  841.6 128.7 %reshape.726 = bf16[1024,1024]{1,0:T(8,128)(2,1)} reshape(bf16[1024,2,2,64,4]{4,3,2,1,0:T(8,128)(2,1)} %bitcast.209) | data formatting | bytes 4194304
  1006.4 19.9 %reshape.727 = bf16[128,2,2,64,4]{4,3,2,1,0:T(8,128)(2,1)} reshape(bf16[128,1024]{1,0:T(8,128)(2,1)} %reduce-scatter.4.cloned.1.call-done) | data formatting | bytes 524288
  1026.3 11.2 copy.162
  1044.8 391.5 %all-reduce.7.cloned.1.call-done = (bf16[4,512,1024]{2,1,0:T(8,128)(2,1)}, bf16[4,512,1024]{2,1,0:T(8,128)(2,1)}, bf16[1024,2048]{1,0:T(8,128)(2,1)}) async-done(((bf16[4,512,1024]{2,1,0:T(8,128)(2,1)}, bf16[4,512,1024]{2,1,0:T(8,128)(2,1)}, bf16[1024,2048]{1,0:T(8,128)(2,1)}), (bf16[4,512,1024]{2,1,0:T(8,128)(2,1)}, bf16[4,512,1024]{2,1,0:T(8,128)(2,1)}, ...) | async-done | bytes 12582928 | tf_op jit(solution)/shard_map/psum | solution.py:218
  1436.4 53.8 %all_to_all.71 = bf16[4,512,1024]{2,1,0:T(8,128)(2,1)} all-to-all(bf16[4,512,1024]{2,1,0:T(8,128)(2,1)} %get-tuple-element.517), channel_id=1, replica_groups=mesh['dp'=4,'z'=4,'core'=2] {'dp'}, dimensions={0} | all-to-all | bytes 8388608 | tf_op jit(solution)/shard_map/all_to_all | solution.py:88
  1504.5 36.9 %all-to-all-done.13 = bf16[4,512,1024]{2,1,0:T(8,128)(2,1)} async-done(((bf16[4,512,1024]{2,1,0:T(8,128)(2,1)}), bf16[4,512,1024]{2,1,0:T(8,128)(2,1)}, u32[]{:S(2)}, u32[]{:S(2)}) %all-to-all-start.13) | async-done | bytes 4194336 | tf_op jit(solution)/shard_map/all_to_all | solution.py:88
  1553.1 42.0 %all-to-all-done.6 = bf16[8,128,2048]{2,1,0:T(8,128)(2,1)} async-done(((bf16[8,128,2048]{2,1,0:T(8,128)(2,1)}), bf16[8,128,2048]{2,1,0:T(8,128)(2,1)}, u32[]{:S(2)}, u32[]{:S(2)}) %all-to-all-start.6) | async-done | bytes 4194336 | tf_op jit(solution)/shard_map/all_to_all | solution.py:175
  1598.7 24.1 %all-to-all-done.8 = bf16[4,128,2048]{2,1,0:T(8,128)(2,1)S(1)} async-done(((bf16[4,128,2048]{2,1,0:T(8,128)(2,1)}), bf16[4,128,2048]{2,1,0:T(8,128)(2,1)S(1)}, u32[]{:S(2)}, u32[]{:S(2)}) %all-to-all-start.8) | async-done | bytes 2097184 | tf_op jit(solution)/shard_map/all_to_all | solution.py:212
  1641.7 39.8 %psum.56 = f32[4224]{0:T(1024)S(1)} all-reduce(f32[4224]{0:T(1024)S(1)} %concatenate.38), channel_id=1, replica_groups=mesh['dp'=4,'z'=4,'core'=2] {'dp','z','core'}, use_global_device_ids=true, to_apply=%region_26.27 | all-reduce | flops 4224 | bytes 33792 | tf_op jit(solution)/shard_map/psum | solution.py:238
  1697.3 13.8 all-to-all-done.9
  1715.9 11.7 convert_element_type.321
  1727.6 11.7 convert_bitcast_fusion.1
  1739.3 28.6 %copy.157 = f32[512,4,2,1024]{3,2,1,0:T(2,128)} copy(f32[512,4,2,1024]{3,0,1,2:T(8,128)} %convert_bitcast_fusion.1) | data formatting | bytes 33554432 | tf_op jit(solution)/shard_map/convert_element_type | solution.py:224
  1767.9 22.1 %reshape.557 = f32[512,8192]{1,0:T(8,128)} reshape(f32[512,4,2,1024]{3,2,1,0:T(2,128)} %copy.157) | data formatting | bytes 33554432 | tf_op jit(solution)/shard_map/convert_element_type | solution.py:224
  1790.0 11.7 convert_bitcast_fusion
  1801.7 28.8 %copy.158 = f32[512,4,2,1024]{3,2,1,0:T(2,128)} copy(f32[512,4,2,1024]{3,0,1,2:T(8,128)} %convert_bitcast_fusion) | data formatting | bytes 33554432 | tf_op jit(solution)/shard_map/convert_element_type | solution.py:224
  1830.5 22.3 %reshape.558 = f32[512,8192]{1,0:T(8,128)} reshape(f32[512,4,2,1024]{3,2,1,0:T(2,128)} %copy.158) | data formatting | bytes 33554432 | tf_op jit(solution)/shard_map/convert_element_type | solution.py:224
  (476 shorter events, 540.8 us)
Async XLA Ops:
  7.2 232.9 %copy-start = (bf16[512,2048]{1,0:T(8,128)(2,1)S(1)}, bf16[512,2048]{1,0:T(8,128)(2,1)}, u32[]{:S(2)}) copy-start(bf16[512,2048]{1,0:T(8,128)(2,1)} %param.28) | copy-start | bytes 6291460
  7.2 38.1 %copy-start.49 = (bf16[64]{0:T(256)(128)(2,1)S(1)}, bf16[64]{0:T(256)(128)(2,1)}, u32[]{:S(2)}) copy-start(bf16[64]{0:T(256)(128)(2,1)} %param.27) | copy-start | bytes 388
  7.2 41.5 %all-gather.25.cloned.1.call-start = ((), (), s32[]{:S(2)}) async-start(), calls=%async_computation.20 | async-start | bytes 2621440 | tf_op jit(solution)/shard_map/all_gather | solution.py:134
  10.2 14.2 all-to-all-start.1
  24.4 22.3 %all-to-all-start.2 = ((bf16[4,512,128]{1,2,0:T(8,128)(2,1)}), bf16[4,512,128]{1,2,0:T(8,128)(2,1)}, u32[]{:S(2)}, u32[]{:S(2)}) async-start(bf16[4,512,128]{1,2,0:T(8,128)(2,1)} %bitcast.19), calls=%async_computation.2 | async-start | bytes 1048576 | tf_op jit(solution)/shard_map/all_to_all | solution.py:82
  28.5 78.8 %all-gather.15.cloned.1.call-start = ((), (), s32[]{:S(2)}) async-start(), calls=%async_computation.15 | async-start | bytes 2359296 | tf_op jit(solution)/shard_map/all_gather | solution.py:143
  38.3 61.1 %copy-start.33 = (f32[4,1,512]{2,1,0:T(1,128)}, f32[4,1,512]{2,1,0:T(1,128)S(1)}, u32[]{:S(2)}) copy-start(f32[4,1,512]{2,1,0:T(1,128)S(1)} %convert_element_type.341) | copy-start | bytes 24580
  45.6 58.6 %copy-start.24 = (f32[512,32]{0,1:T(8,128)}, f32[512,32]{0,1:T(8,128)S(1)}, u32[]{:S(2)}) copy-start(f32[512,32]{0,1:T(8,128)S(1)} %get-tuple-element.553) | copy-start | bytes 196612
  45.7 58.6 %copy-start.26 = (f32[512,32]{0,1:T(8,128)}, f32[512,32]{0,1:T(8,128)S(1)}, u32[]{:S(2)}) copy-start(f32[512,32]{0,1:T(8,128)S(1)} %get-tuple-element.554) | copy-start | bytes 196612
  50.8 48.7 %copy-start.41 = (f32[512]{0:T(512)}, f32[512]{0:T(512)S(1)}, u32[]{:S(2)}) copy-start(f32[512]{0:T(512)S(1)} %add_rsqrt_fusion.2) | copy-start | bytes 6148
  65.8 29.7 %all-to-all-start = ((bf16[4,512,512]{2,1,0:T(8,128)(2,1)}), bf16[4,512,512]{2,1,0:T(8,128)(2,1)}, u32[]{:S(2)}, u32[]{:S(2)}) async-start(bf16[4,512,512]{2,1,0:T(8,128)(2,1)} %copy.133), calls=%async_computation | async-start | bytes 4194304 | tf_op jit(solution)/shard_map/all_to_all | solution.py:82
  242.7 32.3 %all-to-all-start.3 = ((bf16[4,128,2048]{2,1,0:T(8,128)(2,1)}), bf16[4,128,2048]{2,1,0:T(8,128)(2,1)}, u32[]{:S(2)}, u32[]{:S(2)}) async-start(bf16[4,128,2048]{2,1,0:T(8,128)(2,1)} %bitcast.530), calls=%async_computation.3 | async-start | bytes 4194304 | tf_op jit(solution)/shard_map/all_to_all | solution.py:164
  247.4 142.9 %all-gather.17.cloned.1.call-start = ((), (), s32[]{:S(2)}) async-start(), calls=%async_computation.16 | async-start | bytes 4718592 | tf_op jit(solution)/shard_map/all_gather | solution.py:172
  318.0 67.3 %all-to-all-start.4 = ((bf16[4,512,1024]{2,1,0:T(8,128)(2,1)}), bf16[4,512,1024]{2,1,0:T(8,128)(2,1)}, u32[]{:S(2)}, u32[]{:S(2)}) async-start(bf16[4,512,1024]{2,1,0:T(8,128)(2,1)} %bitcast.505), calls=%async_computation.4 | async-start | bytes 8388608 | tf_op jit(solution)/shard_map/all_to_all | solution.py:82
  322.9 120.9 %all-gather.19.cloned.1.call-start = ((), (), s32[]{:S(2)}) async-start(), calls=%async_computation.17 | async-start | bytes 4718592 | tf_op jit(solution)/shard_map/all_gather | solution.py:172
  385.4 48.4 %all-to-all-start.5 = ((bf16[4,512,1024]{2,1,0:T(8,128)(2,1)}), bf16[4,512,1024]{2,1,0:T(8,128)(2,1)}, u32[]{:S(2)}, u32[]{:S(2)}) async-start(bf16[4,512,1024]{2,1,0:T(8,128)(2,1)} %bitcast.504), calls=%async_computation.5 | async-start | bytes 8388608 | tf_op jit(solution)/shard_map/all_to_all | solution.py:82
  390.2 178.9 %all-gather.21.cloned.1.call-start = ((), (), s32[]{:S(2)}) async-start(), calls=%async_computation.18 | async-start | bytes 2621440 | tf_op jit(solution)/shard_map/all_gather | solution.py:193
  534.7 471.7 %reduce-scatter.4.cloned.1.call-start = ((), (), s32[]{:S(2)}) async-start(), calls=%async_computation.23 | async-start | bytes 2359296
  841.6 128.8 %copy-start.53 = (bf16[1024,1024]{1,0:T(8,128)(2,1)S(1)}, bf16[1024,1024]{1,0:T(8,128)(2,1)}, u32[]{:S(2)}) copy-start(bf16[1024,1024]{1,0:T(8,128)(2,1)} %copy-done.52) | copy-start | bytes 6291460
  970.4 465.9 %all-reduce.7.cloned.1.call-start = ((), (), s32[]{:S(2)}) async-start(), calls=%async_computation.25 | async-start | bytes 25165824 | tf_op jit(solution)/shard_map/psum | solution.py:218
  992.0 630.8 %all-reduce.5.cloned.1.call-start = ((), (), s32[]{:S(2)}) async-start(), calls=%async_computation.24 | async-start | bytes 10485760 | tf_op jit(solution)/shard_map/psum | solution.py:231
  1044.8 671.1 %all-gather.23.cloned.1.call-start = ((), (), s32[]{:S(2)}) async-start(), calls=%async_computation.19 | async-start | bytes 12582912 | tf_op jit(solution)/shard_map/all_gather | solution.py:220
  1436.3 291.2 %all-gather.27.cloned.1.call-start = ((), (), s32[]{:S(2)}) async-start(), calls=%async_computation.21 | async-start | bytes 12582912 | tf_op jit(solution)/shard_map/all_gather | solution.py:223
  1490.2 51.2 %all-to-all-start.13 = ((bf16[4,512,1024]{2,1,0:T(8,128)(2,1)}), bf16[4,512,1024]{2,1,0:T(8,128)(2,1)}, u32[]{:S(2)}, u32[]{:S(2)}) async-start(bf16[4,512,1024]{2,1,0:T(8,128)(2,1)} %get-tuple-element.518), calls=%async_computation.13 | async-start | bytes 8388608 | tf_op jit(solution)/shard_map/all_to_all | solution.py:88
  1541.4 53.7 %all-to-all-start.6 = ((bf16[8,128,2048]{2,1,0:T(8,128)(2,1)}), bf16[8,128,2048]{2,1,0:T(8,128)(2,1)}, u32[]{:S(2)}, u32[]{:S(2)}) async-start(bf16[8,128,2048]{2,1,0:T(8,128)(2,1)} %bitcast.520), calls=%async_computation.6 | async-start | bytes 8388608 | tf_op jit(solution)/shard_map/all_to_all | solution.py:175
  1546.0 244.0 %all-gather.29.cloned.1.call-start = ((), (), s32[]{:S(2)}) async-start(), calls=%async_computation.22 | async-start | bytes 12582912 | tf_op jit(solution)/shard_map/all_gather | solution.py:223
  1595.1 27.7 %all-to-all-start.8 = ((bf16[4,128,2048]{2,1,0:T(8,128)(2,1)}), bf16[4,128,2048]{2,1,0:T(8,128)(2,1)S(1)}, u32[]{:S(2)}, u32[]{:S(2)}) async-start(bf16[4,128,2048]{2,1,0:T(8,128)(2,1)} %bitcast.511), calls=%async_computation.8 | async-start | bytes 4194304 | tf_op jit(solution)/shard_map/all_to_all | solution.py:212
  1622.8 11.1 all-to-all-start.10
  1633.9 48.2 %all-to-all-start.11 = ((bf16[4,512,128]{2,1,0:T(8,128)(2,1)}), bf16[4,512,128]{2,1,0:T(8,128)(2,1)}, u32[]{:S(2)}, u32[]{:S(2)}) async-start(bf16[4,512,128]{2,1,0:T(8,128)(2,1)} %get-tuple-element.515), calls=%async_computation.11 | async-start | bytes 1048576 | tf_op jit(solution)/shard_map/all_to_all | solution.py:88
  1638.0 49.2 %copy-start.5 = (f32[128,2048]{1,0:T(8,128)S(1)}, f32[128,2048]{1,0:T(8,128)}, u32[]{:S(2)}) copy-start(f32[128,2048]{1,0:T(8,128)} %copy-done.4) | copy-start | bytes 3145732
  1638.0 49.2 %copy-start.14 = (bf16[1,128,2048]{2,1,0:T(8,128)(2,1)S(1)}, bf16[1,128,2048]{2,1,0:T(8,128)(2,1)}, u32[]{:S(2)}) copy-start(bf16[1,128,2048]{2,1,0:T(8,128)(2,1)} %param.35) | copy-start | bytes 1572868
  1682.1 28.9 %all-to-all-start.9 = ((bf16[4,512,512]{2,1,0:T(8,128)(2,1)}), bf16[4,512,512]{2,1,0:T(8,128)(2,1)}, u32[]{:S(2)}, u32[]{:S(2)}) async-start(bf16[4,512,512]{2,1,0:T(8,128)(2,1)} %get-tuple-element.513), calls=%async_computation.9 | async-start | bytes 4194304 | tf_op jit(solution)/shard_map/all_to_all | solution.py:88
  (47 other events, 383.5 us)
Sparse Core Ops, SparseCore 0:
  9.9 38.7 all-gather.24
  57.8 31.2 all-gather.14
  280.5 36.6 all-gather.16
  325.3 61.6 all-gather.18
  534.8 34.2 all-gather.20
  970.5 35.7 reduce-scatter.3
  1010.3 425.9 all-reduce.6
  1440.0 116.2 all-reduce.4
  1557.9 19.8 all-gather.22
  1579.2 21.0 all-gather.26
  1601.8 21.0 all-gather.28

commit v2 on v1

--- a/solution.py
+++ b/solution.py
@@ -3,6 +3,8 @@
 import jax
 import jax.numpy as jnp
 from jax import lax
+from jax.experimental import pallas as pl
+from jax.experimental.pallas import tpu as pltpu
 from jax.sharding import Mesh, PartitionSpec as P
 
 NORM_EPSILON = 1e-05
@@ -10,6 +12,8 @@
 MASKED_SCORE = -1e30
 BF16 = jnp.bfloat16
 F32 = jnp.float32
+MESH = pl.DeviceIdType.MESH
+MIB = 2**20
 
 
 def dot(left, right):
@@ -45,33 +49,489 @@
     return jnp.concatenate([first * cosine + second * sine, second * cosine - first * sine], axis=-1)
 
 
-def masked_scores(query_rows, key_rows, query_places, key_places, score_scale):
-    scores = contract_cols(query_rows, key_rows) * score_scale
-    allowed = key_places[None, :] <= query_places[:, None]
-    return jnp.where(allowed, scores, MASKED_SCORE)
-
-
-def attend_head(operands, query_places, key_places, score_scale):
-    query_rows, key_rows, value_rows = operands
-    scores = masked_scores(query_rows, key_rows, query_places, key_places, score_scale)
-    top_score = jnp.max(scores, axis=-1, keepdims=True)
-    weights = jnp.exp(scores - top_score)
-    weight_sum = jnp.sum(weights, axis=-1, keepdims=True)
-    probs = (weights / weight_sum).astype(BF16)
-    return (dot(probs, value_rows), (top_score + jnp.log(weight_sum))[:, 0])
-
-
-def attend_back(operands, query_places, key_places, score_scale):
-    query_rows, key_rows, value_rows, grad_rows, log_total = operands
-    scores = masked_scores(query_rows, key_rows, query_places, key_places, score_scale)
-    probs = jnp.exp(scores - log_total[:, None])
-    grad_probs = contract_cols(grad_rows, value_rows)
-    inner = jnp.sum(probs * grad_probs, axis=-1, keepdims=True)
-    grad_scores = (probs * (grad_probs - inner)).astype(BF16)
-    grad_query = dot(grad_scores, key_rows) * score_scale
-    grad_key = contract_rows(grad_scores, query_rows) * score_scale
-    grad_value = contract_rows(probs.astype(BF16), grad_rows)
-    return (grad_query, grad_key, grad_value)
+def attend_kernel(head, group, query, keys_values, bias, mixed, log_total):
+    length = bias.shape[0]
+    rows = query.shape[1]
+    kv_heads = query.shape[2] // head // group
+    scale = head ** (-0.5)
+    both = keys_values[:, 0].reshape(length, 2 * kv_heads * head)
+    mask = jnp.concatenate([bias[...]] * group, axis=1)
+    for g in range(kv_heads):
+        keys = both[:, g * head : (g + 1) * head]
+        values = both[:, (kv_heads + g) * head : (kv_heads + g + 1) * head]
+        queries = stack_heads(query, g, group, head)
+        scores = contract_cols(keys, queries) * scale + mask
+        top = jnp.max(scores, axis=0, keepdims=True)
+        weights = jnp.exp(scores - top)
+        total = jnp.sum(weights, axis=0, keepdims=True)
+        probs = (weights * (1.0 / total)).astype(BF16)
+        out = contract_rows(values, probs)
+        log_total[0, pl.ds(g, 1), :] = top + jnp.log(total)
+        unstack_heads(mixed, out.T.astype(BF16), g, group, head, rows)
+
+
+def stack_heads(ref, g, group, head):
+    return jnp.concatenate([ref[0, :, (g * group + h) * head : (g * group + h + 1) * head] for h in range(group)], axis=0)
+
+
+def unstack_heads(ref, values, g, group, head, rows):
+    ref[0, :, g * group * head : (g + 1) * group * head] = jnp.concatenate(
+        [values[h * rows : (h + 1) * rows] for h in range(group)], axis=1
+    )
+
+
+def attend_back_kernel(head, group, query, keys_values, bias, log_total, grad_mixed, grad_query, grad_kv):
+    length = bias.shape[0]
+    rows = query.shape[1]
+    kv_heads = query.shape[2] // head // group
+    scale = head ** (-0.5)
+    both = keys_values[:, 0].reshape(length, 2 * kv_heads * head)
+    mask = jnp.concatenate([bias[...]] * group, axis=1)
+    grads = [None] * (2 * kv_heads)
+    for g in range(kv_heads):
+        keys = both[:, g * head : (g + 1) * head]
+        values = both[:, (kv_heads + g) * head : (kv_heads + g + 1) * head]
+        queries = stack_heads(query, g, group, head)
+        grad_out = stack_heads(grad_mixed, g, group, head)
+        scores = contract_cols(keys, queries) * scale + mask
+        probs = jnp.exp(scores - log_total[0, pl.ds(g, 1), :])
+        grad_probs = contract_cols(values, grad_out)
+        inner = jnp.sum(probs * grad_probs, axis=0, keepdims=True)
+        grad_scores = (probs * (grad_probs - inner)).astype(BF16)
+        grads[g] = dot(grad_scores, queries) * scale
+        grads[kv_heads + g] = dot(probs.astype(BF16), grad_out)
+        back = contract_rows(keys, grad_scores) * scale
+        unstack_heads(grad_query, back.T.astype(BF16), g, group, head, rows)
+    grad_kv[:, 0] = jnp.concatenate(grads, axis=1).astype(BF16).reshape(grad_kv[:, 0].shape)
+
+
+def attend(query, keys_values, bias, head, group, grad_mixed=None, log_total=None):
+    seqs, rows, width = query.shape
+    spans, _, _, kv_width = keys_values.shape
+    length = bias.shape[0]
+    kv_heads = width // head // group
+    row_spec = pl.BlockSpec((1, rows, width), lambda s: (s, 0, 0))
+    kv_spec = pl.BlockSpec((spans, 1, rows, kv_width), lambda s: (0, s, 0, 0))
+    log_spec = pl.BlockSpec((1, kv_heads, group * rows), lambda s: (s, 0, 0))
+    bias_spec = pl.BlockSpec((length, rows), lambda s: (0, 0))
+    rows_out = jax.ShapeDtypeStruct(query.shape, BF16)
+    params = pltpu.CompilerParams(vmem_limit_bytes=56 * MIB)
+    flops = 4 * seqs * rows * length * width
+    if grad_mixed is None:
+        return pl.pallas_call(
+            partial(attend_kernel, head, group),
+            grid=(seqs,),
+            in_specs=[row_spec, kv_spec, bias_spec],
+            out_specs=(row_spec, log_spec),
+            out_shape=(rows_out, jax.ShapeDtypeStruct((seqs, kv_heads, group * rows), F32)),
+            compiler_params=params,
+            cost_estimate=pl.CostEstimate(flops=flops, bytes_accessed=4 * MIB, transcendentals=flops // 256),
+            name="attend",
+        )(query, keys_values, bias)
+    return pl.pallas_call(
+        partial(attend_back_kernel, head, group),
+        grid=(seqs,),
+        in_specs=[row_spec, kv_spec, bias_spec, log_spec, row_spec],
+        out_specs=(row_spec, kv_spec),
+        out_shape=(rows_out, jax.ShapeDtypeStruct(keys_values.shape, BF16)),
+        compiler_params=params,
+        cost_estimate=pl.CostEstimate(flops=5 * flops // 2, bytes_accessed=8 * MIB, transcendentals=flops // 256),
+        name="attend_back",
+    )(query, keys_values, bias, log_total, grad_mixed)
+
+
+def places():
+    dp, z, core = lax.axis_index("dp"), lax.axis_index("z"), lax.axis_index("core")
+    return dp, z, core
+
+
+def line_of(z, lines):
+    left = z < lines // 2
+    step = jnp.where(left, 1, -1)
+    place = jnp.where(left, z, lines - 1 - z)
+    inner = z + step
+    outer = jnp.clip(z - step, 0, lines - 1)
+    return place, inner, outer
+
+
+def sum_kernel(dims, down, gate_up, out_part, qkv_part,
+               down_sum, gate_sum, up_sum, out_sum, qkv_sum,
+               own, first, second, pair_o, pair_q, mine_q,
+               own_sem, a2a_send, first_send, first_recv, second_send, second_recv,
+               core_send, core_recv, out_sem, pair_send, pair_recv):
+    dp_n, lines, n_down, n_blocks = dims
+    dp, z, core = places()
+    place, inner, outer = line_of(z, lines)
+    middle = lines // 2 - 1
+    rows = own.shape[1]
+    quarter = rows // 4
+    half = rows // 2
+    n_gu = dp_n * n_blocks
+    n_out = 2
+    n_main = own.shape[0]
+    other = 1 - core
+
+    barrier = pltpu.get_barrier_semaphore()
+    for shift in range(1, dp_n):
+        pl.semaphore_signal(barrier, device_id=(lax.rem(dp + shift, dp_n), z, core), device_id_type=MESH)
+    pl.semaphore_signal(barrier, device_id=(dp, z, other), device_id_type=MESH)
+    pl.semaphore_signal(barrier, device_id=(dp, inner, core), device_id_type=MESH)
+
+    @pl.when(place > 0)
+    def _():
+        pl.semaphore_signal(barrier, device_id=(dp, outer, core), device_id_type=MESH)
+
+    pl.semaphore_wait(barrier, dp_n + 1 + jnp.minimum(place, 1))
+
+    def pair_copies(side):
+        copies = []
+        for j in range(n_out):
+            for c in range(4):
+                copies.append((
+                    out_part.at[pl.ds(side * half + j * quarter, quarter), pl.ds(c * 512, 512)],
+                    j, c))
+        return copies
+
+    pair_q_copy = [
+        pltpu.make_async_remote_copy(
+            qkv_part.at[pl.ds(i * rows + other * half, half)], pair_q.at[i],
+            pair_send.at[i], pair_recv.at[i], device_id=(dp, z, other), device_id_type=MESH)
+        for i in range(dp_n)
+    ]
+    pair_o_copy = [
+        pltpu.make_async_remote_copy(
+            src, pair_o.at[j, pl.ds(c * quarter, quarter)], pair_send.at[dp_n + j * 4 + c], pair_recv.at[dp_n + j * 4 + c],
+            device_id=(dp, z, other), device_id_type=MESH)
+        for src, j, c in pair_copies(other)
+    ]
+
+    def down_copies(k):
+        return [
+            pltpu.make_async_copy(
+                down.at[pl.ds(k * quarter, quarter), pl.ds(c * 512, 512)], own.at[k, pl.ds(c * quarter, quarter)],
+                own_sem.at[k * 4 + c])
+            for c in range(4)
+        ]
+
+    gu_sem = 4 * n_down
+
+    def gu_copies(b):
+        local = pltpu.make_async_copy(
+            gate_up.at[pl.ds(dp * rows, rows), pl.ds(b * 512, 512)], own.at[n_down + b * dp_n + dp],
+            own_sem.at[gu_sem + b * dp_n + dp])
+        remote = []
+        for shift in range(1, dp_n):
+            to = lax.rem(dp + shift, dp_n)
+            remote.append(pltpu.make_async_remote_copy(
+                gate_up.at[pl.ds(to * rows, rows), pl.ds(b * 512, 512)], own.at[n_down + b * dp_n + dp],
+                a2a_send.at[b * dp_n + shift], own_sem.at[gu_sem + b * dp_n + dp],
+                device_id=(to, z, core), device_id_type=MESH))
+        return local, remote
+
+    def gu_wait(b, src):
+        pltpu.make_async_copy(
+            gate_up.at[pl.ds(0, rows), pl.ds(0, 512)], own.at[n_down + b * dp_n + src],
+            own_sem.at[gu_sem + b * dp_n + src]).wait()
+
+    @pl.loop(0, n_down)
+    def _(k):
+        for copy in down_copies(k):
+            copy.start()
+
+    @pl.loop(0, n_blocks)
+    def _(b):
+        local, remote = gu_copies(b)
+        local.start()
+        for copy in remote:
+            copy.start()
+
+    for copy in pair_q_copy + pair_o_copy:
+        copy.start()
+    o_base = gu_sem + n_gu
+    own_out = [
+        pltpu.make_async_copy(src, own.at[n_down + n_gu + j, pl.ds(c * quarter, quarter)], own_sem.at[o_base + j * 4 + c])
+        for src, j, c in pair_copies(core)
+    ]
+    q_base = o_base + 4 * n_out
+    own_qkv = [
+        pltpu.make_async_copy(qkv_part.at[pl.ds(i * rows + core * half, half)], mine_q.at[i], own_sem.at[q_base + i])
+        for i in range(dp_n)
+    ]
+    for copy in own_out + own_qkv:
+        copy.start()
+
+    def add(into, left, right):
+        into[...] = (left[...].astype(F32) + right[...].astype(F32)).astype(BF16)
+
+    qs_base = n_blocks * dp_n
+    for i in range(dp_n):
+        own_qkv[i].wait()
+        pair_q_copy[i].wait_recv()
+        add(mine_q.at[i], mine_q.at[i], pair_q.at[i])
+    qr_base = q_base + dp_n
+    piece = mine_q.shape[2] // 3
+    across_n = 512 // piece
+    per_chunk = 2 * across_n
+    n_q = 3 * dp_n // per_chunk
+    q_first = n_down + n_gu + n_out
+
+    def q_place(number):
+        spot = lax.rem(number, per_chunk)
+        column = lax.rem(spot, across_n) * piece
+        if not isinstance(column, int):
+            column = pl.multiple_of(column, 128)
+        return q_first + number // per_chunk, pl.ds((spot // across_n) * half, half), pl.ds(column, piece)
+
+    def q_own(number):
+        chunk, where, columns = q_place(number)
+        return own.at[chunk, where, columns]
+
+    q_remote = []
+    for shift in range(1, dp_n):
+        to = lax.rem(dp + shift, dp_n)
+        for j in range(3):
+            q_remote.append(pltpu.make_async_remote_copy(
+                mine_q.at[to, :, pl.ds(j * piece, piece)], q_own(dp * 3 + j),
+                a2a_send.at[qs_base + shift * 3 + j], own_sem.at[qr_base + dp * 3 + j],
+                device_id=(to, z, core), device_id_type=MESH))
+    for copy in q_remote:
+        copy.start()
+    for j in range(3):
+        pltpu.make_async_copy(
+            mine_q.at[dp, :, pl.ds(j * piece, piece)], q_own(dp * 3 + j), own_sem.at[qr_base + dp * 3 + j]).start()
+    for j in range(n_out):
+        for c in range(4):
+            own_out[j * 4 + c].wait()
+            pair_o_copy[j * 4 + c].wait_recv()
+        add(own.at[n_down + n_gu + j], own.at[n_down + n_gu + j], pair_o.at[j])
+
+    def to_inner(k, buf, n, across):
+        land, sem = (buf[2], second_recv) if across else (buf[1], first_recv)
+        return pltpu.make_async_remote_copy(
+            buf[0].at[n], land.at[n], first_send.at[k], sem.at[k], device_id=(dp, inner, core), device_id_type=MESH)
+
+    def stage_one(k, n, buf):
+        own_b, first_b, second_b = buf
+
+        @pl.when(place > 0)
+        def _():
+            to_inner(k, buf, n, False).wait_recv()
+            add(own_b.at[n], own_b.at[n], first_b.at[n])
+
+        @pl.when(place < middle)
+        def _():
+            to_inner(k, buf, n, False).start()
+
+        @pl.when(place == middle)
+        def _():
+            to_inner(k, buf, n, True).start()
+
+    def stage_two(k, n, buf, finish):
+        own_b, first_b, second_b = buf
+        across = to_inner(k, buf, n, True)
+        across.wait_recv()
+        across.wait_send()
+
+        @pl.when(place == middle)
+        def _():
+            add(second_b.at[n], own_b.at[n], second_b.at[n])
+
+        back = pltpu.make_async_remote_copy(
+            second_b.at[n], second_b.at[n], second_send.at[k], second_recv.at[k],
+            device_id=(dp, outer, core), device_id_type=MESH)
+
+        @pl.when(place > 0)
+        def _():
+            back.start()
+
+        finish(True)
+
+    def stage_three(k, n, buf, finish):
+        back = pltpu.make_async_remote_copy(
+            buf[2].at[n], buf[2].at[n], second_send.at[k], second_recv.at[k],
+            device_id=(dp, outer, core), device_id_type=MESH)
+
+        @pl.when(place > 0)
+        def _():
+            back.wait_send()
+
+        finish(False)
+
+    main = (own, first, second)
+
+    def both(k, c, src, dst, starting):
+        sem = k * 8 + c
+        local = pltpu.make_async_copy(src, dst, out_sem.at[sem])
+        remote = pltpu.make_async_remote_copy(
+            src, dst, core_send.at[sem], core_recv.at[sem], device_id=(dp, z, other), device_id_type=MESH)
+        if starting:
+            remote.start()
+            local.start()
+        else:
+            local.wait()
+            remote.wait_send()
+
+    def arrived(k, c, dst):
+        pltpu.make_async_remote_copy(
+            dst, dst, core_send.at[k * 8 + c], core_recv.at[k * 8 + c], device_id=(dp, z, other),
+            device_id_type=MESH).wait_recv()
+
+    f8 = n_down * quarter
+
+    def down_dst(k, c, who):
+        return down_sum.at[pl.ds(who * f8 + k * quarter, quarter), pl.ds(c * 512, 512)]
+
+    def finish_down(k, starting):
+        for c in range(4):
+            both(k, c, second.at[k, pl.ds(c * quarter, quarter)], down_dst(k, c, core), starting)
+
+    def gu_dst(m, c, who):
+        b, src = m // dp_n, lax.rem(m, dp_n)
+        target = (gate_sum, up_sum)[c]
+        return target.at[:, pl.ds((2 * src + who) * f8 + b * 256, 256)]
+
+    def finish_gu(m, starting):
+        k = n_down + m
+        for c in range(2):
+            both(k, c, second.at[k, :, pl.ds(c * 256, 256)], gu_dst(m, c, core), starting)
+
+    def out_dst(j, c, who):
+        return out_sum.at[pl.ds(who * half + j * quarter, quarter), pl.ds(c * 512, 512)]
+
+    def finish_out(j, starting):
+        k = n_down + n_gu + j
+        for c in range(4):
+            both(k, c, second.at[k, pl.ds(c * quarter, quarter)], out_dst(j, c, core), starting)
+
+    def q_dst(number, who):
+        column = lax.rem(number, 3) * piece
+        return qkv_sum.at[number // 3, pl.ds(who * half, half), pl.ds(pl.multiple_of(column, 128), piece)]
+
+    def finish_q(j, starting):
+        for c in range(per_chunk):
+            chunk, where, columns = q_place(c)
+            both(q_first + j, c, second.at[q_first + j, where, columns], q_dst(j * per_chunk + c, core), starting)
+
+    lag = 2 + 4 * (middle - place)
+    most = 2 + 4 * middle
+
+    def slot_one(k):
+        @pl.when(k < n_down)
+        def _():
+            for copy in down_copies(k):
+                copy.wait()
+
+        @pl.when((k >= n_down) & (k < n_down + n_gu))
+        def _():
+            m = k - n_down
+            gu_wait(m // dp_n, lax.rem(m, dp_n))
+
+        @pl.when(k >= q_first)
+        def _():
+            for c in range(per_chunk):
+                number = (k - q_first) * per_chunk + c
+                pltpu.make_async_copy(
+                    mine_q.at[0, :, pl.ds(0, piece)], q_own(number), own_sem.at[qr_base + number]).wait()
+
+        stage_one(k, k, main)
+
+    def slot_fin(k, starting):
+        @pl.when(k < n_down)
+        def _():
+            finish_down(k, starting)
+
+        @pl.when((k >= n_down) & (k < n_down + n_gu))
+        def _():
+            finish_gu(k - n_down, starting)
+
+        @pl.when((k >= n_down + n_gu) & (k < q_first))
+        def _():
+            finish_out(k - n_down - n_gu, starting)
+
+        @pl.when(k >= q_first)
+        def _():
+            finish_q(k - q_first, starting)
+
+    @pl.loop(0, n_main + most)
+    def _(t):
+        @pl.when(t < n_main)
+        def _():
+            slot_one(t)
+
+        @pl.when((t >= lag) & (t - lag < n_main))
+        def _():
+            k = t - lag
+            stage_two(k, k, main, partial(slot_fin, k))
+
+    @pl.loop(0, n_main)
+    def _(k):
+        stage_three(k, k, main, partial(slot_fin, k))
+
+        @pl.when(k < n_down)
+        def _():
+            for c in range(4):
+                arrived(k, c, down_dst(k, c, other))
+
+        @pl.when((k >= n_down) & (k < n_down + n_gu))
+        def _():
+            for c in range(2):
+                arrived(k, c, gu_dst(k - n_down, c, other))
+
+        @pl.when((k >= n_down + n_gu) & (k < q_first))
+        def _():
+            for c in range(4):
+                arrived(k, c, out_dst(k - n_down - n_gu, c, other))
+
+        @pl.when(k >= q_first)
+        def _():
+            for c in range(per_chunk):
+                arrived(k, c, q_dst((k - q_first) * per_chunk + c, other))
+
+    @pl.loop(0, n_blocks)
+    def _(b):
+        for copy in gu_copies(b)[1]:
+            copy.wait_send()
+
+    for copy in q_remote + pair_q_copy + pair_o_copy:
+        copy.wait_send()
+
+
+def sum_grads(down, gate_up, out_part, qkv_part, dp_n, lines, collective_id):
+    width = out_part.shape[1]
+    rows = width // dp_n
+    f8 = down.shape[0]
+    n_down = f8 // (rows // 4)
+    n_blocks = f8 // 256
+    cols = qkv_part.shape[1]
+    n_main = n_down + dp_n * n_blocks + 2 + dp_n * cols // 1024
+    hbm = pl.BlockSpec(memory_space=pl.ANY)
+    chunk = pltpu.VMEM((n_main, rows, 512), BF16)
+    small = pltpu.VMEM((dp_n, rows // 2, cols), BF16)
+    dma = pltpu.SemaphoreType.DMA
+    own_sems = 4 * n_down + dp_n * n_blocks + 8 + 4 * dp_n
+    return pl.pallas_call(
+        partial(sum_kernel, (dp_n, lines, n_down, n_blocks)),
+        out_shape=(
+            jax.ShapeDtypeStruct((2 * f8, width), BF16),
+            jax.ShapeDtypeStruct((rows, 2 * dp_n * f8), BF16),
+            jax.ShapeDtypeStruct((rows, 2 * dp_n * f8), BF16),
+            jax.ShapeDtypeStruct((rows, width), BF16),
+            jax.ShapeDtypeStruct((dp_n, rows, cols), BF16),
+        ),
+        in_specs=[hbm] * 4,
+        out_specs=(hbm,) * 5,
+        scratch_shapes=[
+            chunk, chunk, chunk,
+            pltpu.VMEM((2, rows, 512), BF16), small, small,
+            dma((own_sems,)), dma((n_blocks * dp_n + 3 * dp_n,)),
+            dma((n_main,)), dma((n_main,)), dma((n_main,)), dma((n_main,)),
+            dma((n_main * 8,)), dma((n_main * 8,)), dma((n_main * 8,)),
+            dma((dp_n + 8,)), dma((dp_n + 8,)),
+        ],
+        compiler_params=pltpu.CompilerParams(collective_id=collective_id, has_side_effects=True, vmem_limit_bytes=60 * MIB),
+        cost_estimate=pl.CostEstimate(flops=10**9, bytes_accessed=10**9, transcendentals=0),
+        name="sum_grads",
+    )(down, gate_up, out_part, qkv_part)
 
 
 def columns_to_owner(weight, dp, parts, part):
@@ -114,7 +574,7 @@
     key_places = jnp.repeat(stretch_map, half, total_repeat_length=length) * half + jnp.tile(
         jnp.arange(half, dtype=jnp.int32), stretches
     )
-    group_places = jnp.tile(query_places, group)
+    bias = jnp.where(key_places[:, None] <= query_places[None, :], 0.0, MASKED_SCORE).astype(F32)
     frequency = jnp.power(F32(ROPE_BASE), -2.0 * jnp.arange(head // 2, dtype=F32) / head)
     positions = lax.all_gather(pos_ids[0], "dp").reshape(tokens)
     angles = positions.astype(F32)[:, None] * frequency[None, :]
@@ -140,26 +600,10 @@
     key_rot = apply_rotary(key_hat * k_gain_f, cosine, sine).astype(BF16)
     value_low = dot(normed_one, wv).astype(BF16)
     keys_values = jnp.concatenate([key_rot.reshape(dp, rows, kv_heads * head), value_low.reshape(dp, rows, kv_heads * head)], axis=2)
-    kv_all = lax.all_gather(keys_values, ("z", "core"), axis=1, tiled=True)
-    kv_all = kv_all.reshape(dp, length, 2, kv_heads, head).transpose(2, 0, 3, 1, 4).reshape(2, dp * kv_heads, length, head)
-    key_heads, value_heads = kv_all[0], kv_all[1]
-
-    def to_heads(values):
-        return (
-            values.reshape(dp, rows, kv_heads, group, head).transpose(0, 2, 3, 1, 4).reshape(dp * kv_heads, group * rows, head)
-        )
-
-    def from_heads(values):
-        return (
-            values.reshape(dp, kv_heads, group, rows, head).transpose(0, 3, 1, 2, 4).reshape(tokens, q_heads * head)
-        )
-
-    query_grouped = to_heads(query_rot)
-    mixed, log_total = lax.map(
-        partial(attend_head, query_places=group_places, key_places=key_places, score_scale=scale),
-        (query_grouped, key_heads, value_heads),
-    )
-    mixed_low = from_heads(mixed).astype(BF16)
+    keys_values = lax.all_gather(keys_values, ("z", "core"))
+    query_rows = query_rot.reshape(dp, rows, q_heads * head)
+    mixed, log_total = attend(query_rows, keys_values, bias, head, group)
+    mixed_low = mixed.reshape(tokens, q_heads * head)
     attn_part = dot(mixed_low, w_out)
     attn_out = jnp.sum(lax.all_to_all(attn_part.astype(BF16).reshape(dp, rows, width), "dp", 0, 0).astype(F32), axis=0)
     hidden_in = own_x + attn_out
@@ -192,15 +636,14 @@
 
     grad_hidden_all = lax.all_gather(grad_hidden.astype(BF16), "dp", axis=0, tiled=True)
     grad_mixed = contract_cols(grad_hidden_all, w_out).astype(BF16)
-    grad_q, grad_k, grad_v = lax.map(
-        partial(attend_back, query_places=group_places, key_places=key_places, score_scale=scale),
-        (query_grouped, key_heads, value_heads, to_heads(grad_mixed), log_total),
+    grad_q, grad_kv = attend(
+        query_rows, keys_values, bias, head, group, grad_mixed.reshape(dp, rows, q_heads * head), log_total
     )
-    grad_query_rot = from_heads(grad_q).astype(BF16).astype(F32).reshape(tokens, q_heads, head)
-    kv_grad = jnp.stack([grad_k, grad_v]).reshape(2, dp, kv_heads, length, head).transpose(3, 1, 0, 2, 4).astype(BF16)
-    kv_grad = lax.psum_scatter(kv_grad, ("z", "core"), scatter_dimension=0, tiled=True).transpose(1, 0, 2, 3, 4).reshape(tokens, 2, kv_heads, head)
-    grad_key_rot = kv_grad[:, 0].astype(F32)
-    grad_value_low = kv_grad[:, 1].reshape(tokens, kv_heads * head)
+    grad_query_rot = grad_q.astype(F32).reshape(tokens, q_heads, head)
+    grad_kv = jnp.sum(lax.all_to_all(grad_kv, ("z", "core"), 0, 0).astype(F32), axis=0).astype(BF16)
+    grad_kv = grad_kv.reshape(tokens, 2, kv_heads, head)
+    grad_key_rot = grad_kv[:, 0].astype(F32)
+    grad_value_low = grad_kv[:, 1].reshape(tokens, kv_heads * head)
     grad_query_gained = rotate_back(grad_query_rot, cosine, sine)
     q_gain_grad = jnp.sum(grad_query_gained * query_hat, axis=(0, 1))
     grad_query_pre = normalize_back(grad_query_gained * q_gain_f, query_hat, query_inverse).reshape(tokens, -1).astype(BF16)
@@ -214,26 +657,21 @@
     gain_grad_one = jnp.sum(grad_normed_one * hat_one, axis=0)
     input_grad = (grad_hidden + normalize_back(grad_normed_one * gain_one, hat_one, inverse_one)).astype(BF16)[None]
 
-    def finish_columns(grad):
-        return rows_to_owner(lax.psum(grad.astype(BF16), "z"), dp)
-
-    down = lax.all_gather(lax.psum(contract_rows(act_low, cot_all).astype(BF16), "z"), "core", axis=0, tiled=True)
-
-    def finish_hidden(grad):
-        mine = lax.all_gather(finish_columns(grad), "core")
-        return mine.transpose(2, 1, 0, 3).reshape(width // dp, hidden).astype(F32)
-
-    gate_grad = finish_hidden(contract_rows(normed_two_all, grad_gate))
-    up_grad = finish_hidden(contract_rows(normed_two_all, grad_up))
-    out_grad = lax.psum(contract_rows(mixed_low, grad_hidden_all).astype(BF16), ("z", "core")).astype(F32)
-
-    def finish_heads(grad):
-        mine = rows_to_owner(lax.psum(grad.astype(BF16), ("z", "core")), dp)
-        return mine.transpose(1, 0, 2).reshape(width // dp, -1).astype(F32)
-
-    query_grad = finish_heads(contract_rows(normed_one, grad_query_pre))
-    key_grad = finish_heads(contract_rows(normed_one, grad_key_pre))
-    value_grad = finish_heads(contract_rows(normed_one, grad_value_low))
+    down_part = contract_rows(act_low, cot_all).astype(BF16)
+    blocks_n = slice_rows // 256
+    grad_both = jnp.stack(
+        [grad_gate.reshape(plane, blocks_n, 256), grad_up.reshape(plane, blocks_n, 256)], axis=2
+    ).reshape(plane, 2 * slice_rows)
+    both_part = contract_rows(normed_two_all, grad_both).astype(BF16)
+    out_part = contract_rows(mixed_low, grad_hidden_all).astype(BF16)
+    grad_qkv = jnp.concatenate([grad_query_pre, grad_key_pre, grad_value_low], axis=1)
+    qkv_part = contract_rows(normed_one, grad_qkv).astype(BF16)
+    down, gate_grad, up_grad, out_grad, qkv_sum = sum_grads(down_part, both_part, out_part, qkv_part, dp, lines, 1)
+    q_cols, kv_cols = q_heads * head, kv_heads * head
+    qkv_rows = qkv_sum.transpose(1, 0, 2).astype(F32)
+    query_grad = qkv_rows[:, :, :q_cols].reshape(width // dp, query_width)
+    key_grad = qkv_rows[:, :, q_cols : q_cols + kv_cols].reshape(width // dp, key_width)
+    value_grad = qkv_rows[:, :, q_cols + kv_cols :].reshape(width // dp, key_width)
     gains = jnp.concatenate([gain_grad_one, gain_grad_two, q_gain_grad, k_gain_grad])
     gains = lax.psum(gains, ("dp", "z", "core"))
     place = lax.axis_index("dp")
@@ -242,8 +680,8 @@
     ffn_gain_grad = lax.dynamic_slice_in_dim(gains, width + place * piece, piece, 0)
     return (
         output, input_grad, attn_gain_grad, query_grad, key_grad, value_grad,
-        gains[2 * width : 2 * width + head], gains[2 * width + head :], out_grad, ffn_gain_grad,
-        gate_grad, up_grad, down.astype(F32),
+        gains[2 * width : 2 * width + head], gains[2 * width + head :], out_grad.astype(F32), ffn_gain_grad,
+        gate_grad.astype(F32), up_grad.astype(F32), down.astype(F32),
     )
 
 

time: 1880 us -> 1090 us (0.58)
  waiting for transfers between devices: 669 us -> 159 us
  Pallas kernels: 0 us -> 416 us
  local copies, waits for them, and re-layouts: 467 us -> 108 us
  other arithmetic: 241 us -> 92.3 us
  matrix products: 222 us -> 111 us
  blocking collectives: 189 us -> 134 us
    pallas_call x0 -> x3, Pallas kernels: none -> 416 us  [the longest x1 389 us: sum_grads(): pl.pallas_call(partial(sum_kernel, (dp_n, lines, n_down, n_blocks)), out_...]
    psum x2 -> x0, waiting for transfers between devices: 391 us -> none  [the longest x1 391 us: finish_columns(): return rows_to_owner(lax.psum(grad.astype(BF16), 'z'), dp)]
    unnamed x124 -> x96, local copies, waits for them, and re-layouts: 302 us -> 48.3 us
    convert_element_type x11 -> x2, local copies, waits for them, and re-layouts: 115 us -> 1.24 us  [local(): query_rot = apply_rotary(query_hat * q_gain_f, cosine, sine).astype(BF16)]
    add x16 -> x1, other arithmetic: 89.2 us -> 5.84 us  [local(): jnp.repeat(stretch_map, half, total_repeat_length=length) * half]
    gather x32 -> x2, other arithmetic: 72.6 us -> 4.62 us  [local(): jnp.repeat(stretch_map, half, total_repeat_length=length) * half]
    all_to_all x1 -> x0, blocking collectives: 53.8 us -> none  [rows_to_owner(): return lax.all_to_all(grad.reshape(dp, rows // dp, width), 'dp', 0, 0)]
    dot_general x31 -> x7, matrix products: 83.8 us -> 41.1 us  [contract_cols(): lax.dot_general(left, right, (((1,), (1,)), ((), ())), preferred_element_...]
  transfers between devices with their start and end apart: 23 -> 14, of which waited for: 13 -> 7; matrix products, arithmetic and copies ran while one was open for 15% -> 22% of each run, Pallas kernels for 0% -> 38%
where the time goes in v2:
time: 1090 us; the launch traced here: 1080 us
  Pallas kernels  416 us (38%)
  waiting for transfers between devices  159 us (15%)
  blocking collectives  134 us (12%)
  matrix products  111 us (10%)
  local copies, waits for them, and re-layouts  108 us (10%)
  other arithmetic  92.3 us (8%)
  starting transfers between devices  42.8 us (4%)
  between operations  14.7 us (1%)
    pallas_call x1, Pallas kernels, sum_grads(): pl.pallas_call(partial(sum_kernel, (dp_n, lines, n_down, n_blocks)), out_...  389 us
    all_to_all x5, waiting for transfers between devices, columns_to_owner(): out = lax.all_to_all(mine.transpose(1, 0, 2), 'dp', 0, 0)  109 us
    all_to_all x1, blocking collectives, plane_sum(): lax.all_to_all(values.reshape(dp * cores, rows, width).astype(BF16), ('dp...  51.8 us
    unnamed x96, local copies, waits for them, and re-layouts  48.3 us
    dot_general x7, matrix products, dot(): return jnp.dot(left, right, preferred_element_type=F32)  41.7 us
    dot_general x7, matrix products, contract_cols(): lax.dot_general(left, right, (((1,), (1,)), ((), ())), preferred_element_...  41.1 us
    psum x1, blocking collectives, local(): gains = lax.psum(gains, ('dp', 'z', 'core'))  38.2 us
    all_gather x1, waiting for transfers between devices, local(): lax.all_gather(grad_hidden.astype(BF16), 'dp', axis=0, tiled=True)  31.8 us
  transfers between devices with their start and end apart: 14, of which 7 were waited for; matrix products, arithmetic and copies ran while one was open for 22% of the time, Pallas kernels for 38%

profile of v2, /device:TPU:0, one launch (start us, length us, event | category | flops | bytes accessed | tf_op | source)
XLA Modules:
  0.0 1077.1 jit_solution(2377001020198551112)
XLA Ops:
  17.4 7.0 all-to-all-done.1
  28.6 8.4 all-gather.3
  37.0 8.3 all-gather.2
  75.8 5.8 fusion.40
  82.6 12.7 %all-to-all-done = bf16[4,512,512]{2,1,0:T(8,128)(2,1)} async-done(((bf16[4,512,512]{2,1,0:T(8,128)(2,1)}), bf16[4,512,512]{2,1,0:T(8,128)(2,1)}, u32[]{:S(2)}, u32[]{:S(2)}) %all-to-all-start) | async-done | bytes 2097184 | tf_op jit(solution)/shard_map/all_to_all | solution.py:542
  105.6 11.2 %attend.1 = (bf16[4,128,512]{2,1,0:T(8,128)(2,1)}, f32[4,2,512]{2,1,0:T(2,128)}) custom-call(bf16[4,128,512]{2,1,0:T(8,128)(2,1)} %copy.123.query, bf16[8,4,128,256]{3,2,1,0:T(8,128)(2,1)} %bitcast.267, f32[1024,128]{1,0:T(8,128)} %compare_select_fusion.bias), custom_call_target="tpu_custom_call" | custom-call | flops 1073741824 | bytes 4194304 | tf_op jit(solution)/shard_map/attend/pallas_call | solution.py:121
  125.1 27.5 %all-gather.4 = bf16[4,1,512]{2,1,0:T(2,128)(2,1)S(1)} all-gather(bf16[1,1,512]{2,1,0:T(2,128)(2,1)S(1)} %reshape.562), channel_id=1, replica_groups=mesh['dp'=4,'z'=4,'core'=2] {'dp'}, dimensions={0}, use_global_device_ids=true | all-gather | bytes 5120 | tf_op jit(solution)/shard_map/all_gather | solution.py:584
  157.9 12.0 %copy.124 = bf16[512,8192]{0,1:T(8,128)(2,1)} copy(bf16[512,8192]{1,0:T(8,128)(2,1)} %param.26) | data formatting | bytes 16777216 | tf_op args[9]
  169.9 12.0 %copy.126 = bf16[512,8192]{0,1:T(8,128)(2,1)} copy(bf16[512,8192]{1,0:T(8,128)(2,1)} %param.27) | data formatting | bytes 16777216 | tf_op args[10]
  181.9 7.4 constant_dynamic-slice_fusion
  189.3 6.3 copy.127
  201.1 6.2 copy.125
  207.3 55.7 %all-to-all-done.5 = bf16[4,512,1024]{2,1,0:T(8,128)(2,1)} async-done(((bf16[4,512,1024]{2,1,0:T(8,128)(2,1)}), bf16[4,512,1024]{2,1,0:T(8,128)(2,1)}, u32[]{:S(2)}, u32[]{:S(2)}) %all-to-all-start.5) | async-done | bytes 4194336 | tf_op jit(solution)/shard_map/all_to_all | solution.py:542
  268.1 10.0 fusion.56
  278.1 33.4 %all-to-all-done.4 = bf16[4,512,1024]{2,1,0:T(8,128)(2,1)} async-done(((bf16[4,512,1024]{2,1,0:T(8,128)(2,1)}), bf16[4,512,1024]{2,1,0:T(8,128)(2,1)}, u32[]{:S(2)}, u32[]{:S(2)}) %all-to-all-start.4) | async-done | bytes 4194336 | tf_op jit(solution)/shard_map/all_to_all | solution.py:542
  311.5 10.0 fusion.55
  321.6 13.6 %fusion.6 = (bf16[1024,1024]{0,1:T(8,128)(2,1)S(1)}, bf16[1024,1024]{0,1:T(8,128)(2,1)S(1)}, bf16[1024,1024]{0,1:T(8,128)(2,1)}) fusion(f32[1024,1024]{0,1:T(8,128)} %fusion.55, f32[1024,1024]{0,1:T(8,128)} %fusion.56, bf16[1024,2048]{1,0:T(8,128)(2,1)} %bitcast.265, bf16[2048,2048]{1,0:T(8,128)(2,1)} %param.28, s32[]{:T(128)S(6)} %select_n.79), kind=kOutput, calls=%fused_computation.16 | convolution fusion | flops 4310695936 | bytes 23068676 | tf_op jit(solution)/shard_map/dot_general | solution.py:28
  335.2 7.9 fusion.57
  343.1 7.2 add_convert_fusion
  350.3 51.8 %all_to_all.50 = bf16[8,128,2048]{2,1,0:T(8,128)(2,1)S(1)} all-to-all(bf16[8,128,2048]{2,1,0:T(8,128)(2,1)S(1)} %bitcast.229), channel_id=1, replica_groups=mesh['dp'=4,'z'=4,'core'=2] {'dp','core'}, dimensions={0} | all-to-all | bytes 8388608 | tf_op jit(solution)/shard_map/all_to_all | solution.py:619
  405.4 9.4 convolution_convert_fusion.2
  424.6 6.0 convolution_convert_fusion.1.down
  430.6 31.8 %all-gather.15.cloned.1.call-done = bf16[512,2048]{1,0:T(8,128)(2,1)} async-done(((bf16[128,2048]{1,0:T(8,128)(2,1)}), bf16[512,2048]{1,0:T(8,128)(2,1)}) %all-gather.15.cloned.1.call-update) | async-done | bytes 2097168 | tf_op jit(solution)/shard_map/all_gather | solution.py:637
  466.0 16.3 %attend_back.1 = (bf16[4,128,512]{2,1,0:T(8,128)(2,1)}, bf16[8,4,128,256]{3,2,1,0:T(8,128)(2,1)}) custom-call(bf16[4,128,512]{2,1,0:T(8,128)(2,1)} %copy.123.query, bf16[8,4,128,256]{3,2,1,0:T(8,128)(2,1)} %bitcast.268, f32[1024,128]{1,0:T(8,128)} %compare_select_fusion.bias, f32[4,2,512]{2,1,0:T(2,128)} %get-tuple-element.35.log_total, ...), custom_call_target="tpu_custom_call" | custom-call | flops 2684354560 | bytes 8388608 | tf_op jit(solution)/shard_map/attend_back/pallas_call | solution.py:131
  487.3 14.1 %convolution_convert_fusion.gate_up = bf16[2048,2048]{1,0:T(8,128)(2,1)} fusion(bf16[1024,2048]{1,0:T(8,128)(2,1)} %bitcast.264, bf16[1024,2048]{0,1:T(8,128)(2,1)} %bitcast.228), kind=kOutput, calls=%fused_computation.3 | convolution fusion | flops 8594128896 | bytes 16777216 | tf_op jit(solution)/shard_map/dot_general | solution.py:24
  520.4 16.1 %all-to-all-done.8 = bf16[8,4,128,256]{3,2,1,0:T(8,128)(2,1)} async-done(((bf16[8,4,128,256]{3,2,1,0:T(8,128)(2,1)}), bf16[8,4,128,256]{3,2,1,0:T(8,128)(2,1)}, u32[]{:S(2)}, u32[]{:S(2)}) %all-to-all-start.8) | async-done | bytes 2097184 | tf_op jit(solution)/shard_map/all_to_all | solution.py:643
  563.1 388.5 %sum_grads.1 = (bf16[2048,2048]{1,0:T(8,128)(2,1)}, bf16[512,8192]{1,0:T(8,128)(2,1)}, bf16[512,8192]{1,0:T(8,128)(2,1)}, bf16[512,2048]{1,0:T(8,128)(2,1)}, bf16[4,512,768]{2,1,0:T(8,128)(2,1)}) custom-call(bf16[1024,2048]{1,0:T(8,128)(2,1)} %convolution_convert_fusion.1.down, bf16[2048,2048]{1,0:T(8,128)(2,1)} %convolution_convert_fusion.gate_up, ...), custom_call_target="tpu_custom_call" | custom-call | flops 1000000000 | bytes 1000000000 | tf_op jit(solution)/shard_map/sum_grads/pallas_call | solution.py:512
  964.7 5.3 copy.136
  987.3 11.7 %convert_element_type.215 = f32[512,8192]{1,0:T(8,128)} convert(bf16[512,8192]{1,0:T(8,128)(2,1)} %get-tuple-element.40) | non-fusion elementwise | flops 4194304 | bytes 25165824 | tf_op jit(solution)/shard_map/convert_element_type | solution.py:684
  999.0 11.7 %convert_element_type.216 = f32[512,8192]{1,0:T(8,128)} convert(bf16[512,8192]{1,0:T(8,128)(2,1)} %get-tuple-element.41) | non-fusion elementwise | flops 4194304 | bytes 25165824 | tf_op jit(solution)/shard_map/convert_element_type | solution.py:684
  1010.8 11.7 %convert_element_type.217 = f32[2048,2048]{1,0:T(8,128)} convert(bf16[2048,2048]{1,0:T(8,128)(2,1)} %get-tuple-element.42) | non-fusion elementwise | flops 4194304 | bytes 25165824 | tf_op jit(solution)/shard_map/convert_element_type | solution.py:684
  1027.1 38.2 %psum.7 = f32[4224]{0:T(1024)S(1)} all-reduce(f32[4224]{0:T(1024)S(1)} %concatenate.32), channel_id=1, replica_groups=mesh['dp'=4,'z'=4,'core'=2] {'dp','z','core'}, use_global_device_ids=true, to_apply=%region_19.20 | all-reduce | flops 4224 | bytes 33792 | tf_op jit(solution)/shard_map/psum | solution.py:676
  (207 shorter events, 187.1 us)
Async XLA Ops:
  7.2 109.6 %copy-start = (bf16[512,2048]{1,0:T(8,128)(2,1)S(1)}, bf16[512,2048]{1,0:T(8,128)(2,1)}, u32[]{:S(2)}) copy-start(bf16[512,2048]{1,0:T(8,128)(2,1)} %param.24) | copy-start | bytes 6291460
  7.2 21.4 %copy-start.40 = (bf16[64]{0:T(256)(128)(2,1)S(1)}, bf16[64]{0:T(256)(128)(2,1)}, u32[]{:S(2)}) copy-start(bf16[64]{0:T(256)(128)(2,1)} %param.23) | copy-start | bytes 388
  7.2 21.4 %copy-start.36 = (bf16[512]{0:T(512)(128)(2,1)S(1)}, bf16[512]{0:T(512)(128)(2,1)}, u32[]{:S(2)}) copy-start(bf16[512]{0:T(512)(128)(2,1)} %param.18) | copy-start | bytes 3076
  7.2 21.4 %copy-start.38 = (s32[1,128]{1,0:T(1,128)S(1)}, s32[1,128]{1,0:T(1,128)}, u32[]{:S(2)}) copy-start(s32[1,128]{1,0:T(1,128)} %param.30) | copy-start | bytes 1540
  7.2 41.5 %all-gather.17.cloned.1.call-start = ((), (), s32[]{:S(2)}) async-start(), calls=%async_computation.13 | async-start | bytes 2621440 | tf_op jit(solution)/shard_map/all_gather | solution.py:594
  10.2 14.2 %all-to-all-start.1 = ((bf16[4,512,128]{2,1,0:T(8,128)(2,1)}), bf16[4,512,128]{2,1,0:T(8,128)(2,1)S(1)}, u32[]{:S(2)}, u32[]{:S(2)}) async-start(bf16[4,512,128]{2,1,0:T(8,128)(2,1)} %copy.118), calls=%async_computation.1 | async-start | bytes 1048576 | tf_op jit(solution)/shard_map/all_to_all | solution.py:542
  24.4 29.0 %copy-start.8 = (bf16[4,512,128]{2,1,0:T(8,128)(2,1)}, bf16[4,512,128]{2,1,0:T(8,128)(2,1)S(1)}, u32[]{:S(2)}) copy-start(bf16[4,512,128]{2,1,0:T(8,128)(2,1)S(1)} %all-to-all-done.1) | copy-start | bytes 1572868
  24.4 22.3 %all-to-all-start.2 = ((bf16[4,512,128]{1,2,0:T(8,128)(2,1)}), bf16[4,512,128]{1,2,0:T(8,128)(2,1)}, u32[]{:S(2)}, u32[]{:S(2)}) async-start(bf16[4,512,128]{1,2,0:T(8,128)(2,1)} %bitcast.17), calls=%async_computation.2 | async-start | bytes 1048576 | tf_op jit(solution)/shard_map/all_to_all | solution.py:542
  28.5 77.1 %all-gather.19.cloned.1.call-start = ((), (), s32[]{:S(2)}) async-start(), calls=%async_computation.14 | async-start | bytes 2359296 | tf_op jit(solution)/shard_map/all_gather | solution.py:603
  28.6 24.8 %copy-start.28 = (f32[64]{0:T(128)}, f32[64]{0:T(128)S(1)}, u32[]{:S(2)}) copy-start(f32[64]{0:T(128)S(1)} %convert_element_type.176) | copy-start | bytes 772
  45.3 54.0 %copy-start.22 = (f32[4,1,512]{2,1,0:T(1,128)}, f32[4,1,512]{2,1,0:T(1,128)S(1)}, u32[]{:S(2)}) copy-start(f32[4,1,512]{2,1,0:T(1,128)S(1)} %convert_element_type.223) | copy-start | bytes 24580
  50.8 48.5 %copy-start.32 = (f32[512]{0:T(512)}, f32[512]{0:T(512)S(1)}, u32[]{:S(2)}) copy-start(f32[512]{0:T(512)S(1)} %add_rsqrt_fusion.2) | copy-start | bytes 6148
  61.5 8.8 copy-start.21
  61.5 9.6 copy-start.27
  65.7 29.6 %all-to-all-start = ((bf16[4,512,512]{2,1,0:T(8,128)(2,1)}), bf16[4,512,512]{2,1,0:T(8,128)(2,1)}, u32[]{:S(2)}, u32[]{:S(2)}) async-start(bf16[4,512,512]{2,1,0:T(8,128)(2,1)} %copy.115), calls=%async_computation | async-start | bytes 4194304 | tf_op jit(solution)/shard_map/all_to_all | solution.py:542
  120.4 32.1 %all-to-all-start.3 = ((bf16[4,128,2048]{2,1,0:T(8,128)(2,1)}), bf16[4,128,2048]{2,1,0:T(8,128)(2,1)}, u32[]{:S(2)}, u32[]{:S(2)}) async-start(bf16[4,128,2048]{2,1,0:T(8,128)(2,1)} %bitcast.236), calls=%async_computation.3 | async-start | bytes 4194304 | tf_op jit(solution)/shard_map/all_to_all | solution.py:608
  125.0 143.0 %all-gather.11.cloned.1.call-start = ((), (), s32[]{:S(2)}) async-start(), calls=%async_computation.10 | async-start | bytes 4718592 | tf_op jit(solution)/shard_map/all_gather | solution.py:616
  195.6 67.4 %all-to-all-start.5 = ((bf16[4,512,1024]{2,1,0:T(8,128)(2,1)}), bf16[4,512,1024]{2,1,0:T(8,128)(2,1)}, u32[]{:S(2)}, u32[]{:S(2)}) async-start(bf16[4,512,1024]{2,1,0:T(8,128)(2,1)} %bitcast.221), calls=%async_computation.5 | async-start | bytes 8388608 | tf_op jit(solution)/shard_map/all_to_all | solution.py:542
  200.6 121.0 %all-gather.13.cloned.1.call-start = ((), (), s32[]{:S(2)}) async-start(), calls=%async_computation.11 | async-start | bytes 4718592 | tf_op jit(solution)/shard_map/all_gather | solution.py:616
  263.0 48.5 %all-to-all-start.4 = ((bf16[4,512,1024]{2,1,0:T(8,128)(2,1)}), bf16[4,512,1024]{2,1,0:T(8,128)(2,1)}, u32[]{:S(2)}, u32[]{:S(2)}) async-start(bf16[4,512,1024]{2,1,0:T(8,128)(2,1)} %bitcast.220), calls=%async_computation.4 | async-start | bytes 8388608 | tf_op jit(solution)/shard_map/all_to_all | solution.py:542
  268.0 194.4 %all-gather.15.cloned.1.call-start = ((), (), s32[]{:S(2)}) async-start(), calls=%async_computation.12 | async-start | bytes 2621440 | tf_op jit(solution)/shard_map/all_gather | solution.py:637
  404.2 10.7 copy-start.29
  414.8 67.5 %all-to-all-start.6 = ((bf16[8,128,2048]{2,1,0:T(8,128)(2,1)}), bf16[8,128,2048]{2,1,0:T(8,128)(2,1)}, u32[]{:S(2)}, u32[]{:S(2)}) async-start(bf16[8,128,2048]{2,1,0:T(8,128)(2,1)} %bitcast.227), calls=%async_computation.6 | async-start | bytes 8388608 | tf_op jit(solution)/shard_map/all_to_all | solution.py:619
  482.3 54.1 %all-to-all-start.8 = ((bf16[8,4,128,256]{3,2,1,0:T(8,128)(2,1)}), bf16[8,4,128,256]{3,2,1,0:T(8,128)(2,1)}, u32[]{:S(2)}, u32[]{:S(2)}) async-start(bf16[8,4,128,256]{3,2,1,0:T(8,128)(2,1)} %get-tuple-element.37), calls=%async_computation.8 | async-start | bytes 4194304 | tf_op jit(solution)/shard_map/all_to_all | solution.py:643
  520.4 23.5 %copy-start.13 = (f32[512,2,64]{0,2,1:T(8,128)S(1)}, f32[512,2,64]{0,2,1:T(8,128)}, u32[]{:S(2)}) copy-start(f32[512,2,64]{0,2,1:T(8,128)} %copy-done.12) | copy-start | bytes 786436
  520.4 23.5 %copy-start.25 = (f32[512,2]{0,1:T(2,128)S(1)}, f32[512,2]{0,1:T(2,128)}, u32[]{:S(2)}) copy-start(f32[512,2]{0,1:T(2,128)} %copy-done.24) | copy-start | bytes 12292
  550.3 9.1 copy-start.20
  550.3 9.1 copy-start.23
  550.3 9.1 copy-start.33
  550.3 472.2 %all-to-all-start.9 = ((bf16[4,128,2048]{2,1,0:T(8,128)(2,1)}), bf16[4,128,2048]{2,1,0:T(8,128)(2,1)}, u32[]{:S(2)}, u32[]{:S(2)}) async-start(bf16[4,128,2048]{2,1,0:T(8,128)(2,1)} %bitcast.224), calls=%async_computation.9 | async-start | bytes 4194304 | tf_op jit(solution)/shard_map/all_to_all | solution.py:655
  1010.8 14.8 %copy-start.31 = (f32[128]{0:T(128)S(1)}, f32[128]{0:T(128)}, u32[]{:S(2)}) copy-start(f32[128]{0:T(128)} %add_rsqrt_fusion.3) | copy-start | bytes 1540
  1022.5 43.4 %copy-start.30 = (f32[128]{0:T(128)S(1)}, f32[128]{0:T(128)}, u32[]{:S(2)}) copy-start(f32[128]{0:T(128)} %copy-done.29) | copy-start | bytes 1540
  (25 other events, 100.3 us)
Sparse Core Ops, SparseCore 0:
  9.9 38.7 all-gather.16
  57.7 29.4 all-gather.18
  158.1 36.6 all-gather.10
  203.0 61.6 all-gather.12
  405.5 56.8 all-gather.14

commit v3 on v1

v3 whole, which is shorter than its diff:
```python
from functools import partial
from types import SimpleNamespace
from typing import Any, NamedTuple

import jax
import jax.numpy as jnp
from jax import lax
from jax.experimental import pallas as pl
from jax.experimental.pallas import tpu as pltpu
from jax.sharding import Mesh, PartitionSpec as P

NORM_EPSILON = 1e-05
ROPE_BASE = 1000000.0
MASKED_SCORE = -1e30
BF16 = jnp.bfloat16
F32 = jnp.float32
MESH = pl.DeviceIdType.MESH
MIB = 2**20


def dot(left, right):
    return jnp.dot(left, right, preferred_element_type=F32)


def contract_rows(left, right):
    return lax.dot_general(left, right, (((0,), (0,)), ((), ())), preferred_element_type=F32)


def contract_cols(left, right):
    return lax.dot_general(left, right, (((1,), (1,)), ((), ())), preferred_element_type=F32)


def places():
    dp, z, core = lax.axis_index("dp"), lax.axis_index("z"), lax.axis_index("core")
    return dp, z, core


def line_of(z, lines):
    left = z < lines // 2
    step = jnp.where(left, 1, -1)
    place = jnp.where(left, z, lines - 1 - z)
    inner = z + step
    outer = jnp.clip(z - step, 0, lines - 1)
    return place, inner, outer


class Line:
    def __init__(self, refs, dims):
        vars(self).update(vars(refs))
        vars(self).update(vars(dims))
        self.dp, self.z, self.core = places()
        self.place, self.inner, self.outer = line_of(self.z, self.lines)
        self.middle = self.lines // 2 - 1
        self.side = self.z // (self.lines // 2)
        self.other = 1 - self.core
        self.second = self.totals.at[self.core]
        self.quarter = self.rows // 4
        self.half = self.rows // 2
        self.lag = 5 + 2 * (self.middle - self.place)
        self.most = 5 + 2 * self.middle + 3
        self.n_ffn = self.n_blocks * self.per_block
        self.q_first = self.n_ffn + 2
        self.piece = self.qkv_cols // 3
        self.across = 512 // self.piece
        self.per_chunk = 2 * self.across
        self.position = 0

    def ours(self, k):
        return lax.rem(k // self.per_block + lax.rem(k, self.per_block), 2) == self.side

    def shift_of(self, k):
        part = lax.rem(k, self.per_block) - self.down_block
        return jnp.where(k < self.n_ffn, jnp.maximum(part, 0), 0)

    def send_inner(self, k, src):
        return pltpu.make_async_remote_copy(
            src, self.first.at[k], self.first_send.at[k], self.first_recv.at[k],
            device_id=(self.dp, self.inner, self.core), device_id_type=MESH)

    def send_across(self, k, src):
        return pltpu.make_async_remote_copy(
            src, self.cross.at[k], self.first_send.at[k], self.cross_recv.at[k],
            device_id=(self.dp, self.inner, self.core), device_id_type=MESH)

    def send_owner(self, k):
        total = self.total_slot.at[lax.rem(k, 4)]
        shift = self.shift_of(k)
        local = pltpu.make_async_copy(total, self.second.at[k], self.second_recv.at[k])
        remote = pltpu.make_async_remote_copy(
            total, self.second.at[k], self.owner_send.at[k], self.second_recv.at[k],
            device_id=(lax.rem(self.dp + shift, self.dp_n), self.z, self.core), device_id_type=MESH)
        return shift, local, remote

    def spread_across(self, k):
        return pltpu.make_async_remote_copy(
            self.second.at[k], self.second.at[k], self.across_send.at[k], self.second_recv.at[k],
            device_id=(self.dp, self.inner, self.core), device_id_type=MESH)

    def spread_outer(self, k):
        return pltpu.make_async_remote_copy(
            self.second.at[k], self.second.at[k], self.second_send.at[k], self.second_recv.at[k],
            device_id=(self.dp, self.outer, self.core), device_id_type=MESH)

    def load(self, src, dst, n):
        return pltpu.make_async_copy(src, dst, self.load_sem.at[n])

    def ready(self, k):
        @pl.when(k >= self.q_first)
        def _():
            for c in range(self.per_chunk):
                number = (k - self.q_first) * self.per_chunk + c
                spot = self.q_own(number)
                pltpu.make_async_copy(spot, spot, self.own_sem.at[number]).wait()

    def stage_one(self, k):
        self.ready(k)
        mine = self.sum_slot.at[lax.rem(k, 4)]

        @pl.when(self.place == 0)
        def _():
            @pl.when(k >= 2)
            def _():
                self.send_inner(k - 2, self.own.at[k - 2]).wait_send()

            self.send_inner(k, self.own.at[k]).start()

        @pl.when(self.place > 0)
        def _():
            self.load(self.own.at[k], mine, 0).start()
            self.send_inner(k, mine).wait_recv()
            self.load(self.first.at[k], self.in_slot, 1).start()
            self.load(self.own.at[k], mine, 0).wait()
            self.load(self.first.at[k], self.in_slot, 1).wait()
            add_chunk(mine, mine, self.in_slot)

            @pl.when(self.place < self.middle)
            def _():
                self.send_inner(k, mine).start()

            @pl.when((self.place == self.middle) & jnp.logical_not(self.ours(k)))
            def _():
                self.send_across(k, mine).start()

    def stage_sum(self, k):
        @pl.when((self.place == self.middle) & self.ours(k))
        def _():
            mine = self.sum_slot.at[lax.rem(k, 4)]
            self.send_across(k, mine).wait_recv()
            arrived = self.load(self.cross.at[k], self.in_slot, 2)
            arrived.start()
            arrived.wait()
            add_chunk(self.total_slot.at[lax.rem(k, 4)], mine, self.in_slot)
            shift, local, remote = self.send_owner(k)

            @pl.when(shift == 0)
            def _():
                local.start()

            @pl.when(shift > 0)
            def _():
                remote.start()

    def stage_sent(self, k):
        @pl.when((self.place > 0) & ((self.place < self.middle) | jnp.logical_not(self.ours(k))))
        def _():
            self.send_inner(k, self.own.at[k]).wait_send()

    def stage_handed(self, k):
        shift, _, remote = self.send_owner(k)

        @pl.when((self.place == self.middle) & self.ours(k) & (shift > 0))
        def _():
            remote.wait_send()

    def stage_two(self, k):
        self.spread_outer(k).wait_recv()

        @pl.when((self.place == self.middle) & self.ours(k))
        def _():
            self.spread_across(k).start()

        @pl.when(self.place > 0)
        def _():
            self.spread_outer(k).start()

        self.deliver(k).start()

    def stage_three(self, k):
        @pl.when((self.place == self.middle) & self.ours(k))
        def _():
            self.spread_across(k).wait_send()

        @pl.when(self.place > 0)
        def _():
            self.spread_outer(k).wait_send()

        @pl.when((self.place == 0) & (k >= self.chunks - 2))
        def _():
            self.send_inner(k, self.own.at[k]).wait_send()

        self.deliver(k).wait_send()

    def q_place(self, number):
        spot = lax.rem(number, self.per_chunk)
        column = lax.rem(spot, self.across) * self.piece
        if not isinstance(column, int):
            column = pl.multiple_of(column, 128)
        return number // self.per_chunk, pl.ds((spot // self.across) * self.half, self.half), pl.ds(column, self.piece)

    def q_own(self, number):
        chunk, where, columns = self.q_place(number)
        return self.own.at[self.q_first + chunk, where, columns]

    def deliver(self, k):
        return pltpu.make_async_remote_copy(
            self.second.at[k], self.second.at[k], self.core_send.at[k], self.core_recv.at[k],
            device_id=(self.dp, self.z, self.other), device_id_type=MESH)

    def advance(self, count):
        start = self.position
        self.position += count

        @pl.loop(start, start + count)
        def _(t):
            self.slot(t)

    def slot(self, t):
        @pl.when(t < self.chunks)
        def _():
            self.stage_one(t)

        def when(k, act, extra=True):
            @pl.when((k >= 0) & (k < self.chunks) & extra)
            def _():
                act(k)

        at_middle = self.place == self.middle
        when(t - 2, self.stage_sum)
        when(t - 3, self.stage_sent)
        when(t - 4, self.stage_handed)
        early = at_middle & self.ours(jnp.maximum(t - 3, 0))
        late = jnp.logical_not(at_middle & self.ours(jnp.maximum(t - self.lag, 0)))
        when(t - 3, self.stage_two, early)
        when(t - self.lag, self.stage_two, late)
        when(t - self.lag - 3, self.stage_three)

    def advance_at(self, first, count):
        for j in range(count):
            self.slot(first + j)

    def finish(self):
        self.advance(self.chunks + self.most - self.position)

        @pl.loop(0, self.chunks)
        def _(k):
            self.deliver(k).wait_recv()


def add_chunk(into, left, right):
    rows = into.shape[0]

    @pl.loop(0, rows // 64)
    def _(i):
        part = pl.ds(i * 64, 64)
        into[part] = (left[part].astype(F32) + right[part].astype(F32)).astype(BF16)


class BackIn(NamedTuple):
    normed_two: Any
    cot_all: Any
    w_first: Any
    w_gate: Any
    w_up: Any
    w_down: Any
    hidden_in: Any
    w_out: Any
    w_qkv: Any
    normed_one: Any
    qk_pre: Any
    query: Any
    keys_values: Any
    log_total: Any
    mixed: Any
    bias: Any
    tables: Any
    gains: Any
    own_x: Any


class BackOut(NamedTuple):
    output: Any
    input_grad: Any
    gain_sum: Any
    totals: Any
    own: Any
    first: Any
    cross: Any
    w_land: Any
    dn2_pair: Any
    out_pair: Any
    out_land: Any
    out_keep: Any
    pair_o: Any
    pair_q: Any


class BackScratch(NamedTuple):
    sum_slot: Any
    total_slot: Any
    in_slot: Any
    kv_sum: Any
    grad_query: Any
    grad_qkv: Any
    dn2_land: Any
    land_slot: Any
    hidden_v: Any
    grad_hidden: Any
    own_x_v: Any
    cot_own: Any
    gains_v: Any
    gain_acc: Any
    dx_all: Any
    kv_pair: Any
    kv_land: Any
    gain_core: Any
    gain_dp: Any
    gain_z: Any
    dn1_land: Any
    result: Any
    pair_slot: Any
    pair_q_slot: Any
    load_sem: Any
    own_sem: Any
    first_send: Any
    first_recv: Any
    second_send: Any
    cross_recv: Any
    owner_send: Any
    across_send: Any
    second_recv: Any
    core_send: Any
    core_recv: Any
    w_send: Any
    w_recv: Any
    stage_sem: Any
    in_sem: Any
    sum_send: Any
    pair_recv: Any
    land_recv: Any
    dx_send: Any
    dx_recv: Any
    kv_send: Any
    kv_recv: Any
    pair_send: Any
    pair_land: Any
    dn1_send: Any
    dn1_recv: Any
    q_send: Any
    gain_send: Any
    gain_recv: Any


def norm_rows(values):
    inverse = lax.rsqrt(jnp.mean(values * values, axis=-1, keepdims=True) + NORM_EPSILON)
    return values * inverse, inverse


def back_kernel(dims, *refs):
    r = SimpleNamespace()
    for kind, first in ((BackIn, 0), (BackOut, len(BackIn._fields)), (BackScratch, len(BackIn._fields + BackOut._fields))):
        vars(r).update(kind(*refs[first : first + len(kind._fields)])._asdict())
    dp_n, lines, tokens, width = dims.dp_n, dims.lines, dims.tokens, dims.width
    rows, f8, n_blocks, per_block, down_block = dims.rows, dims.f8, dims.n_blocks, dims.per_block, dims.down_block
    head, group, kv_heads = dims.head, dims.group, dims.kv_heads
    q_cols, kv_cols, cols = dims.q_cols, dims.kv_cols, dims.qkv_cols
    plane = 2 * dp_n * tokens
    seq_tokens = dp_n * tokens
    length = lines * 2 * tokens
    scale = head ** (-0.5)
    line = Line(r, dims)
    dp, z, core, other = line.dp, line.z, line.core, line.other
    own = r.own
    half, quarter = rows // 2, rows // 4
    partner = (dp, z, other)
    n_ffn = line.n_ffn
    pairs = range(1, dp_n)

    def peer(shift):
        return lax.rem(dp + shift, dp_n)

    def local(src, dst, sem, n=0):
        return pltpu.make_async_copy(src, dst, sem.at[n])

    def remote(src, dst, send, n, recv, m, device):
        return pltpu.make_async_remote_copy(
            src, dst, send.at[n], recv.at[m], device_id=device, device_id_type=MESH)

    def span(index, size):
        return pl.ds(pl.multiple_of(index * size, size), size)

    def start(copies):
        for copy in copies:
            copy.start()

    def wait(copies):
        for copy in copies:
            copy.wait()

    barrier = pltpu.get_barrier_semaphore()
    for shift in pairs:
        pl.semaphore_signal(barrier, device_id=(peer(shift), z, core), device_id_type=MESH)
    for shift in range(1, 2 * lines):
        spot = lax.rem(2 * z + core + shift, 2 * lines)
        pl.semaphore_signal(barrier, device_id=(dp, spot // 2, lax.rem(spot, 2)), device_id_type=MESH)

    w_land = r.w_land

    def weight_copies(b):
        mine, sent = [], []
        for c, weight in enumerate((r.w_gate, r.w_up)):
            for shift in range(dp_n):
                to = peer(shift)
                src = weight.at[:, pl.ds(pl.multiple_of((2 * to + core) * f8 + b * 256, 256), 256)]
                dst = w_land.at[b, span(dp, rows), pl.ds(c * 256, 256)]
                slot = (b * dp_n + dp) * 2 + c
                if shift == 0:
                    mine.append(local(src, dst, r.w_recv, slot))
                else:
                    sent.append(remote(src, dst, r.w_send, (b * dp_n + shift) * 2 + c, r.w_recv, slot, (to, z, core)))
        return mine, sent

    def feed_forward(act, grads, wd, w_gu, stage):
        def blocks(n2, dy):
            loads = [
                local(r.normed_two, n2, r.in_sem, 0), local(r.cot_all, dy, r.in_sem, 1),
                local(r.w_down.at[span(core, f8)], wd, r.in_sem, 2),
            ]
            start(loads)

            first_weights = local(r.w_first, w_gu.at[0], r.in_sem, 3)
            first_weights.start()

            @pl.loop(1, n_blocks)
            def _(b):
                start(weight_copies(b)[0])

            pl.semaphore_wait(barrier, dp_n - 1 + 2 * lines - 1)

            start(weight_copies(1)[1])
            wait(loads)
            first_weights.wait()

            @pl.loop(0, n_blocks)
            def _(b):
                @pl.when(b > 0)
                def _():
                    @pl.loop(0, dp_n)
                    def _(src):
                        for c in range(2):
                            dst = w_land.at[b, pl.ds(0, rows), pl.ds(c * 256, 256)]
                            local(dst, dst, r.w_recv, (b * dp_n + src) * 2 + c).wait()

                    weights = local(w_land.at[b], w_gu.at[b], r.in_sem, 3)
                    weights.start()

                    @pl.when(b + 1 < n_blocks)
                    def _():
                        start(weight_copies(b + 1)[1])

                    weights.wait()

                @pl.loop(0, plane // 256)
                def _(i):
                    where = span(i, 256)
                    both = dot(n2[where], w_gu[b])
                    gate, up = both[:, :256], both[:, 256:]
                    grad_act = contract_cols(dy[where], wd[span(b, 256)])
                    sig = jax.nn.sigmoid(gate)
                    silu = gate * sig
                    act[b, where] = (silu * up).astype(BF16)
                    grads[b, where, 0:256] = (grad_act * up * sig * (1.0 + gate * (1.0 - sig))).astype(BF16)
                    grads[b, where, 256:512] = (grad_act * silu).astype(BF16)

                def to_own(j):
                    return local(stage.at[j], own.at[b * per_block + j], r.stage_sem, j)

                @pl.loop(0, 4)
                def _(c):
                    grad = contract_rows(act[b], dy[:, span(c, 512)]).astype(BF16)
                    for j in range(down_block):
                        stage[j, span(c, quarter), :] = grad[j * quarter : (j + 1) * quarter]

                for j in range(down_block):
                    to_own(j).start()

                @pl.loop(0, dp_n)
                def _(shift):
                    stage[down_block + shift] = contract_rows(n2[:, span(peer(shift), rows)], grads[b]).astype(BF16)
                    to_own(down_block + shift).start()

                @pl.loop(0, per_block)
                def _(j):
                    to_own(j).wait()


                line.advance_at(b * 2, 2)

        pl.run_scoped(blocks, pltpu.VMEM((plane, width), BF16), pltpu.VMEM((plane, width), BF16))
        line.position = n_blocks * 2

        def sums(part):
            def to_partner(hidden):
                base = 0 if hidden else dp_n
                return [
                    remote(part.at[i, span(other, tokens)], (r.dn2_pair if hidden else r.out_pair).at[i], r.sum_send, base + i, r.pair_recv, base + i, partner)
                    for i in range(dp_n)
                ]

            def plane_sum(hidden, product):
                @pl.loop(0, dp_n)
                def _(i):
                    @pl.loop(0, width // 512)
                    def _(n):
                        part[i, :, span(n, 512)] = product(span(i, 2 * tokens), span(n, 512)).astype(BF16)

                to_pair = to_partner(hidden)
                start(to_pair)
                for i in range(dp_n):
                    to_pair[i].wait_recv()
                    copy = local((r.dn2_pair if hidden else r.out_pair).at[i], r.land_slot, r.in_sem, 3)
                    copy.start()
                    copy.wait()
                    mine = part.at[i, span(core, tokens)]
                    add_rows(mine, mine, r.land_slot)

            def own_sums():
                return [
                    remote(part.at[peer(shift), span(core, tokens)], r.dn2_land.at[dp], r.sum_send, 2 * dp_n + shift,
                           r.land_recv, dp, (peer(shift), z, core))
                    for shift in pairs
                ]

            def hidden_grad(where, columns):
                total = contract_cols(grads[0, where], w_gu[0, columns])
                for b in range(1, n_blocks):
                    total += contract_cols(grads[b, where], w_gu[b, columns])
                return total

            def ffn_out(where, columns):
                total = dot(act[0, where], wd[pl.ds(0, 256), columns])
                for b in range(1, n_blocks):
                    total += dot(act[b, where], wd[pl.ds(b * 256, 256), columns])
                return total

            plane_sum(True, hidden_grad)
            mine = local(part.at[dp, span(core, tokens)], r.dn2_land.at[dp], r.in_sem, 4)
            start(own_sums() + [mine])
            line.advance(2)
            mine.wait()
            for copy in own_sums() + to_partner(True):
                copy.wait_send()
            plane_sum(False, ffn_out)
            keep = [local(part.at[i, span(core, tokens)], r.out_keep.at[i], r.in_sem, 8 + i) for i in range(dp_n)]
            start(keep)
            line.advance(1)
            wait(keep)
            for copy in to_partner(False):
                copy.wait_send()

        pl.run_scoped(sums, pltpu.VMEM((dp_n, 2 * tokens, width), BF16))

    pl.run_scoped(
        feed_forward,
        pltpu.VMEM((n_blocks, plane, 256), BF16), pltpu.VMEM((n_blocks, plane, 512), BF16), pltpu.VMEM((f8, width), BF16),
        pltpu.VMEM((n_blocks, width, 512), BF16), pltpu.VMEM((per_block, rows, 512), BF16),
    )

    def landed(land, base):
        for shift in pairs:
            src = peer(shift)
            local(land.at[src], land.at[src], r.land_recv, base + src).wait()

    hidden_in, grad_hidden, gains = r.hidden_v, r.grad_hidden, r.gains_v
    own_loads = [
        local(r.cot_all.at[span(2 * dp + core, tokens)], r.cot_own, r.in_sem, 4), local(r.hidden_in, hidden_in, r.in_sem, 5), local(r.gains, gains, r.in_sem, 6), local(r.own_x, r.own_x_v, r.in_sem, 7),
    ]
    start(own_loads)
    wait(own_loads)
    landed(r.dn2_land, 0)
    gain_acc = r.gain_acc
    gain_acc[...] = jnp.zeros_like(gain_acc)

    @pl.loop(0, tokens // 32)
    def _(i):
        where = span(i, 32)
        grad = r.dn2_land[0, where].astype(F32)
        for src in range(1, dp_n):
            grad += r.dn2_land[src, where].astype(F32)
        hat, inverse = norm_rows(hidden_in[where])
        gain_acc[1:2] += jnp.sum(grad * hat, axis=0, keepdims=True)
        back = grad * gains[1:2]
        dy_own = r.cot_own
        total = dy_own[where].astype(F32) + inverse * (back - hat * jnp.mean(back * hat, axis=-1, keepdims=True))
        grad_hidden[where] = total
        r.dx_all[dp, where] = total.astype(BF16)

    dx_sends = []
    for shift in pairs:
        to = peer(shift)
        dx_sends.append(remote(r.dx_all.at[dp], r.dx_all.at[dp], r.dx_send, shift, r.dx_recv, dp, (to, z, core)))
    start(dx_sends)
    line.advance(2)

    kv_sum, grad_query, grad_qkv = r.kv_sum, r.grad_query, r.grad_qkv
    step = max(1, min(group, MIB // (4 * length * tokens)))

    def kv_copies(s):
        found = []
        for shift in range(1, lines):
            to = lax.rem(z + shift, lines)
            found.append(remote(kv_sum.at[s, to], r.kv_land.at[z, s], r.kv_send, dp_n + s * lines + shift,
                                r.kv_recv, dp_n + s * lines + z, (dp, to, core)))
        return found

    def sequences(w_out, query, keys_values, bias, grad_mixed, grad_kv):
        loads = [
            local(src, dst, r.in_sem, 8 + n)
            for n, (src, dst) in enumerate(((r.w_out, w_out), (r.query, query), (r.keys_values, keys_values), (r.bias, bias)))
        ]
        start(loads)
        wait(loads)

        def pair_copy(s):
            return remote(grad_kv.at[s, :, other], r.kv_pair.at[s], r.kv_send, s, r.kv_recv, s, partner)

        def one_sequence(turn):
            s = peer(turn)

            @pl.when(turn > 0)
            def _():
                local(r.dx_all.at[s], r.dx_all.at[s], r.dx_recv, s).wait()

            grad_mixed[...] = contract_cols(r.dx_all[s], w_out[...]).astype(BF16)
            both = keys_values[:, s].reshape(length, 2 * kv_cols)
            grads = [None] * (2 * kv_heads)
            mask = jnp.concatenate([bias[...]] * step, axis=1)
            for g in range(kv_heads):
                keys = both[:, g * head : (g + 1) * head]
                values = both[:, (kv_heads + g) * head : (kv_heads + g + 1) * head]
                key_grad = value_grad = None
                for first in range(g * group, (g + 1) * group, step):
                    names = [slice(h * head, (h + 1) * head) for h in range(first, first + step)]
                    queries = jnp.concatenate([query[s, :, n] for n in names], axis=0)
                    grad_out = jnp.concatenate([grad_mixed[:, n] for n in names], axis=0)
                    scores = contract_cols(keys, queries) * scale + mask
                    offset = (first - g * group) * tokens
                    probs = jnp.exp(scores - r.log_total[s, pl.ds(g, 1), offset : offset + step * tokens])
                    grad_probs = contract_cols(values, grad_out)
                    inner = jnp.sum(probs * grad_probs, axis=0, keepdims=True)
                    grad_scores = (probs * (grad_probs - inner)).astype(BF16)
                    key_part = dot(grad_scores, queries)
                    value_part = dot(probs.astype(BF16), grad_out)
                    key_grad = key_part if key_grad is None else key_grad + key_part
                    value_grad = value_part if value_grad is None else value_grad + value_part
                    back = (contract_rows(keys, grad_scores) * scale).T.astype(BF16)
                    grad_query[s, :, first * head : (first + step) * head] = jnp.concatenate(
                        [back[h * tokens : (h + 1) * tokens] for h in range(step)], axis=1)
                grads[g] = key_grad * scale
                grads[kv_heads + g] = value_grad
            grad_kv[s] = jnp.concatenate(grads, axis=1).astype(BF16).reshape(lines, 2, tokens, 2 * kv_cols)
            pair_copy(s).start()

        def pass_on(turn):
            s = peer(turn)
            pair_copy(s).wait_recv()

            @pl.loop(0, lines)
            def _(n):
                kv_sum[s, n] = (grad_kv[s, n, core].astype(F32) + r.kv_pair[s, n].astype(F32)).astype(BF16)

            start(kv_copies(s))

        @pl.loop(0, dp_n)
        def _(turn):
            one_sequence(turn)

            @pl.when(turn > 0)
            def _():
                pass_on(turn - 1)

            line.advance_at(line.position + turn * dims.pace, dims.pace)

        pass_on(dp_n - 1)

        @pl.loop(0, dp_n)
        def _(s):
            pair_copy(s).wait_send()

    seqs = lambda *shape: pltpu.VMEM((dp_n,) + shape, BF16)
    pl.run_scoped(
        sequences,
        pltpu.VMEM((rows, width), BF16), seqs(tokens, q_cols), pltpu.VMEM((2 * lines, dp_n, tokens, 2 * kv_cols), BF16),
        pltpu.VMEM((length, tokens), F32), pltpu.VMEM((tokens, q_cols), BF16), seqs(lines, 2, tokens, 2 * kv_cols),
    )
    line.position += dp_n * dims.pace
    assert line.position <= n_ffn

    def projections(w_qkv, normed_one, qk_pre, mixed, tables, out_part, qkv_part, dn1_part):
        loads = [
            local(src, dst, r.in_sem, 8 + n)
            for n, (src, dst) in enumerate((
                (r.qk_pre, qk_pre), (r.tables, tables), (r.mixed, mixed), (r.normed_one, normed_one), (r.w_qkv, w_qkv)))
        ]
        start(loads)
        wait(loads)

        @pl.loop(0, width // 512)
        def _(n):
            total = jnp.zeros((rows, 512), F32)
            for s in range(dp_n):
                total += contract_rows(mixed[s], r.dx_all[s, :, span(n, 512)])
            out_part[:, span(n, 512)] = total.astype(BF16)

        pair_o = remote(out_part.at[span(other, half)], r.pair_o, r.pair_send, 0, r.pair_land, 0, partner)
        pair_o.start()
        line.advance(1)

        q_gain, k_gain = gains[2:3, 0:head], gains[3:4, 0:head]
        zero = jnp.zeros((1, head), F32)

        def rotate(turn, carry):
            s = peer(turn)
            for shift in range(1, lines):
                src = lax.rem(z + shift, lines)
                land = r.kv_land.at[src, s]
                local(land, land, r.kv_recv, dp_n + s * lines + src).wait()
            kv = kv_sum[s, z].astype(F32)
            for shift in range(1, lines):
                kv += r.kv_land[lax.rem(z + shift, lines), s].astype(F32)
            kv = kv.astype(BF16)
            cosine, sine = tables[s, :, 0:head], tables[s, :, head : 2 * head]
            sums = list(carry)
            outs = []
            for h in range(kv_heads * (group + 1)):
                is_key = h >= kv_heads * group
                if is_key:
                    g = h - kv_heads * group
                    grad = kv[:, g * head : (g + 1) * head].astype(F32)
                else:
                    grad = grad_query[s, :, h * head : (h + 1) * head].astype(F32)
                turned = jnp.concatenate([grad[:, head // 2 :], grad[:, : head // 2]], axis=1)
                grad = grad * cosine - turned * sine
                hat, inverse = norm_rows(qk_pre[s, :, h * head : (h + 1) * head])
                sums[is_key] = sums[is_key] + jnp.sum(grad * hat, axis=0, keepdims=True)
                back = grad * (k_gain if is_key else q_gain)
                outs.append((inverse * (back - hat * jnp.mean(back * hat, axis=-1, keepdims=True))).astype(BF16))
            grad_qkv[s] = jnp.concatenate(outs + [kv[:, kv_cols:]], axis=1)
            return tuple(sums)

        q_sum, k_sum = lax.fori_loop(0, dp_n, rotate, (zero, zero))
        gain_acc[2:3, 0:head] = q_sum
        gain_acc[3:4, 0:head] = k_sum
        line.advance(1)

        @pl.loop(0, width // 512)
        def _(n):
            weights = w_qkv[span(n, 512)]
            for s in range(dp_n):
                dn1_part[s, :, span(n, 512)] = contract_cols(grad_qkv[s], weights).astype(BF16)

        dn1_sends = []
        for shift in pairs:
            to = peer(shift)
            dn1_sends.append(remote(dn1_part.at[to], r.dn1_land.at[dp], r.dn1_send, shift, r.dn1_recv, dp, (to, z, core)))
        start(dn1_sends)
        r.dn1_land[dp] = dn1_part[dp]

        @pl.loop(0, dp_n)
        def _(i):
            total = jnp.zeros((rows, cols), F32)
            for s in range(dp_n):
                total += contract_rows(normed_one[s, :, span(i, rows)], grad_qkv[s])
            qkv_part[i] = total.astype(BF16)

        pair_q = [
            remote(qkv_part.at[i, span(other, half)], r.pair_q.at[i], r.pair_send, 1 + i, r.pair_land, 1 + i, partner)
            for i in range(dp_n)
        ]
        start(pair_q)

        line.advance(1)

        slot = r.pair_slot
        pair_o.wait_recv()
        for j in range(2):
            for c in range(4):
                copy = local(r.pair_o.at[pl.ds(j * quarter, quarter), pl.ds(c * 512, 512)], slot.at[span(c, quarter), pl.ds(0, 512)], r.stage_sem, c)
                copy.start()
                copy.wait()
                mine = out_part[pl.ds(pl.multiple_of(core * half + j * quarter, quarter), quarter), pl.ds(c * 512, 512)]
                where = pl.ds(c * quarter, quarter)
                slot[where, 0:512] = (mine.astype(F32) + slot[where, 0:512].astype(F32)).astype(BF16)
            copy = local(slot.at[pl.ds(0, rows), pl.ds(0, 512)], own.at[n_ffn + j], r.stage_sem, 0)
            copy.start()
            copy.wait()
        piece = line.piece
        q_sends = []
        q_mine = []
        for i in range(dp_n):
            pair_q[i].wait_recv()
            copy = local(r.pair_q.at[i], r.pair_q_slot, r.stage_sem, 0)
            copy.start()
            copy.wait()
            mine = qkv_part.at[i, span(core, half)]
            mine[...] = (mine[...].astype(F32) + r.pair_q_slot[...].astype(F32)).astype(BF16)
        for shift in range(dp_n):
            to = peer(shift)
            for j in range(3):
                number = dp * 3 + j
                src = qkv_part.at[to, span(core, half), pl.ds(j * piece, piece)]
                if shift == 0:
                    q_mine.append(local(src, line.q_own(number), r.own_sem, number))
                else:
                    q_sends.append(remote(src, line.q_own(number), r.q_send, shift * 3 + j, r.own_sem, number, (to, z, core)))
        start(q_sends + q_mine)

        out_sends = [
            remote(r.out_keep.at[peer(shift)], r.out_land.at[dp], r.sum_send, 3 * dp_n + shift, r.land_recv, dp_n + dp, (peer(shift), z, core))
            for shift in pairs
        ]
        out_mine = local(r.out_keep.at[dp], r.out_land.at[dp], r.in_sem, 4)
        start(out_sends + [out_mine])
        line.advance(2)

        for shift in pairs:
            src = peer(shift)
            local(r.dn1_land.at[src], r.dn1_land.at[src], r.dn1_recv, src).wait()

        @pl.loop(0, tokens // 32)
        def _(i):
            where = span(i, 32)
            grad = r.dn1_land[0, where].astype(F32)
            for src in range(1, dp_n):
                grad += r.dn1_land[src, where].astype(F32)
            hat, inverse = norm_rows(r.own_x_v[where].astype(F32))
            gain_acc[0:1] += jnp.sum(grad * hat, axis=0, keepdims=True)
            back = grad * gains[0:1]
            total = grad_hidden[where] + inverse * (back - hat * jnp.mean(back * hat, axis=-1, keepdims=True))
            r.result[where] = total.astype(BF16)

        written = local(r.result, r.input_grad, r.in_sem, 0)
        written.start()
        written.wait()

        def gain_total(land, count, me):
            land[me] = gain_acc[...]
            total = land[0]
            for n in range(1, count):
                total = total + land[n]
            return total

        sends = [remote(gain_acc, r.gain_core.at[core], r.gain_send, 0, r.gain_recv, 0, partner)]
        start(sends)
        line.advance(1)
        wait(sends)
        gain_acc[...] = gain_total(r.gain_core, 2, core)
        sends = [
            remote(gain_acc, r.gain_dp.at[dp], r.gain_send, shift, r.gain_recv, shift, (peer(shift), z, core)) for shift in pairs
        ]
        start(sends)
        line.advance(1)
        wait(sends)
        gain_acc[...] = gain_total(r.gain_dp, dp_n, dp)
        sends = [
            remote(gain_acc, r.gain_z.at[z], r.gain_send, dp_n + shift, r.gain_recv, dp_n + shift,
                   (dp, lax.rem(z + shift, lines), core))
            for shift in range(1, lines)
        ]
        start(sends)
        line.advance(1)
        wait(sends)
        gain_acc[...] = gain_total(r.gain_z, lines, z)
        written = local(gain_acc, r.gain_sum, r.in_sem, 1)
        written.start()
        written.wait()

        landed(r.out_land, dp_n)
        wait([out_mine])

        @pl.loop(0, dp_n)
        def _(src):
            copy = local(r.out_land.at[src], r.land_slot, r.in_sem, 3)
            copy.start()
            copy.wait()

            @pl.loop(0, tokens // 32)
            def _(i):
                where = span(i, 32)
                hidden_in[where] += r.land_slot[where].astype(F32)

        r.result[...] = hidden_in[...].astype(BF16)
        done = local(r.result, r.output, r.in_sem, 0)
        done.start()
        done.wait()
        line.finish()

        for copy in out_sends + q_sends + dn1_sends + pair_q + [pair_o]:
            copy.wait_send()

        @pl.loop(0, dp_n)
        def _(s):
            for copy in kv_copies(s):
                copy.wait_send()

    pl.run_scoped(
        projections,
        pltpu.VMEM((width, cols), BF16), seqs(tokens, width), pltpu.VMEM((dp_n, tokens, q_cols + kv_cols), F32), seqs(tokens, q_cols),
        pltpu.VMEM((dp_n, tokens, 2 * head), F32), pltpu.VMEM((rows, width), BF16), seqs(rows, cols), seqs(tokens, width),
    )

    for copy in dx_sends:
        copy.wait_send()

    @pl.loop(1, n_blocks)
    def _(b):
        for copy in weight_copies(b)[1]:
            copy.wait_send()


def add_rows(into, left, right):
    @pl.loop(0, into.shape[0] // 32)
    def _(i):
        where = pl.ds(pl.multiple_of(i * 32, 32), 32)
        into[where] = (left[where].astype(F32) + right[where].astype(F32)).astype(BF16)


def backward(arrays, dp_n, lines, head, collective_id):
    x = arrays
    tokens, width = x.own_x.shape
    rows = width // dp_n
    f8 = x.w_down.shape[0] // 2
    n_blocks = f8 // 256
    down_block = 1024 // rows
    q_cols = x.query.shape[2]
    cols = x.w_qkv.shape[1]
    kv_cols = (cols - q_cols) // 2
    kv_heads = kv_cols // head
    per_block = down_block + dp_n
    chunks = n_blocks * per_block + 2 + dp_n * cols // 1024
    plane = 2 * dp_n * tokens
    dims = SimpleNamespace(
        dp_n=dp_n, lines=lines, tokens=tokens, width=width, rows=rows, f8=f8, n_blocks=n_blocks, per_block=per_block,
        down_block=down_block, head=head, group=q_cols // kv_cols, kv_heads=kv_heads, q_cols=q_cols, kv_cols=kv_cols,
        qkv_cols=cols, chunks=chunks, pace=1,
    )
    bf16 = lambda *shape: jax.ShapeDtypeStruct(shape, BF16)
    outs = BackOut(
        output=bf16(tokens, width), input_grad=bf16(tokens, width), gain_sum=jax.ShapeDtypeStruct((8, width), F32),
        totals=bf16(2, chunks, rows, 512), own=bf16(chunks, rows, 512), first=bf16(chunks, rows, 512),
        cross=bf16(chunks, rows, 512), w_land=bf16(n_blocks, width, 512), dn2_pair=bf16(dp_n, tokens, width), out_pair=bf16(dp_n, tokens, width), out_land=bf16(dp_n, tokens, width), out_keep=bf16(dp_n, tokens, width),
        pair_o=bf16(rows // 2, width), pair_q=bf16(dp_n, rows // 2, cols),
    )
    vmem = lambda *shape: pltpu.VMEM(shape, BF16)
    dma = lambda n: pltpu.SemaphoreType.DMA((n,))
    scratch = BackScratch(
        sum_slot=vmem(4, rows, 512), total_slot=vmem(4, rows, 512), in_slot=vmem(rows, 512),
        kv_sum=vmem(dp_n, lines, tokens, 2 * kv_cols), grad_query=vmem(dp_n, tokens, q_cols), grad_qkv=vmem(dp_n, tokens, cols),
        dn2_land=vmem(dp_n, tokens, width),
        land_slot=vmem(tokens, width), hidden_v=pltpu.VMEM((tokens, width), F32), grad_hidden=pltpu.VMEM((tokens, width), F32),
        own_x_v=vmem(tokens, width), cot_own=vmem(tokens, width), gains_v=pltpu.VMEM((8, width), F32), gain_acc=pltpu.VMEM((8, width), F32),
        dx_all=vmem(dp_n, tokens, width), kv_pair=vmem(dp_n, lines, tokens, 2 * kv_cols), kv_land=vmem(lines, dp_n, tokens, 2 * kv_cols),
        gain_core=pltpu.VMEM((2, 8, width), F32), gain_dp=pltpu.VMEM((dp_n, 8, width), F32), gain_z=pltpu.VMEM((lines, 8, width), F32),
        dn1_land=vmem(dp_n, tokens, width), result=vmem(tokens, width), pair_slot=vmem(rows, 512), pair_q_slot=vmem(rows // 2, cols),
        load_sem=dma(3), own_sem=dma(3 * dp_n), first_send=dma(chunks), first_recv=dma(chunks),
        second_send=dma(chunks), cross_recv=dma(chunks), owner_send=dma(chunks), across_send=dma(chunks), second_recv=dma(chunks), core_send=dma(chunks), core_recv=dma(chunks),
        w_send=dma(2 * n_blocks * dp_n), w_recv=dma(2 * n_blocks * dp_n), stage_sem=dma(per_block),
        in_sem=dma(8 + max(8, dp_n)), sum_send=dma(4 * dp_n), pair_recv=dma(2 * dp_n), land_recv=dma(2 * dp_n), dx_send=dma(dp_n), dx_recv=dma(dp_n),
        kv_send=dma(dp_n + dp_n * lines), kv_recv=dma(dp_n + dp_n * lines), pair_send=dma(1 + dp_n), pair_land=dma(1 + dp_n),
        dn1_send=dma(dp_n), dn1_recv=dma(dp_n), q_send=dma(3 * dp_n), gain_send=dma(dp_n + lines), gain_recv=dma(dp_n + lines),
    )
    hbm = pl.BlockSpec(memory_space=pl.ANY)
    in_vmem = pl.BlockSpec(memory_space=pltpu.VMEM)
    flops = 6 * plane * width * f8 * 3
    results = pl.pallas_call(
        partial(back_kernel, dims),
        out_shape=tuple(outs),
        in_specs=list(BackIn(*[hbm] * len(x))._replace(log_total=in_vmem)),
        out_specs=(hbm,) * len(outs),
        scratch_shapes=list(scratch),
        compiler_params=pltpu.CompilerParams(collective_id=collective_id, has_side_effects=True, vmem_limit_bytes=63 * MIB),
        cost_estimate=pl.CostEstimate(flops=flops, bytes_accessed=100 * MIB, transcendentals=0),
        name="backward",
    )(*x)
    return BackOut(*results)


def widen_piece_kernel(place, totals, out):
    out[...] = totals[0, 0].astype(F32)


def widen_halves_kernel(place, totals, left, right):
    middle = left.shape[1]
    left[...] = totals[0, 0, :, :middle].astype(F32)
    right[...] = totals[0, 0, :, middle:].astype(F32)


def widen_pair_kernel(place, totals, gate, up):
    gate[...] = totals[0, 0, :, 0:256].astype(F32)
    up[...] = totals[0, 0, :, 256:512].astype(F32)


def widen_rows_kernel(place, totals, out):
    quarter = out.shape[0]
    for c in range(4):
        out[:, c * 512 : (c + 1) * 512] = totals[0, 0, c * quarter : (c + 1) * quarter, :].astype(F32)


def widen(totals, place, dp_n, width, f8, cols, q_cols, kv_cols):
    _, chunks, rows, _ = totals.shape
    quarter, half = rows // 4, rows // 2
    down_block = 256 // quarter
    per_block = down_block + dp_n
    n_blocks = f8 // 256
    n_ffn = n_blocks * per_block
    f32 = lambda *shape: jax.ShapeDtypeStruct(shape, F32)
    params = pltpu.CompilerParams(vmem_limit_bytes=40 * MIB)

    def call(kernel, grid, in_map, out_specs, out_shape, name):
        return pl.pallas_call(
            kernel,
            grid_spec=pltpu.PrefetchScalarGridSpec(
                num_scalar_prefetch=1, grid=grid, in_specs=[pl.BlockSpec((1, 1, rows, 512), in_map)], out_specs=out_specs),
            out_shape=out_shape, compiler_params=params, name=name,
        )(place, totals)

    columns = lambda src, who, b, place: (0, (2 * src + who) * n_blocks + b)
    gate, up = call(
        widen_pair_kernel, (dp_n, 2, n_blocks),
        lambda src, who, b, place: (who, b * per_block + down_block + lax.rem(place[0] - src + dp_n, dp_n), 0, 0),
        (pl.BlockSpec((rows, 256), columns),) * 2, (f32(rows, 2 * dp_n * f8),) * 2, "widen_gate_up")
    down = call(
        widen_rows_kernel, (2, n_blocks, down_block),
        lambda who, b, j, place: (who, b * per_block + j, 0, 0),
        pl.BlockSpec((quarter, width), lambda who, b, j, place: ((who * n_blocks + b) * down_block + j, 0)),
        f32(2 * f8, width), "widen_down")
    out = call(
        widen_rows_kernel, (2, 2), lambda who, j, place: (who, n_ffn + j, 0, 0),
        pl.BlockSpec((quarter, width), lambda who, j, place: (2 * who + j, 0)), f32(rows, width), "widen_out")
    piece = cols // 3
    across = 512 // piece
    per_chunk = 2 * across

    def piece_map(number, who):
        spot = lax.rem(number, per_chunk)
        return (who, n_ffn + 2 + number // per_chunk, spot // across, lax.rem(spot, across))

    def pieces(kernel, grid, in_map, out_specs, out_shape, name):
        return pl.pallas_call(
            kernel,
            grid_spec=pltpu.PrefetchScalarGridSpec(
                num_scalar_prefetch=1, grid=grid, in_specs=[pl.BlockSpec((1, 1, half, piece), in_map)], out_specs=out_specs),
            out_shape=out_shape, compiler_params=params, name=name,
        )(place, totals)

    query = pieces(
        widen_piece_kernel, (dp_n, 2, 2), lambda src, who, j, place: piece_map(3 * src + j, who),
        pl.BlockSpec((half, piece), lambda src, who, j, place: (who, 2 * src + j)), f32(rows, dp_n * q_cols), "widen_query")
    kv_in = lambda src, who, place: piece_map(3 * src + 2, who)
    if kv_cols % 128 == 0:
        key, value = pieces(
            widen_halves_kernel, (dp_n, 2), kv_in, (pl.BlockSpec((half, kv_cols), lambda src, who, place: (who, src)),) * 2,
            (f32(rows, dp_n * kv_cols),) * 2, "widen_key_value")
    else:
        both = pieces(
            widen_piece_kernel, (dp_n, 2), kv_in, pl.BlockSpec((half, piece), lambda src, who, place: (who, src)),
            f32(rows, dp_n * piece), "widen_key_value").reshape(rows, dp_n, 2, kv_cols)
        key, value = (both[:, :, n].reshape(rows, dp_n * kv_cols) for n in range(2))
    return query, key, value, out, gate, up, down


class FrontIn(NamedTuple):
    own_x: Any
    own_cot: Any
    w_query: Any
    w_pair: Any
    gain_piece: Any
    own_tables: Any
    bias: Any
    w_out: Any
    w_gate: Any
    w_up: Any


class FrontOut(NamedTuple):
    normed_two: Any
    cot_all: Any
    w_first: Any
    hidden_in: Any
    w_qkv: Any
    normed_one: Any
    qk_pre: Any
    query: Any
    keys_values: Any
    log_total: Any
    mixed: Any
    tables: Any
    gains: Any


class FrontScratch(NamedTuple):
    x_all: Any
    n1: Any
    w_all: Any
    qk: Any
    value: Any
    q_rot: Any
    kv: Any
    log_v: Any
    mix: Any
    tables_v: Any
    gains_v: Any
    bias_v: Any
    w_out_v: Any
    part: Any
    land: Any
    hidden: Any
    n2: Any
    in_sem: Any
    out_sem: Any
    x_send: Any
    x_recv: Any
    w_send: Any
    w_recv: Any
    w_pass: Any
    w_passed: Any
    kv_send: Any
    kv_recv: Any
    kv_pass: Any
    kv_passed: Any
    part_send: Any
    part_recv: Any
    plane_send: Any
    plane_recv: Any
    plane_pass: Any
    plane_passed: Any
    first_send: Any
    first_recv: Any


def front_kernel(dims, *refs):
    r = SimpleNamespace()
    for kind, first in ((FrontIn, 0), (FrontOut, len(FrontIn._fields)), (FrontScratch, len(FrontIn._fields + FrontOut._fields))):
        vars(r).update(kind(*refs[first : first + len(kind._fields)])._asdict())
    dp_n, lines, tokens, width, rows, f8 = dims.dp_n, dims.lines, dims.tokens, dims.width, dims.rows, dims.f8
    head, group, kv_heads, q_cols, kv_cols = dims.head, dims.group, dims.kv_heads, dims.q_cols, dims.kv_cols
    length = 2 * lines * tokens
    half = rows // 2
    scale = head ** (-0.5)
    dp, z, core = places()
    other = 1 - core
    partner = (dp, z, other)
    pairs = range(1, dp_n)
    me = 2 * z + core

    def peer(shift):
        return lax.rem(dp + shift, dp_n)

    def local(src, dst, sem, n=0):
        return pltpu.make_async_copy(src, dst, sem.at[n])

    def remote(src, dst, send, n, recv, m, device):
        return pltpu.make_async_remote_copy(
            src, dst, send.at[n], recv.at[m], device_id=device, device_id_type=MESH)

    def span(index, size):
        return pl.ds(pl.multiple_of(index * size, size), size)

    def start(copies):
        for copy in copies:
            copy.start()

    def wait(copies):
        for copy in copies:
            copy.wait()

    def landed(ref, sem, n):
        local(ref, ref, sem, n).wait()

    barrier = pltpu.get_barrier_semaphore()
    for shift in pairs:
        pl.semaphore_signal(barrier, device_id=(peer(shift), z, core), device_id_type=MESH)
    pl.semaphore_signal(barrier, device_id=partner, device_id_type=MESH)
    for shift in range(1, lines):
        pl.semaphore_signal(barrier, device_id=(dp, lax.rem(z + shift, lines), core), device_id_type=MESH)

    mine = [
        local(r.own_x, r.x_all.at[dp], r.in_sem, 0), local(r.own_tables, r.tables_v.at[dp], r.in_sem, 1),
        local(r.gain_piece, r.gains_v.at[:, span(dp, rows)], r.in_sem, 2), local(r.bias, r.bias_v, r.in_sem, 3),
        local(r.w_out, r.w_out_v, r.in_sem, 4),
        local(r.w_query.at[:, span(dp, q_cols)], r.w_all.at[span(dp, rows), pl.ds(0, q_cols)], r.in_sem, 5),
        local(r.w_pair.at[dp], r.w_all.at[span(dp, rows), pl.ds(q_cols, 2 * kv_cols)], r.in_sem, 6),
    ]
    start(mine)
    pl.semaphore_wait(barrier, dp_n + lines - 1)

    small = []
    for shift in pairs:
        to = peer(shift)
        device = (to, z, core)
        small += [
            remote(r.own_x, r.x_all.at[dp], r.x_send, 3 * shift, r.x_recv, 3 * dp, device),
            remote(r.own_tables, r.tables_v.at[dp], r.x_send, 3 * shift + 1, r.x_recv, 3 * dp + 1, device),
            remote(r.gain_piece, r.gains_v.at[:, span(dp, rows)], r.x_send, 3 * shift + 2, r.x_recv, 3 * dp + 2, device),
        ]
    start(small)

    def weight_spot(src, side):
        where = pl.ds(pl.multiple_of(src * rows + side * half, half), half)
        return r.w_all.at[where, pl.ds(0, q_cols)], r.w_all.at[where, pl.ds(q_cols, 2 * kv_cols)]

    weights = []
    for shift in pairs:
        to = peer(shift)
        spots = weight_spot(dp, core)
        where = span(core, half)
        for n, src in enumerate((r.w_query.at[where, span(to, q_cols)], r.w_pair.at[to, where])):
            weights.append(remote(src, spots[n], r.w_send, 2 * shift + n, r.w_recv, 2 * dp + n, (to, z, core)))
    start(weights)

    wait(mine[1:3])
    for shift in pairs:
        landed(r.gains_v.at[:, span(peer(shift), rows)], r.x_recv, 3 * peer(shift) + 2)
    mine[0].wait()

    @pl.loop(0, dp_n)
    def _(turn):
        s = peer(turn)

        @pl.when(turn > 0)
        def _():
            landed(r.x_all.at[s], r.x_recv, 3 * s)

        @pl.loop(0, tokens // 32)
        def _(i):
            hat, _ = norm_rows(r.x_all[s, span(i, 32)].astype(F32))
            r.n1[pl.ds(pl.multiple_of(s * tokens + i * 32, 32), 32)] = (hat * r.gains_v[0:1]).astype(BF16)

    passes = []
    for shift in pairs:
        src = peer(shift)
        for n, spot in enumerate(weight_spot(src, core)):
            landed(spot, r.w_recv, 2 * src + n)
            copy = remote(spot, spot, r.w_pass, 2 * shift + n, r.w_passed, 2 * src + n, partner)
            copy.start()
            passes.append(copy)
    wait(mine[3:])
    for shift in pairs:
        src = peer(shift)
        for n, spot in enumerate(weight_spot(src, other)):
            landed(spot, r.w_passed, 2 * src + n)
        landed(r.tables_v.at[src], r.x_recv, 3 * src + 1)

    slot_of = lambda d, c: pl.ds(pl.multiple_of((2 * d + c) * tokens, tokens), tokens)

    def plane_copies(src, target, base):
        spot = target.at[slot_of(dp, core)]
        found = [remote(src, spot, r.plane_send, base + shift, r.plane_recv, base + dp, (peer(shift), z, core)) for shift in pairs]
        return found + [remote(src, spot, r.plane_send, base, r.plane_recv, base + dp_n, partner)]

    def plane_pass(target, base):
        found = []
        for shift in pairs:
            src = peer(shift)
            spot = target.at[slot_of(src, core)]
            landed(spot, r.plane_recv, base + src)
            copy = remote(spot, spot, r.plane_pass, base + shift, r.plane_passed, base + src, partner)
            copy.start()
            found.append(copy)
        return found

    def plane_done(target, base):
        landed(target.at[slot_of(dp, other)], r.plane_recv, base + dp_n)
        for shift in pairs:
            src = peer(shift)
            landed(target.at[slot_of(src, other)], r.plane_passed, base + src)

    cots = plane_copies(r.own_cot, r.cot_all, 0)
    firsts, first_mine = [], []
    for n, weight in enumerate((r.w_gate, r.w_up)):
        for shift in range(dp_n):
            to = peer(shift)
            src = weight.at[:, pl.ds(pl.multiple_of((2 * to + core) * f8, 256), 256)]
            dst = r.w_first.at[span(dp, rows), pl.ds(256 * n, 256)]
            if shift == 0:
                first_mine.append(local(src, dst, r.out_sem, n))
            else:
                firsts.append(remote(src, dst, r.first_send, 2 * shift + n, r.first_recv, 2 * dp + n, (to, z, core)))
    cot_mine = local(r.own_cot, r.cot_all.at[slot_of(dp, core)], r.out_sem, 2)
    start(cots + firsts + first_mine + [cot_mine])

    split = q_cols + kv_cols
    r.qk[:, 0:q_cols] = dot(r.n1[...], r.w_all[:, 0:q_cols])
    pair = dot(r.n1[...], r.w_all[:, q_cols : q_cols + 2 * kv_cols])
    r.qk[:, q_cols:split] = pair[:, :kv_cols]
    r.value[...] = pair[:, kv_cols:].astype(BF16)
    outs = [
        local(r.n1, r.normed_one, r.out_sem, 3), local(r.w_all, r.w_qkv, r.out_sem, 4), local(r.qk, r.qk_pre, r.out_sem, 5),
        local(r.tables_v, r.tables, r.out_sem, 6), local(r.gains_v, r.gains, r.out_sem, 7),
    ]
    start(outs)

    def kv_copies(s):
        spot = r.kv.at[me, s]
        found = [
            remote(spot, spot, r.kv_send, s * lines + shift, r.kv_recv, s * (lines + 1) + z, (dp, lax.rem(z + shift, lines), core))
            for shift in range(1, lines)
        ]
        return found + [remote(spot, spot, r.kv_send, s * lines, r.kv_recv, s * (lines + 1) + lines, partner)]

    def kv_pass(s):
        found = []
        for shift in range(1, lines):
            src = lax.rem(z + shift, lines)
            spot = r.kv.at[2 * src + core, s]
            found.append((spot, s * (lines + 1) + src,
                          remote(spot, spot, r.kv_pass, s * lines + shift, r.kv_passed, s * lines + src, partner)))
        return found

    @pl.loop(0, dp_n)
    def _(turn):
        s = peer(turn + 1)
        cosine, sine = r.tables_v[s, :, 0:head], r.tables_v[s, :, head : 2 * head]
        turned = []
        where = span(s, tokens)
        for h in range(kv_heads * (group + 1)):
            gain = r.gains_v[2:3, 0:head] if h < kv_heads * group else r.gains_v[3:4, 0:head]
            hat, _ = norm_rows(r.qk[where, h * head : (h + 1) * head])
            hat = hat * gain
            swapped = jnp.concatenate([hat[:, head // 2 :], hat[:, : head // 2]], axis=1)
            turned.append((hat * cosine + swapped * sine).astype(BF16))
        r.q_rot[s] = jnp.concatenate(turned[: kv_heads * group], axis=1)
        r.kv[me, s] = jnp.concatenate(turned[kv_heads * group :] + [r.value[where]], axis=1)
        start(kv_copies(s))

    step = max(1, min(group, MIB // (2 * length * tokens)))

    def part_copy(s, shift):
        return remote(r.part.at[s], r.land.at[dp], r.part_send, shift, r.part_recv, dp, (s, z, core))

    @pl.loop(0, dp_n)
    def _(turn):
        s = peer(turn + 1)
        for spot, n, copy in kv_pass(s):
            landed(spot, r.kv_recv, n)
            copy.start()
        landed(r.kv.at[2 * z + other, s], r.kv_recv, s * (lines + 1) + lines)
        for shift in range(1, lines):
            src = lax.rem(z + shift, lines)
            landed(r.kv.at[2 * src + other, s], r.kv_passed, s * lines + src)
        both = r.kv[:, s].reshape(length, 2 * kv_cols)
        mask = jnp.concatenate([r.bias_v[...]] * step, axis=1)
        for g in range(kv_heads):
            keys = both[:, g * head : (g + 1) * head]
            values = both[:, (kv_heads + g) * head : (kv_heads + g + 1) * head]
            for first in range(g * group, (g + 1) * group, step):
                queries = jnp.concatenate([r.q_rot[s, :, h * head : (h + 1) * head] for h in range(first, first + step)], axis=0)
                scores = contract_cols(keys, queries) * scale + mask
                top = jnp.max(scores, axis=0, keepdims=True)
                weight = jnp.exp(scores - top)
                total = jnp.sum(weight, axis=0, keepdims=True)
                probs = (weight * (1.0 / total)).astype(BF16)
                offset = (first - g * group) * tokens
                r.log_v[s, pl.ds(g, 1), offset : offset + step * tokens] = top + jnp.log(total)
                out = contract_rows(values, probs).T.astype(BF16)
                r.mix[s, :, first * head : (first + step) * head] = jnp.concatenate(
                    [out[h * tokens : (h + 1) * tokens] for h in range(step)], axis=1)
        r.part[s] = dot(r.mix[s], r.w_out_v[...]).astype(BF16)

        @pl.when(turn < dp_n - 1)
        def _():
            part_copy(s, turn + 1).start()

    outs += [
        local(r.q_rot, r.query, r.out_sem, 8), local(r.kv, r.keys_values, r.out_sem, 9),
        local(r.log_v, r.log_total, r.out_sem, 10), local(r.mix, r.mixed, r.out_sem, 11),
    ]
    start(outs[5:])

    for shift in pairs:
        landed(r.land.at[peer(shift)], r.part_recv, peer(shift))
    r.land[dp] = r.part[dp]

    @pl.loop(0, tokens // 32)
    def _(i):
        where = span(i, 32)
        total = r.land[0, where].astype(F32)
        for src in range(1, dp_n):
            total += r.land[src, where].astype(F32)
        total += r.x_all[dp, where].astype(F32)
        r.hidden[where] = total
        hat, _ = norm_rows(total)
        r.n2[where] = (hat * r.gains_v[1:2]).astype(BF16)

    n2_base = dp_n + 1
    n2_copies = plane_copies(r.n2, r.normed_two, n2_base)
    start(n2_copies)
    n2_mine = local(r.n2, r.normed_two.at[slot_of(dp, core)], r.out_sem, 12)
    outs += [local(r.hidden, r.hidden_in, r.out_sem, 13), n2_mine]
    start(outs[9:])
    passed = plane_pass(r.cot_all, 0)
    passed += plane_pass(r.normed_two, n2_base)
    plane_done(r.cot_all, 0)
    for shift in pairs:
        src = peer(shift)
        for n in range(2):
            landed(r.w_first.at[span(src, rows), pl.ds(256 * n, 256)], r.first_recv, 2 * src + n)
    plane_done(r.normed_two, n2_base)
    wait(outs + first_mine + [cot_mine])
    for copy in small + weights + passes + cots + firsts + n2_copies + passed:
        copy.wait_send()

    @pl.loop(0, dp_n)
    def _(s):
        for copy in kv_copies(s):
            copy.wait_send()
        for _, _, copy in kv_pass(s):
            copy.wait_send()

    @pl.loop(0, dp_n - 1)
    def _(turn):
        part_copy(peer(turn + 1), turn + 1).wait_send()


def forward(x, dp_n, lines, head, collective_id):
    tokens, width = x.own_x.shape
    rows = width // dp_n
    kv_cols = x.w_pair.shape[2] // 2
    q_cols = x.w_query.shape[1] // dp_n
    kv_heads = kv_cols // head
    f8 = x.w_gate.shape[1] // (2 * dp_n)
    cols = q_cols + 2 * kv_cols
    length = 2 * lines * tokens
    dims = SimpleNamespace(
        dp_n=dp_n, lines=lines, tokens=tokens, width=width, rows=rows, f8=f8, head=head, group=q_cols // kv_cols,
        kv_heads=kv_heads, q_cols=q_cols, kv_cols=kv_cols,
    )
    bf16 = lambda *shape: jax.ShapeDtypeStruct(shape, BF16)
    f32 = lambda *shape: jax.ShapeDtypeStruct(shape, F32)
    all_tokens = dp_n * tokens
    group_rows = q_cols // kv_cols * tokens
    outs = FrontOut(
        normed_two=bf16(2 * all_tokens, width), cot_all=bf16(2 * all_tokens, width), w_first=bf16(width, 512),
        hidden_in=f32(tokens, width), w_qkv=bf16(width, cols), normed_one=bf16(all_tokens, width), qk_pre=f32(all_tokens, q_cols + kv_cols),
        query=bf16(dp_n, tokens, q_cols), keys_values=bf16(2 * lines, dp_n, tokens, 2 * kv_cols), log_total=f32(dp_n, kv_heads, group_rows),
        mixed=bf16(dp_n, tokens, q_cols), tables=f32(dp_n, tokens, 2 * head), gains=f32(8, width),
    )
    vmem = lambda *shape: pltpu.VMEM(shape, BF16)
    wide = lambda *shape: pltpu.VMEM(shape, F32)
    dma = lambda n: pltpu.SemaphoreType.DMA((n,))
    scratch = FrontScratch(
        x_all=vmem(dp_n, tokens, width), n1=vmem(all_tokens, width), w_all=vmem(width, cols), qk=wide(all_tokens, q_cols + kv_cols),
        value=vmem(all_tokens, kv_cols), q_rot=vmem(dp_n, tokens, q_cols), kv=vmem(2 * lines, dp_n, tokens, 2 * kv_cols),
        log_v=wide(dp_n, kv_heads, group_rows), mix=vmem(dp_n, tokens, q_cols), tables_v=wide(dp_n, tokens, 2 * head), gains_v=wide(8, width),
        bias_v=wide(length, tokens), w_out_v=vmem(rows, width), part=vmem(dp_n, tokens, width), land=vmem(dp_n, tokens, width),
        hidden=wide(tokens, width), n2=vmem(tokens, width), in_sem=dma(7), out_sem=dma(14), x_send=dma(3 * dp_n), x_recv=dma(3 * dp_n),
        w_send=dma(2 * dp_n), w_recv=dma(2 * dp_n), w_pass=dma(2 * dp_n), w_passed=dma(2 * dp_n), kv_send=dma(dp_n * lines),
        kv_recv=dma(dp_n * (lines + 1)), kv_pass=dma(dp_n * lines), kv_passed=dma(dp_n * lines), part_send=dma(dp_n), part_recv=dma(dp_n),
        plane_send=dma(2 * dp_n + 2), plane_recv=dma(2 * dp_n + 2), plane_pass=dma(2 * dp_n + 2), plane_passed=dma(2 * dp_n + 2),
        first_send=dma(2 * dp_n), first_recv=dma(2 * dp_n),
    )
    hbm = pl.BlockSpec(memory_space=pl.ANY)
    results = pl.pallas_call(
        partial(front_kernel, dims),
        out_shape=tuple(outs),
        in_specs=[hbm] * len(x),
        out_specs=(hbm,) * len(outs),
        scratch_shapes=list(scratch),
        compiler_params=pltpu.CompilerParams(collective_id=collective_id, has_side_effects=True, vmem_limit_bytes=63 * MIB),
        cost_estimate=pl.CostEstimate(flops=10**10, bytes_accessed=50 * MIB, transcendentals=0),
        name="forward",
    )(*x)
    return FrontOut(*results)


def local(
    inputs, attn_gain, w_query, w_key, w_value, q_gain, key_norm_gain, w_out, ffn_gain,
    w_gate, w_up, w_down, stretch_map, pos_ids, cotangent,
):
    dp, lines, cores = lax.axis_size("dp"), lax.axis_size("z"), lax.axis_size("core")
    core = lax.axis_index("core")
    rows, width = inputs.shape[1], inputs.shape[2]
    head = q_gain.shape[0]
    query_width, key_width, hidden = w_query.shape[1], w_key.shape[1], w_gate.shape[1]
    half = rows // 2
    stretches = stretch_map.shape[0]
    length = stretches * half
    ctx = lax.axis_index("z") * cores + core

    index = jnp.arange(rows, dtype=jnp.int32)
    blocks = jnp.arange(stretches, dtype=jnp.int32)
    own = 2 * ctx + index // half
    query_places = jnp.sum(jnp.where(blocks[None, :] == own[:, None], stretch_map[None, :], 0), axis=1) * half + index % half
    key_places = jnp.repeat(stretch_map, half, total_repeat_length=length) * half + jnp.tile(
        jnp.arange(half, dtype=jnp.int32), stretches
    )
    bias = jnp.where(key_places[:, None] <= query_places[None, :], 0.0, MASKED_SCORE).astype(F32)
    frequency = jnp.power(F32(ROPE_BASE), -2.0 * jnp.arange(head // 2, dtype=F32) / head)
    angles = pos_ids[0].astype(F32)[:, None] * frequency[None, :]
    cosine, sine = jnp.cos(angles), jnp.sin(angles)
    tables = jnp.concatenate([cosine, cosine, -sine, sine], axis=1)
    piece = width // dp
    gain_piece = jnp.zeros((8, piece), F32).at[0].set(attn_gain.astype(F32)).at[1].set(ffn_gain.astype(F32))
    gain_piece = gain_piece.at[2, :head].set(q_gain.astype(F32)).at[3, :head].set(key_norm_gain.astype(F32))
    kv_cols, q_cols = key_width // dp, query_width // dp
    w_pair = jnp.stack(
        [jnp.concatenate([w[:, n * kv_cols : (n + 1) * kv_cols] for w in (w_key, w_value)], axis=1) for n in range(dp)]
    )
    front = forward(
        FrontIn(
            own_x=inputs[0], own_cot=cotangent[0], w_query=w_query, w_pair=w_pair, gain_piece=gain_piece, own_tables=tables,
            bias=bias, w_out=w_out, w_gate=w_gate, w_up=w_up,
        ),
        dp, lines, head, 2,
    )
    f8 = hidden // (2 * dp)
    made = backward(
        BackIn(
            normed_two=front.normed_two, cot_all=front.cot_all, w_first=front.w_first, w_gate=w_gate, w_up=w_up, w_down=w_down,
            hidden_in=front.hidden_in, w_out=w_out, w_qkv=front.w_qkv, normed_one=front.normed_one.reshape(dp, rows, width),
            qk_pre=front.qk_pre.reshape(dp, rows, q_cols + kv_cols), query=front.query, keys_values=front.keys_values,
            log_total=front.log_total, mixed=front.mixed, bias=bias, tables=front.tables, gains=front.gains, own_x=inputs[0],
        ),
        dp, lines, head, 1,
    )
    place = lax.axis_index("dp").reshape(1)
    query_grad, key_grad, value_grad, out_grad, gate_grad, up_grad, down_grad = widen(
        made.totals, place, dp, width, f8, q_cols + 2 * kv_cols, q_cols, kv_cols
    )
    gains = made.gain_sum
    return (
        made.output[None], made.input_grad[None], lax.dynamic_slice_in_dim(gains[0], place[0] * piece, piece, 0), query_grad, key_grad,
        value_grad, gains[2, :head], gains[3, :head], out_grad, lax.dynamic_slice_in_dim(gains[1], place[0] * piece, piece, 0),
        gate_grad, up_grad, down_grad,
    )


def solution(mesh):
    dp, ctx = mesh.shape["dp"], mesh.shape["ctx"]
    fine = Mesh(mesh.devices.reshape(dp, ctx // 2, 2), ("dp", "z", "core"))
    tokens = P("dp", ("z", "core"), None)
    rows = P("dp", None)
    in_specs = (
        tokens, P("dp"), rows, rows, rows, P(), P(), rows, P("dp"), rows, rows, rows, P(), P("dp", ("z", "core")), tokens,
    )
    out_specs = (tokens, tokens, P("dp"), rows, rows, rows, P(), P(), rows, P("dp"), rows, rows, rows)
    return jax.shard_map(local, mesh=fine, in_specs=in_specs, out_specs=out_specs, check_vma=False)
```

time: 1880 us -> 753 us (0.40)
  Pallas kernels: 0 us -> 718 us
  waiting for transfers between devices: 669 us -> 0 us
  local copies, waits for them, and re-layouts: 467 us -> 10.4 us
  other arithmetic: 241 us -> 16 us
  matrix products: 222 us -> 0 us
  blocking collectives: 189 us -> 0 us
  starting transfers between devices: 54.7 us -> 0 us
    pallas_call x0 -> x7, Pallas kernels: none -> 718 us  [the longest x1 507 us: backward(): pl.pallas_call(partial(back_kernel, dims), out_shape=tuple(outs), in_spec...]
    psum x2 -> x0, waiting for transfers between devices: 391 us -> none  [the longest x1 391 us: finish_columns(): return rows_to_owner(lax.psum(grad.astype(BF16), 'z'), dp)]
    unnamed x124 -> x18, local copies, waits for them, and re-layouts: 302 us -> 2.21 us
    all_to_all x12 -> x0, waiting for transfers between devices: 240 us -> none  [the longest x5 120 us: columns_to_owner(): out = lax.all_to_all(mine.transpose(1, 0, 2), 'dp', 0, 0)]
    dot_general x77 -> x0, matrix products: 222 us -> none  [the longest x31 83.8 us: contract_cols(): lax.dot_general(left, right, (((1,), (1,)), ((), ())), preferred_element_...]
    convert_element_type x12 -> x0, local copies, waits for them, and re-layouts: 115 us -> none  [the longest x4 102 us: finish_hidden(): return mine.transpose(2, 1, 0, 3).reshape(width // dp, hidden).astype(F32)]
    all_to_all x2 -> x0, blocking collectives: 105 us -> none  [the longest x1 53.8 us: rows_to_owner(): return lax.all_to_all(grad.reshape(dp, rows // dp, width), 'dp', 0, 0)]
    add x16 -> x1, other arithmetic: 89.2 us -> 6.48 us  [local(): jnp.repeat(stretch_map, half, total_repeat_length=length) * half]
  transfers between devices with their start and end apart: 23 -> 0, of which waited for: 13 -> 0; matrix products, arithmetic and copies ran while one was open for 15% -> 0% of each run, Pallas kernels for 0% -> 0%
where the time goes in v3:
time: 753 us; the launch traced here: 745 us
  Pallas kernels  718 us (95%)
  other arithmetic  16 us (2%)
  local copies, waits for them, and re-layouts  10.4 us (1%)
    pallas_call x1, Pallas kernels, backward(): pl.pallas_call(partial(back_kernel, dims), out_shape=tuple(outs), in_spec...  507 us
    pallas_call x1, Pallas kernels, forward(): pl.pallas_call(partial(front_kernel, dims), out_shape=tuple(outs), in_spe...  153 us
    pallas_call x3, Pallas kernels, call(): pl.pallas_call(kernel, grid_spec=pltpu.PrefetchScalarGridSpec(num_scalar_...  42.8 us
    pallas_call x2, Pallas kernels, pieces(): pl.pallas_call(kernel, grid_spec=pltpu.PrefetchScalarGridSpec(num_scalar_...  15.3 us

profile of v3, /device:TPU:0, one launch (start us, length us, event | category | flops | bytes accessed | tf_op | source)
XLA Modules:
  0.0 745.3 jit_solution(13921200767206561227)
XLA Ops:
  0.7 1.9 fusion.8
  2.6 0.8 add_add_fusion.1
  3.4 4.6 compare_select_fusion.2
  8.0 0.1 compare_reduce_fusion.8
  8.1 0.1 tile.10
  8.2 6.5 fusion.2
  14.7 0.7 select_reduce_fusion
  15.4 1.0 compare_select_fusion.refs_6_.refs_15_
  16.4 1.1 fusion.5
  17.6 1.1 fusion.6
  18.7 0.1 maximum_bitcast_fusion
  18.8 0.1 maximum_bitcast_fusion.2
  18.8 1.1 pad_maximum_fusion.refs_3_
  20.0 0.3 multiply_cosine_fusion
  20.3 0.8 pad_maximum_fusion.1.refs_5_
  21.1 0.1 scatter.20
  21.2 0.2 scatter.21
  21.4 0.2 scatter.24.refs_4_
  21.7 0.6 copy-done.2
  22.3 152.5 %forward.1 = (bf16[1024,2048]{1,0:T(8,128)(2,1)}, bf16[1024,2048]{1,0:T(8,128)(2,1)}, bf16[2048,512]{1,0:T(8,128)(2,1)}, f32[128,2048]{1,0:T(8,128)}, bf16[2048,...) custom-call(bf16[128,2048]{1,0:T(8,128)(2,1)} %bitcast.66, ...), custom_call_target="tpu_custom_call" | custom-call | flops 10000000000 | bytes 52428800 | tf_op jit(solution)/shard_map/forward/pallas_call | solution.py:1472
  174.8 507.3 %backward.1 = (bf16[128,2048]{1,0:T(8,128)(2,1)}, bf16[128,2048]{1,0:T(8,128)(2,1)}, f32[8,2048]{1,0:T(8,128)}, bf16[2,29,512,512]{3,2,1,0:T(8,128)(2,1)}, bf16[...) custom-call(bf16[1024,2048]{1,0:T(8,128)(2,1)} %get-tuple-element.94, ...), custom_call_target="tpu_custom_call" | custom-call | flops 38654705664 | bytes 104857600 | tf_op jit(solution)/shard_map/backward/pallas_call | solution.py:984
  682.2 25.1 %widen_gate_up.1 = (f32[512,8192]{1,0:T(8,128)}, f32[512,8192]{1,0:T(8,128)}) custom-call(s32[1]{0:T(128)} %bitcast.36.place, bf16[2,29,512,512]{3,2,1,0:T(8,128)(2,1)} %get-tuple-element.110.totals), custom_call_target="tpu_custom_call" | custom-call | tf_op jit(solution)/shard_map/widen_gate_up/pallas_call | solution.py:1029
  707.3 13.5 %widen_down.1 = f32[2048,2048]{1,0:T(8,128)} custom-call(s32[1]{0:T(128)} %bitcast.36.place, bf16[2,29,512,512]{3,2,1,0:T(8,128)(2,1)} %get-tuple-element.110.totals), custom_call_target="tpu_custom_call" | custom-call | tf_op jit(solution)/shard_map/widen_down/pallas_call | solution.py:1029
  720.8 9.8 %widen_query.1 = f32[512,2048]{1,0:T(8,128)} custom-call(s32[1]{0:T(128)} %bitcast.36.place, bf16[2,29,512,512]{3,2,1,0:T(8,128)(2,1)} %get-tuple-element.110.totals), custom_call_target="tpu_custom_call" | custom-call | tf_op jit(solution)/shard_map/widen_query/pallas_call | solution.py:1058
  730.6 4.2 widen_out.1
  734.8 5.5 widen_key_value.1
  740.3 0.9 fusion.7
  741.2 0.6 constant_dynamic-slice_fusion
  741.8 0.6 constant_dynamic-slice_fusion.1
  742.4 1.3 slice_bitcast_fusion
  743.7 0.8 copy.34
  744.5 0.8 copy.35
  (26 shorter events, 0.1 us)
Async XLA Ops:
  0.6 19.3 %copy-start.5 = (s32[1,128]{1,0:T(1,128)S(1)}, s32[1,128]{1,0:T(1,128)}, u32[]{:S(2)}) copy-start(s32[1,128]{1,0:T(1,128)} %param.38) | copy-start | bytes 1540
  0.7 20.4 %copy-start.3 = (bf16[512]{0:T(512)(128)(2,1)S(1)}, bf16[512]{0:T(512)(128)(2,1)}, u32[]{:S(2)}) copy-start(bf16[512]{0:T(512)(128)(2,1)} %param.26) | copy-start | bytes 3076
  0.7 20.4 %copy-start.4 = (bf16[512]{0:T(512)(128)(2,1)S(1)}, bf16[512]{0:T(512)(128)(2,1)}, u32[]{:S(2)}) copy-start(bf16[512]{0:T(512)(128)(2,1)} %param.33) | copy-start | bytes 3076
  0.7 20.5 %copy-start.6 = (bf16[64]{0:T(256)(128)(2,1)S(1)}, bf16[64]{0:T(256)(128)(2,1)}, u32[]{:S(2)}) copy-start(bf16[64]{0:T(256)(128)(2,1)} %param.30) | copy-start | bytes 388
  0.7 20.7 %copy-start.7 = (bf16[64]{0:T(256)(128)(2,1)S(1)}, bf16[64]{0:T(256)(128)(2,1)}, u32[]{:S(2)}) copy-start(bf16[64]{0:T(256)(128)(2,1)} %param.31) | copy-start | bytes 388
  21.7 0.6 copy-start.2
  734.8 8.9 %copy-start.1 = (bf16[128,2048]{1,0:T(8,128)(2,1)S(1)}, bf16[128,2048]{1,0:T(8,128)(2,1)}, u32[]{:S(2)}) copy-start(bf16[128,2048]{1,0:T(8,128)(2,1)} %get-tuple-element.107) | copy-start | bytes 1572868
  734.8 9.7 %copy-start = (bf16[128,2048]{1,0:T(8,128)(2,1)S(1)}, bf16[128,2048]{1,0:T(8,128)(2,1)}, u32[]{:S(2)}) copy-start(bf16[128,2048]{1,0:T(8,128)(2,1)} %get-tuple-element.108) | copy-start | bytes 1572868

commit v4 on v3

--- a/solution.py
+++ b/solution.py
@@ -56,8 +56,9 @@
         self.second = self.totals.at[self.core]
         self.quarter = self.rows // 4
         self.half = self.rows // 2
-        self.lag = 5 + 2 * (self.middle - self.place)
-        self.most = 5 + 2 * self.middle + 3
+        self.ahead = 4
+        self.lag = 7 + 3 * (self.middle - self.place)
+        self.most = 7 + 3 * self.middle + 3
         self.n_ffn = self.n_blocks * self.per_block
         self.q_first = self.n_ffn + 2
         self.piece = self.qkv_cols // 3
@@ -83,7 +84,7 @@
             device_id=(self.dp, self.inner, self.core), device_id_type=MESH)
 
     def send_owner(self, k):
-        total = self.total_slot.at[lax.rem(k, 4)]
+        total = self.total_slot.at[lax.rem(k, 8)]
         shift = self.shift_of(k)
         local = pltpu.make_async_copy(total, self.second.at[k], self.second_recv.at[k])
         remote = pltpu.make_async_remote_copy(
@@ -114,13 +115,13 @@
 
     def stage_one(self, k):
         self.ready(k)
-        mine = self.sum_slot.at[lax.rem(k, 4)]
+        mine = self.sum_slot.at[lax.rem(k, 8)]
 
         @pl.when(self.place == 0)
         def _():
-            @pl.when(k >= 2)
+            @pl.when(k >= self.ahead)
             def _():
-                self.send_inner(k - 2, self.own.at[k - 2]).wait_send()
+                self.send_inner(k - self.ahead, self.own.at[k - self.ahead]).wait_send()
 
             self.send_inner(k, self.own.at[k]).start()
 
@@ -144,12 +145,12 @@
     def stage_sum(self, k):
         @pl.when((self.place == self.middle) & self.ours(k))
         def _():
-            mine = self.sum_slot.at[lax.rem(k, 4)]
+            mine = self.sum_slot.at[lax.rem(k, 8)]
             self.send_across(k, mine).wait_recv()
             arrived = self.load(self.cross.at[k], self.in_slot, 2)
             arrived.start()
             arrived.wait()
-            add_chunk(self.total_slot.at[lax.rem(k, 4)], mine, self.in_slot)
+            add_chunk(self.total_slot.at[lax.rem(k, 8)], mine, self.in_slot)
             shift, local, remote = self.send_owner(k)
 
             @pl.when(shift == 0)
@@ -194,7 +195,7 @@
         def _():
             self.spread_outer(k).wait_send()
 
-        @pl.when((self.place == 0) & (k >= self.chunks - 2))
+        @pl.when((self.place == 0) & (k >= self.chunks - self.ahead))
         def _():
             self.send_inner(k, self.own.at[k]).wait_send()
 
@@ -229,20 +230,45 @@
         def _():
             self.stage_one(t)
 
-        def when(k, act, extra=True):
-            @pl.when((k >= 0) & (k < self.chunks) & extra)
+        at_middle = self.place == self.middle
+
+        def upto(most, least):
+            begin = self.n_ffn - 2
+
+            def last(n):
+                caught = jnp.minimum(n - least, 2 * n - begin - most)
+                return jnp.clip(jnp.where(n < begin, n - most, caught), -1, self.chunks - 1)
+
+            return pl.loop(last(t - 1) + 1, last(t) + 1)
+
+        def fixed(k, act):
+            @pl.when((k >= 0) & (k < self.chunks))
             def _():
                 act(k)
 
-        at_middle = self.place == self.middle
-        when(t - 2, self.stage_sum)
-        when(t - 3, self.stage_sent)
-        when(t - 4, self.stage_handed)
-        early = at_middle & self.ours(jnp.maximum(t - 3, 0))
-        late = jnp.logical_not(at_middle & self.ours(jnp.maximum(t - self.lag, 0)))
-        when(t - 3, self.stage_two, early)
-        when(t - self.lag, self.stage_two, late)
-        when(t - self.lag - 3, self.stage_three)
+        fixed(t - 9, self.stage_handed)
+
+        @upto(2, 1)
+        def _(k):
+            self.stage_sum(k)
+
+        fixed(t - 7, self.stage_sent)
+
+        @upto(4, 2)
+        def _(k):
+            @pl.when(at_middle & self.ours(k))
+            def _():
+                self.stage_two(k)
+
+        steps = self.middle - self.place
+
+        @upto(7 + 3 * steps, 3 + 2 * steps)
+        def _(k):
+            @pl.when(jnp.logical_not(at_middle & self.ours(k)))
+            def _():
+                self.stage_two(k)
+
+        fixed(t - self.lag - 3, self.stage_three)
 
     def advance_at(self, first, count):
         for j in range(count):
@@ -300,8 +326,6 @@
     out_pair: Any
     out_land: Any
     out_keep: Any
-    pair_o: Any
-    pair_q: Any
 
 
 class BackScratch(NamedTuple):
@@ -328,7 +352,8 @@
     dn1_land: Any
     result: Any
     pair_slot: Any
-    pair_q_slot: Any
+    pair_o: Any
+    pair_q: Any
     load_sem: Any
     own_sem: Any
     first_send: Any
@@ -509,36 +534,50 @@
         line.position = n_blocks * 2
 
         def sums(part):
-            def to_partner(hidden):
-                base = 0 if hidden else dp_n
-                return [
-                    remote(part.at[i, span(other, tokens)], (r.dn2_pair if hidden else r.out_pair).at[i], r.sum_send, base + i, r.pair_recv, base + i, partner)
-                    for i in range(dp_n)
-                ]
-
-            def plane_sum(hidden, product):
-                @pl.loop(0, dp_n)
-                def _(i):
-                    @pl.loop(0, width // 512)
-                    def _(n):
-                        part[i, :, span(n, 512)] = product(span(i, 2 * tokens), span(n, 512)).astype(BF16)
-
-                to_pair = to_partner(hidden)
-                start(to_pair)
-                for i in range(dp_n):
-                    to_pair[i].wait_recv()
-                    copy = local((r.dn2_pair if hidden else r.out_pair).at[i], r.land_slot, r.in_sem, 3)
-                    copy.start()
-                    copy.wait()
-                    mine = part.at[i, span(core, tokens)]
-                    add_rows(mine, mine, r.land_slot)
-
-            def own_sums():
-                return [
-                    remote(part.at[peer(shift), span(core, tokens)], r.dn2_land.at[dp], r.sum_send, 2 * dp_n + shift,
-                           r.land_recv, dp, (peer(shift), z, core))
-                    for shift in pairs
-                ]
+            def own_sum(turn):
+                to = peer(turn)
+                return remote(part.at[to, span(core, tokens)], r.dn2_land.at[dp], r.sum_send, 2 * dp_n + turn, r.land_recv, dp, (to, z, core))
+
+            def plane_sum(hidden, product, every):
+                def to_pair(i):
+                    base = 0 if hidden else dp_n
+                    pair = r.dn2_pair if hidden else r.out_pair
+                    return remote(part.at[i, span(other, tokens)], pair.at[i], r.sum_send, base + i, r.pair_recv, base + i, partner), pair
+
+                @pl.loop(0, dp_n + 1)
+                def _(turn):
+                    @pl.when(turn < dp_n)
+                    def _():
+                        i = peer(turn + 1)
+
+                        @pl.loop(0, width // 512)
+                        def _(n):
+                            part[i, :, span(n, 512)] = product(span(i, 2 * tokens), span(n, 512)).astype(BF16)
+
+                        to_pair(i)[0].start()
+
+                    @pl.when(turn > 0)
+                    def _():
+                        i = peer(turn)
+                        copy, pair = to_pair(i)
+                        copy.wait_recv()
+                        copy = local(pair.at[i], r.land_slot, r.in_sem, 3)
+                        copy.start()
+                        copy.wait()
+                        mine = part.at[i, span(core, tokens)]
+                        add_rows(mine, mine, r.land_slot)
+                        if hidden:
+                            @pl.when(turn < dp_n)
+                            def _():
+                                own_sum(turn).start()
+                        else:
+                            local(mine, r.out_keep.at[i], r.in_sem, 7 + turn).start()
+
+                        @pl.when(lax.rem(turn, every) == 0)
+                        def _():
+                            line.advance_at(line.position + turn // every - 1, 1)
+
+                line.position += dp_n // every
 
             def hidden_grad(where, columns):
                 total = contract_cols(grads[0, where], w_gu[0, columns])
@@ -552,20 +591,21 @@
                     total += dot(act[b, where], wd[pl.ds(b * 256, 256), columns])
                 return total
 
-            plane_sum(True, hidden_grad)
+            def pair_sent(base):
+                for i in range(dp_n):
+                    remote(part.at[i, span(other, tokens)], r.dn2_pair.at[i], r.sum_send, base + i, r.pair_recv, base + i, partner).wait_send()
+
+            plane_sum(True, hidden_grad, max(1, dp_n // 4))
             mine = local(part.at[dp, span(core, tokens)], r.dn2_land.at[dp], r.in_sem, 4)
-            start(own_sums() + [mine])
-            line.advance(2)
+            mine.start()
             mine.wait()
-            for copy in own_sums() + to_partner(True):
-                copy.wait_send()
-            plane_sum(False, ffn_out)
-            keep = [local(part.at[i, span(core, tokens)], r.out_keep.at[i], r.in_sem, 8 + i) for i in range(dp_n)]
-            start(keep)
-            line.advance(1)
-            wait(keep)
-            for copy in to_partner(False):
-                copy.wait_send()
+            pair_sent(0)
+            for shift in pairs:
+                own_sum(shift).wait_send()
+            plane_sum(False, ffn_out, max(1, dp_n // 2))
+            for turn in range(1, dp_n + 1):
+                local(part.at[0, span(core, tokens)], r.out_keep.at[0], r.in_sem, 7 + turn).wait()
+            pair_sent(dp_n)
 
         pl.run_scoped(sums, pltpu.VMEM((dp_n, 2 * tokens, width), BF16))
 
@@ -621,6 +661,8 @@
             found.append(remote(kv_sum.at[s, to], r.kv_land.at[z, s], r.kv_send, dp_n + s * lines + shift,
                                 r.kv_recv, dp_n + s * lines + z, (dp, to, core)))
         return found
+
+    every = max(1, dp_n // 4)
 
     def sequences(w_out, query, keys_values, bias, grad_mixed, grad_kv):
         loads = [
@@ -688,7 +730,9 @@
             def _():
                 pass_on(turn - 1)
 
-            line.advance_at(line.position + turn * dims.pace, dims.pace)
+            @pl.when(lax.rem(turn, every) == 0)
+            def _():
+                line.advance_at(line.position + turn // every, 1)
 
         pass_on(dp_n - 1)
 
@@ -702,7 +746,7 @@
         pltpu.VMEM((rows, width), BF16), seqs(tokens, q_cols), pltpu.VMEM((2 * lines, dp_n, tokens, 2 * kv_cols), BF16),
         pltpu.VMEM((length, tokens), F32), pltpu.VMEM((tokens, q_cols), BF16), seqs(lines, 2, tokens, 2 * kv_cols),
     )
-    line.position += dp_n * dims.pace
+    line.position += dp_n // every
     assert line.position <= n_ffn
 
     def projections(w_qkv, normed_one, qk_pre, mixed, tables, out_part, qkv_part, dn1_part):
@@ -721,9 +765,14 @@
                 total += contract_rows(mixed[s], r.dx_all[s, :, span(n, 512)])
             out_part[:, span(n, 512)] = total.astype(BF16)
 
+            @pl.when(n == 1)
+            def _():
+                line.advance_at(line.position, 1)
+
+        line.position += 1
+
         pair_o = remote(out_part.at[span(other, half)], r.pair_o, r.pair_send, 0, r.pair_land, 0, partner)
         pair_o.start()
-        line.advance(1)
 
         q_gain, k_gain = gains[2:3, 0:head], gains[3:4, 0:head]
         zero = jnp.zeros((1, head), F32)
@@ -755,25 +804,29 @@
                 back = grad * (k_gain if is_key else q_gain)
                 outs.append((inverse * (back - hat * jnp.mean(back * hat, axis=-1, keepdims=True))).astype(BF16))
             grad_qkv[s] = jnp.concatenate(outs + [kv[:, kv_cols:]], axis=1)
+
+            @pl.when(lax.rem(turn, max(1, dp_n // 2)) == 0)
+            def _():
+                line.advance_at(line.position + turn // max(1, dp_n // 2), 1)
+
             return tuple(sums)
 
         q_sum, k_sum = lax.fori_loop(0, dp_n, rotate, (zero, zero))
+        line.position += 2
+        assert line.position <= n_ffn
+        slot = r.pair_slot
+        pair_o.wait_recv()
+        for j in range(2):
+            for c in range(4):
+                mine = out_part[pl.ds(pl.multiple_of(core * half + j * quarter, quarter), quarter), pl.ds(c * 512, 512)]
+                arrived = r.pair_o[pl.ds(j * quarter, quarter), pl.ds(c * 512, 512)]
+                slot[j, pl.ds(c * quarter, quarter), :] = (mine.astype(F32) + arrived.astype(F32)).astype(BF16)
+        copies = [local(slot.at[j], own.at[n_ffn + j], r.stage_sem, j) for j in range(2)]
+        start(copies)
+        wait(copies)
         gain_acc[2:3, 0:head] = q_sum
         gain_acc[3:4, 0:head] = k_sum
         line.advance(1)
-
-        @pl.loop(0, width // 512)
-        def _(n):
-            weights = w_qkv[span(n, 512)]
-            for s in range(dp_n):
-                dn1_part[s, :, span(n, 512)] = contract_cols(grad_qkv[s], weights).astype(BF16)
-
-        dn1_sends = []
-        for shift in pairs:
-            to = peer(shift)
-            dn1_sends.append(remote(dn1_part.at[to], r.dn1_land.at[dp], r.dn1_send, shift, r.dn1_recv, dp, (to, z, core)))
-        start(dn1_sends)
-        r.dn1_land[dp] = dn1_part[dp]
 
         @pl.loop(0, dp_n)
         def _(i):
@@ -787,32 +840,28 @@
             for i in range(dp_n)
         ]
         start(pair_q)
-
         line.advance(1)
 
-        slot = r.pair_slot
-        pair_o.wait_recv()
-        for j in range(2):
-            for c in range(4):
-                copy = local(r.pair_o.at[pl.ds(j * quarter, quarter), pl.ds(c * 512, 512)], slot.at[span(c, quarter), pl.ds(0, 512)], r.stage_sem, c)
-                copy.start()
-                copy.wait()
-                mine = out_part[pl.ds(pl.multiple_of(core * half + j * quarter, quarter), quarter), pl.ds(c * 512, 512)]
-                where = pl.ds(c * quarter, quarter)
-                slot[where, 0:512] = (mine.astype(F32) + slot[where, 0:512].astype(F32)).astype(BF16)
-            copy = local(slot.at[pl.ds(0, rows), pl.ds(0, 512)], own.at[n_ffn + j], r.stage_sem, 0)
-            copy.start()
-            copy.wait()
+        @pl.loop(0, width // 512)
+        def _(n):
+            weights = w_qkv[span(n, 512)]
+            for s in range(dp_n):
+                dn1_part[s, :, span(n, 512)] = contract_cols(grad_qkv[s], weights).astype(BF16)
+
+        dn1_sends = []
+        for shift in pairs:
+            to = peer(shift)
+            dn1_sends.append(remote(dn1_part.at[to], r.dn1_land.at[dp], r.dn1_send, shift, r.dn1_recv, dp, (to, z, core)))
+        r.dn1_land[dp] = dn1_part[dp]
+        line.advance(1)
+
         piece = line.piece
         q_sends = []
         q_mine = []
         for i in range(dp_n):
             pair_q[i].wait_recv()
-            copy = local(r.pair_q.at[i], r.pair_q_slot, r.stage_sem, 0)
-            copy.start()
-            copy.wait()
             mine = qkv_part.at[i, span(core, half)]
-            mine[...] = (mine[...].astype(F32) + r.pair_q_slot[...].astype(F32)).astype(BF16)
+            mine[...] = (mine[...].astype(F32) + r.pair_q[i].astype(F32)).astype(BF16)
         for shift in range(dp_n):
             to = peer(shift)
             for j in range(3):
@@ -823,14 +872,16 @@
                 else:
                     q_sends.append(remote(src, line.q_own(number), r.q_send, shift * 3 + j, r.own_sem, number, (to, z, core)))
         start(q_sends + q_mine)
-
+        assert line.position <= line.q_first
+        start(dn1_sends)
+        line.advance(1)
         out_sends = [
             remote(r.out_keep.at[peer(shift)], r.out_land.at[dp], r.sum_send, 3 * dp_n + shift, r.land_recv, dp_n + dp, (peer(shift), z, core))
             for shift in pairs
         ]
         out_mine = local(r.out_keep.at[dp], r.out_land.at[dp], r.in_sem, 4)
         start(out_sends + [out_mine])
-        line.advance(2)
+        line.advance(1)
 
         for shift in pairs:
             src = peer(shift)
@@ -951,26 +1002,25 @@
     dims = SimpleNamespace(
         dp_n=dp_n, lines=lines, tokens=tokens, width=width, rows=rows, f8=f8, n_blocks=n_blocks, per_block=per_block,
         down_block=down_block, head=head, group=q_cols // kv_cols, kv_heads=kv_heads, q_cols=q_cols, kv_cols=kv_cols,
-        qkv_cols=cols, chunks=chunks, pace=1,
+        qkv_cols=cols, chunks=chunks,
     )
     bf16 = lambda *shape: jax.ShapeDtypeStruct(shape, BF16)
     outs = BackOut(
         output=bf16(tokens, width), input_grad=bf16(tokens, width), gain_sum=jax.ShapeDtypeStruct((8, width), F32),
         totals=bf16(2, chunks, rows, 512), own=bf16(chunks, rows, 512), first=bf16(chunks, rows, 512),
         cross=bf16(chunks, rows, 512), w_land=bf16(n_blocks, width, 512), dn2_pair=bf16(dp_n, tokens, width), out_pair=bf16(dp_n, tokens, width), out_land=bf16(dp_n, tokens, width), out_keep=bf16(dp_n, tokens, width),
-        pair_o=bf16(rows // 2, width), pair_q=bf16(dp_n, rows // 2, cols),
     )
     vmem = lambda *shape: pltpu.VMEM(shape, BF16)
     dma = lambda n: pltpu.SemaphoreType.DMA((n,))
     scratch = BackScratch(
-        sum_slot=vmem(4, rows, 512), total_slot=vmem(4, rows, 512), in_slot=vmem(rows, 512),
+        sum_slot=vmem(8, rows, 512), total_slot=vmem(8, rows, 512), in_slot=vmem(rows, 512),
         kv_sum=vmem(dp_n, lines, tokens, 2 * kv_cols), grad_query=vmem(dp_n, tokens, q_cols), grad_qkv=vmem(dp_n, tokens, cols),
         dn2_land=vmem(dp_n, tokens, width),
         land_slot=vmem(tokens, width), hidden_v=pltpu.VMEM((tokens, width), F32), grad_hidden=pltpu.VMEM((tokens, width), F32),
         own_x_v=vmem(tokens, width), cot_own=vmem(tokens, width), gains_v=pltpu.VMEM((8, width), F32), gain_acc=pltpu.VMEM((8, width), F32),
         dx_all=vmem(dp_n, tokens, width), kv_pair=vmem(dp_n, lines, tokens, 2 * kv_cols), kv_land=vmem(lines, dp_n, tokens, 2 * kv_cols),
         gain_core=pltpu.VMEM((2, 8, width), F32), gain_dp=pltpu.VMEM((dp_n, 8, width), F32), gain_z=pltpu.VMEM((lines, 8, width), F32),
-        dn1_land=vmem(dp_n, tokens, width), result=vmem(tokens, width), pair_slot=vmem(rows, 512), pair_q_slot=vmem(rows // 2, cols),
+        dn1_land=vmem(dp_n, tokens, width), result=vmem(tokens, width), pair_slot=vmem(2, rows, 512), pair_o=vmem(rows // 2, width), pair_q=vmem(dp_n, rows // 2, cols),
         load_sem=dma(3), own_sem=dma(3 * dp_n), first_send=dma(chunks), first_recv=dma(chunks),
         second_send=dma(chunks), cross_recv=dma(chunks), owner_send=dma(chunks), across_send=dma(chunks), second_recv=dma(chunks), core_send=dma(chunks), core_recv=dma(chunks),
         w_send=dma(2 * n_blocks * dp_n), w_recv=dma(2 * n_blocks * dp_n), stage_sem=dma(per_block),
@@ -994,87 +1044,83 @@
     return BackOut(*results)
 
 
-def widen_piece_kernel(place, totals, out):
-    out[...] = totals[0, 0].astype(F32)
-
-
-def widen_halves_kernel(place, totals, left, right):
-    middle = left.shape[1]
-    left[...] = totals[0, 0, :, :middle].astype(F32)
-    right[...] = totals[0, 0, :, middle:].astype(F32)
-
-
-def widen_pair_kernel(place, totals, gate, up):
-    gate[...] = totals[0, 0, :, 0:256].astype(F32)
-    up[...] = totals[0, 0, :, 256:512].astype(F32)
-
-
-def widen_rows_kernel(place, totals, out):
-    quarter = out.shape[0]
-    for c in range(4):
-        out[:, c * 512 : (c + 1) * 512] = totals[0, 0, c * quarter : (c + 1) * quarter, :].astype(F32)
-
-
-def widen(totals, place, dp_n, width, f8, cols, q_cols, kv_cols):
+def widen_pair_kernel(n_blocks, place, *refs):
+    gate, up = refs[n_blocks:]
+    for b in range(n_blocks):
+        columns = slice(b * 256, (b + 1) * 256)
+        gate[:, columns] = refs[b][0, 0, :, 0:256].astype(F32)
+        up[:, columns] = refs[b][0, 0, :, 256:512].astype(F32)
+
+
+def widen_rows(out, chunks):
+    quarter = chunks[0].shape[2] // 4
+    for j, chunk in enumerate(chunks):
+        for c in range(4):
+            out[j * quarter : (j + 1) * quarter, c * 512 : (c + 1) * 512] = chunk[0, 0, c * quarter : (c + 1) * quarter, :].astype(F32)
+
+
+def widen_rows_kernel(place, *refs):
+    widen_rows(refs[-1], refs[:-1])
+
+
+def widen_heads_kernel(dp_n, q_cols, kv_cols, place, *refs):
+    out, query, key, value = refs[-4:]
+    widen_rows(out, refs[:2])
+    chunks = refs[2:-4]
+    half = query.shape[0]
+    piece = (q_cols + 2 * kv_cols) // 3
+    across = 512 // piece
+    for src in range(dp_n):
+        for j in range(3):
+            chunk, spot = divmod(3 * src + j, 2 * across)
+            row, column = spot // across * half, spot % across * piece
+            part = chunks[chunk][0, 0, row : row + half, column : column + piece].astype(F32)
+            if j < 2:
+                query[:, src * q_cols + j * piece : src * q_cols + (j + 1) * piece] = part
+            else:
+                key[:, src * kv_cols : (src + 1) * kv_cols] = part[:, :kv_cols]
+                value[:, src * kv_cols : (src + 1) * kv_cols] = part[:, kv_cols:]
+
+
+def widen(totals, place, dp_n, width, f8, q_cols, kv_cols):
     _, chunks, rows, _ = totals.shape
-    quarter, half = rows // 4, rows // 2
-    down_block = 256 // quarter
+    half = rows // 2
+    down_block = 1024 // rows
     per_block = down_block + dp_n
     n_blocks = f8 // 256
     n_ffn = n_blocks * per_block
     f32 = lambda *shape: jax.ShapeDtypeStruct(shape, F32)
-    params = pltpu.CompilerParams(vmem_limit_bytes=40 * MIB)
-
-    def call(kernel, grid, in_map, out_specs, out_shape, name):
+
+    def call(kernel, grid, in_maps, out_specs, out_shape, name):
         return pl.pallas_call(
             kernel,
             grid_spec=pltpu.PrefetchScalarGridSpec(
-                num_scalar_prefetch=1, grid=grid, in_specs=[pl.BlockSpec((1, 1, rows, 512), in_map)], out_specs=out_specs),
-            out_shape=out_shape, compiler_params=params, name=name,
-        )(place, totals)
-
-    columns = lambda src, who, b, place: (0, (2 * src + who) * n_blocks + b)
+                num_scalar_prefetch=1, grid=grid, in_specs=[pl.BlockSpec((1, 1, rows, 512), m) for m in in_maps], out_specs=out_specs),
+            out_shape=out_shape, compiler_params=pltpu.CompilerParams(vmem_limit_bytes=48 * MIB), name=name,
+        )(place, *[totals] * len(in_maps))
+
+    def gate_map(b):
+        return lambda src, who, place: (who, b * per_block + down_block + lax.rem(place[0] - src + dp_n, dp_n), 0, 0)
+
     gate, up = call(
-        widen_pair_kernel, (dp_n, 2, n_blocks),
-        lambda src, who, b, place: (who, b * per_block + down_block + lax.rem(place[0] - src + dp_n, dp_n), 0, 0),
-        (pl.BlockSpec((rows, 256), columns),) * 2, (f32(rows, 2 * dp_n * f8),) * 2, "widen_gate_up")
+        partial(widen_pair_kernel, n_blocks), (dp_n, 2), [gate_map(b) for b in range(n_blocks)],
+        (pl.BlockSpec((rows, f8), lambda src, who, place: (0, 2 * src + who)),) * 2, (f32(rows, 2 * dp_n * f8),) * 2, "widen_gate_up")
+
+    def down_map(j):
+        return lambda who, b, place: (who, b * per_block + j, 0, 0)
+
     down = call(
-        widen_rows_kernel, (2, n_blocks, down_block),
-        lambda who, b, j, place: (who, b * per_block + j, 0, 0),
-        pl.BlockSpec((quarter, width), lambda who, b, j, place: ((who * n_blocks + b) * down_block + j, 0)),
-        f32(2 * f8, width), "widen_down")
-    out = call(
-        widen_rows_kernel, (2, 2), lambda who, j, place: (who, n_ffn + j, 0, 0),
-        pl.BlockSpec((quarter, width), lambda who, j, place: (2 * who + j, 0)), f32(rows, width), "widen_out")
-    piece = cols // 3
-    across = 512 // piece
-    per_chunk = 2 * across
-
-    def piece_map(number, who):
-        spot = lax.rem(number, per_chunk)
-        return (who, n_ffn + 2 + number // per_chunk, spot // across, lax.rem(spot, across))
-
-    def pieces(kernel, grid, in_map, out_specs, out_shape, name):
-        return pl.pallas_call(
-            kernel,
-            grid_spec=pltpu.PrefetchScalarGridSpec(
-                num_scalar_prefetch=1, grid=grid, in_specs=[pl.BlockSpec((1, 1, half, piece), in_map)], out_specs=out_specs),
-            out_shape=out_shape, compiler_params=params, name=name,
-        )(place, totals)
-
-    query = pieces(
-        widen_piece_kernel, (dp_n, 2, 2), lambda src, who, j, place: piece_map(3 * src + j, who),
-        pl.BlockSpec((half, piece), lambda src, who, j, place: (who, 2 * src + j)), f32(rows, dp_n * q_cols), "widen_query")
-    kv_in = lambda src, who, place: piece_map(3 * src + 2, who)
-    if kv_cols % 128 == 0:
-        key, value = pieces(
-            widen_halves_kernel, (dp_n, 2), kv_in, (pl.BlockSpec((half, kv_cols), lambda src, who, place: (who, src)),) * 2,
-            (f32(rows, dp_n * kv_cols),) * 2, "widen_key_value")
-    else:
-        both = pieces(
-            widen_piece_kernel, (dp_n, 2), kv_in, pl.BlockSpec((half, piece), lambda src, who, place: (who, src)),
-            f32(rows, dp_n * piece), "widen_key_value").reshape(rows, dp_n, 2, kv_cols)
-        key, value = (both[:, :, n].reshape(rows, dp_n * kv_cols) for n in range(2))
+        widen_rows_kernel, (2, n_blocks), [down_map(j) for j in range(down_block)],
+        pl.BlockSpec((256, width), lambda who, b, place: (who * n_blocks + b, 0)), f32(2 * f8, width), "widen_down")
+
+    def tail_map(k):
+        return lambda who, place: (who, k, 0, 0)
+
+    half_rows = lambda columns: pl.BlockSpec((half, columns), lambda who, place: (who, 0))
+    widths = (width, dp_n * q_cols, dp_n * kv_cols, dp_n * kv_cols)
+    out, query, key, value = call(
+        partial(widen_heads_kernel, dp_n, q_cols, kv_cols), (2,), [tail_map(k) for k in range(n_ffn, chunks)],
+        tuple(half_rows(columns) for columns in widths), tuple(f32(rows, columns) for columns in widths), "widen_heads")
     return query, key, value, out, gate, up, down
 
 
@@ -1082,7 +1128,8 @@
     own_x: Any
     own_cot: Any
     w_query: Any
-    w_pair: Any
+    w_key: Any
+    w_value: Any
     gain_piece: Any
     own_tables: Any
     bias: Any
@@ -1197,9 +1244,20 @@
         local(r.own_x, r.x_all.at[dp], r.in_sem, 0), local(r.own_tables, r.tables_v.at[dp], r.in_sem, 1),
         local(r.gain_piece, r.gains_v.at[:, span(dp, rows)], r.in_sem, 2), local(r.bias, r.bias_v, r.in_sem, 3),
         local(r.w_out, r.w_out_v, r.in_sem, 4),
-        local(r.w_query.at[:, span(dp, q_cols)], r.w_all.at[span(dp, rows), pl.ds(0, q_cols)], r.in_sem, 5),
-        local(r.w_pair.at[dp], r.w_all.at[span(dp, rows), pl.ds(q_cols, 2 * kv_cols)], r.in_sem, 6),
     ]
+    ends = (0, q_cols, q_cols + kv_cols, q_cols + 2 * kv_cols) if kv_cols % 128 == 0 else (0, q_cols, q_cols + 2 * kv_cols)
+    n_pieces = len(ends) - 1
+
+    def weight_from(to, where):
+        if n_pieces == 3:
+            return [r.w_query.at[where, span(to, q_cols)], r.w_key.at[where, span(to, kv_cols)], r.w_value.at[where, span(to, kv_cols)]]
+        return [r.w_query.at[where, span(to, q_cols)], r.w_key.at[to, where]]
+
+    def weight_to(where):
+        return [r.w_all.at[where, pl.ds(a, b - a)] for a, b in zip(ends, ends[1:])]
+
+    whole = pl.ds(0, rows)
+    mine += [local(src, dst, r.in_sem, 5 + n) for n, (src, dst) in enumerate(zip(weight_from(dp, whole), weight_to(span(dp, rows))))]
     start(mine)
     pl.semaphore_wait(barrier, dp_n + lines - 1)
 
@@ -1215,16 +1273,13 @@
     start(small)
 
     def weight_spot(src, side):
-        where = pl.ds(pl.multiple_of(src * rows + side * half, half), half)
-        return r.w_all.at[where, pl.ds(0, q_cols)], r.w_all.at[where, pl.ds(q_cols, 2 * kv_cols)]
+        return weight_to(pl.ds(pl.multiple_of(src * rows + side * half, half), half))
 
     weights = []
     for shift in pairs:
         to = peer(shift)
-        spots = weight_spot(dp, core)
-        where = span(core, half)
-        for n, src in enumerate((r.w_query.at[where, span(to, q_cols)], r.w_pair.at[to, where])):
-            weights.append(remote(src, spots[n], r.w_send, 2 * shift + n, r.w_recv, 2 * dp + n, (to, z, core)))
+        for n, (src, dst) in enumerate(zip(weight_from(to, span(core, half)), weight_spot(dp, core))):
+            weights.append(remote(src, dst, r.w_send, 3 * shift + n, r.w_recv, 3 * dp + n, (to, z, core)))
     start(weights)
 
     wait(mine[1:3])
@@ -1249,15 +1304,15 @@
     for shift in pairs:
         src = peer(shift)
         for n, spot in enumerate(weight_spot(src, core)):
-            landed(spot, r.w_recv, 2 * src + n)
-            copy = remote(spot, spot, r.w_pass, 2 * shift + n, r.w_passed, 2 * src + n, partner)
+            landed(spot, r.w_recv, 3 * src + n)
+            copy = remote(spot, spot, r.w_pass, 3 * shift + n, r.w_passed, 3 * src + n, partner)
             copy.start()
             passes.append(copy)
     wait(mine[3:])
     for shift in pairs:
         src = peer(shift)
         for n, spot in enumerate(weight_spot(src, other)):
-            landed(spot, r.w_passed, 2 * src + n)
+            landed(spot, r.w_passed, 3 * src + n)
         landed(r.tables_v.at[src], r.x_recv, 3 * src + 1)
 
     slot_of = lambda d, c: pl.ds(pl.multiple_of((2 * d + c) * tokens, tokens), tokens)
@@ -1434,8 +1489,8 @@
 def forward(x, dp_n, lines, head, collective_id):
     tokens, width = x.own_x.shape
     rows = width // dp_n
-    kv_cols = x.w_pair.shape[2] // 2
     q_cols = x.w_query.shape[1] // dp_n
+    kv_cols = x.w_value.shape[1] // dp_n
     kv_heads = kv_cols // head
     f8 = x.w_gate.shape[1] // (2 * dp_n)
     cols = q_cols + 2 * kv_cols
@@ -1462,8 +1517,8 @@
         value=vmem(all_tokens, kv_cols), q_rot=vmem(dp_n, tokens, q_cols), kv=vmem(2 * lines, dp_n, tokens, 2 * kv_cols),
         log_v=wide(dp_n, kv_heads, group_rows), mix=vmem(dp_n, tokens, q_cols), tables_v=wide(dp_n, tokens, 2 * head), gains_v=wide(8, width),
         bias_v=wide(length, tokens), w_out_v=vmem(rows, width), part=vmem(dp_n, tokens, width), land=vmem(dp_n, tokens, width),
-        hidden=wide(tokens, width), n2=vmem(tokens, width), in_sem=dma(7), out_sem=dma(14), x_send=dma(3 * dp_n), x_recv=dma(3 * dp_n),
-        w_send=dma(2 * dp_n), w_recv=dma(2 * dp_n), w_pass=dma(2 * dp_n), w_passed=dma(2 * dp_n), kv_send=dma(dp_n * lines),
+        hidden=wide(tokens, width), n2=vmem(tokens, width), in_sem=dma(8), out_sem=dma(14), x_send=dma(3 * dp_n), x_recv=dma(3 * dp_n),
+        w_send=dma(3 * dp_n), w_recv=dma(3 * dp_n), w_pass=dma(3 * dp_n), w_passed=dma(3 * dp_n), kv_send=dma(dp_n * lines),
         kv_recv=dma(dp_n * (lines + 1)), kv_pass=dma(dp_n * lines), kv_passed=dma(dp_n * lines), part_send=dma(dp_n), part_recv=dma(dp_n),
         plane_send=dma(2 * dp_n + 2), plane_recv=dma(2 * dp_n + 2), plane_pass=dma(2 * dp_n + 2), plane_passed=dma(2 * dp_n + 2),
         first_send=dma(2 * dp_n), first_recv=dma(2 * dp_n),
@@ -1496,13 +1551,9 @@
     length = stretches * half
     ctx = lax.axis_index("z") * cores + core
 
-    index = jnp.arange(rows, dtype=jnp.int32)
-    blocks = jnp.arange(stretches, dtype=jnp.int32)
-    own = 2 * ctx + index // half
-    query_places = jnp.sum(jnp.where(blocks[None, :] == own[:, None], stretch_map[None, :], 0), axis=1) * half + index % half
-    key_places = jnp.repeat(stretch_map, half, total_repeat_length=length) * half + jnp.tile(
-        jnp.arange(half, dtype=jnp.int32), stretches
-    )
+    within = jnp.arange(half, dtype=jnp.int32)
+    key_places = (stretch_map[:, None] * half + within[None, :]).reshape(length)
+    query_places = lax.dynamic_slice_in_dim(key_places, ctx * rows, rows, 0)
     bias = jnp.where(key_places[:, None] <= query_places[None, :], 0.0, MASKED_SCORE).astype(F32)
     frequency = jnp.power(F32(ROPE_BASE), -2.0 * jnp.arange(head // 2, dtype=F32) / head)
     angles = pos_ids[0].astype(F32)[:, None] * frequency[None, :]
@@ -1512,12 +1563,14 @@
     gain_piece = jnp.zeros((8, piece), F32).at[0].set(attn_gain.astype(F32)).at[1].set(ffn_gain.astype(F32))
     gain_piece = gain_piece.at[2, :head].set(q_gain.astype(F32)).at[3, :head].set(key_norm_gain.astype(F32))
     kv_cols, q_cols = key_width // dp, query_width // dp
-    w_pair = jnp.stack(
-        [jnp.concatenate([w[:, n * kv_cols : (n + 1) * kv_cols] for w in (w_key, w_value)], axis=1) for n in range(dp)]
-    )
+    if kv_cols % 128 == 0:
+        pair = (w_key, w_value)
+    else:
+        cut = [jnp.concatenate([w[:, n * kv_cols : (n + 1) * kv_cols] for w in (w_key, w_value)], axis=1) for n in range(dp)]
+        pair = (jnp.stack(cut), w_value)
     front = forward(
         FrontIn(
-            own_x=inputs[0], own_cot=cotangent[0], w_query=w_query, w_pair=w_pair, gain_piece=gain_piece, own_tables=tables,
+            own_x=inputs[0], own_cot=cotangent[0], w_query=w_query, w_key=pair[0], w_value=pair[1], gain_piece=gain_piece, own_tables=tables,
             bias=bias, w_out=w_out, w_gate=w_gate, w_up=w_up,
         ),
         dp, lines, head, 2,
@@ -1534,7 +1587,7 @@
     )
     place = lax.axis_index("dp").reshape(1)
     query_grad, key_grad, value_grad, out_grad, gate_grad, up_grad, down_grad = widen(
-        made.totals, place, dp, width, f8, q_cols + 2 * kv_cols, q_cols, kv_cols
+        made.totals, place, dp, width, f8, q_cols, kv_cols
     )
     gains = made.gain_sum
     return (

time: 753 us -> 674 us (0.90)
  Pallas kernels: 718 us -> 658 us
  other arithmetic: 16 us -> 5.47 us
    pallas_call x1, Pallas kernels: 507 us -> 472 us  [backward(): pl.pallas_call(partial(back_kernel, dims), out_shape=tuple(outs), in_spec...]
    pallas_call x2 -> x0, Pallas kernels: 15.3 us -> none  [pieces(): pl.pallas_call(kernel, grid_spec=pltpu.PrefetchScalarGridSpec(num_scalar_...]
    pallas_call x3, Pallas kernels: 42.8 us -> 34.3 us  [call(): pl.pallas_call(kernel, grid_spec=pltpu.PrefetchScalarGridSpec(num_scalar_...]
where the time goes in v4:
time: 674 us; the launch traced here: 671 us
  Pallas kernels  658 us (98%)
    pallas_call x1, Pallas kernels, backward(): pl.pallas_call(partial(back_kernel, dims), out_shape=tuple(outs), in_spec...  472 us
    pallas_call x1, Pallas kernels, forward(): pl.pallas_call(partial(front_kernel, dims), out_shape=tuple(outs), in_spe...  153 us
    pallas_call x3, Pallas kernels, call(): pl.pallas_call(kernel, grid_spec=pltpu.PrefetchScalarGridSpec(num_scalar_...  34.3 us

profile of v4, /device:TPU:0, one launch (start us, length us, event | category | flops | bytes accessed | tf_op | source)
XLA Modules:
  0.0 670.6 jit_solution(10960556618011827920)
XLA Ops:
  0.7 0.7 broadcast_multiply_fusion
  1.3 0.1 iota_add_fusion
  1.4 0.1 add.44
  1.5 0.1 dynamic_slice.13
  1.5 1.0 compare_select_fusion.refs_7_.refs_15_
  2.5 0.7 convert_bitcast_fusion
  3.2 0.3 multiply_cosine_fusion
  3.5 0.8 pad_maximum_fusion.refs_6_
  4.3 0.7 reshape.182
  5.0 0.7 convert.15
  5.7 0.7 bitcast_convert_fusion.1
  6.3 0.1 scatter.25
  6.5 0.7 bitcast_convert_fusion
  7.1 0.1 scatter.26.refs_5_
  7.2 0.0 copy-start.2
  7.3 0.6 copy-done.2
  7.9 152.6 %forward.1 = (bf16[1024,2048]{1,0:T(8,128)(2,1)}, bf16[1024,2048]{1,0:T(8,128)(2,1)}, bf16[2048,512]{1,0:T(8,128)(2,1)}, f32[128,2048]{1,0:T(8,128)}, bf16[2048,...) custom-call(bf16[128,2048]{1,0:T(8,128)(2,1)} %bitcast.28, ...), custom_call_target="tpu_custom_call" | custom-call | flops 10000000000 | bytes 52428800 | tf_op jit(solution)/shard_map/forward/pallas_call | solution.py:1527
  160.5 471.5 %backward.1 = (bf16[128,2048]{1,0:T(8,128)(2,1)}, bf16[128,2048]{1,0:T(8,128)(2,1)}, f32[8,2048]{1,0:T(8,128)}, bf16[2,29,512,512]{3,2,1,0:T(8,128)(2,1)}, bf16[...) custom-call(bf16[1024,2048]{1,0:T(8,128)(2,1)} %get-tuple-element.84, ...), custom_call_target="tpu_custom_call" | custom-call | flops 38654705664 | bytes 104857600 | tf_op jit(solution)/shard_map/backward/pallas_call | solution.py:1034
  632.0 18.1 %widen_gate_up.1 = (f32[512,8192]{1,0:T(8,128)}, f32[512,8192]{1,0:T(8,128)}) custom-call(s32[1]{0:T(128)} %bitcast.11.place, bf16[2,29,512,512]{3,2,1,0:T(8,128)(2,1)} %get-tuple-element.100.refs_0_.refs_1_.refs_2_.refs_3_.refs_4_, bf16[2,29,512,512]{3,2,1,0:T(8,128)(2,1)} %get-tuple-element.100.refs_0_.refs_1_.refs_2_.refs_3_.refs_4_, ...), custom_call_target="tpu_custom_call" | custom-call | tf_op jit(solution)/shard_map/widen_gate_up/pallas_call | solution.py:1095
  650.1 10.2 %widen_down.1 = f32[2048,2048]{1,0:T(8,128)} custom-call(s32[1]{0:T(128)} %bitcast.11.place, bf16[2,29,512,512]{3,2,1,0:T(8,128)(2,1)} %get-tuple-element.100.refs_0_.refs_1_.refs_2_.refs_3_.refs_4_, bf16[2,29,512,512]{3,2,1,0:T(8,128)(2,1)} %get-tuple-element.100.refs_0_.refs_1_.refs_2_.refs_3_.refs_4_), custom_call_target="tpu_custom_call" | custom-call | tf_op jit(solution)/shard_map/widen_down/pallas_call | solution.py:1095
  660.4 0.0 copy-start.1
  660.4 0.0 copy-start
  660.4 5.9 widen_heads.1
  666.3 0.9 fusion.1
  667.2 0.6 constant_dynamic-slice_fusion
  667.8 1.3 slice_bitcast_fusion
  669.1 0.0 copy-done.1
  669.1 0.8 copy.34
  669.8 0.0 copy-done
  669.9 0.8 copy.35
  (3 shorter events, 0.1 us)
Async XLA Ops:
  7.2 0.6 copy-start.2
  660.4 8.7 %copy-start.1 = (bf16[128,2048]{1,0:T(8,128)(2,1)S(1)}, bf16[128,2048]{1,0:T(8,128)(2,1)}, u32[]{:S(2)}) copy-start(bf16[128,2048]{1,0:T(8,128)(2,1)} %get-tuple-element.97) | copy-start | bytes 1572868
  660.4 9.5 %copy-start = (bf16[128,2048]{1,0:T(8,128)(2,1)S(1)}, bf16[128,2048]{1,0:T(8,128)(2,1)}, u32[]{:S(2)}) copy-start(bf16[128,2048]{1,0:T(8,128)(2,1)} %get-tuple-element.98) | copy-start | bytes 1572868

commit v5 on v4

--- a/solution.py
+++ b/solution.py
@@ -57,8 +57,8 @@
         self.quarter = self.rows // 4
         self.half = self.rows // 2
         self.ahead = 4
-        self.lag = 7 + 3 * (self.middle - self.place)
-        self.most = 7 + 3 * self.middle + 3
+        self.lag = 7 + 4 * (self.middle - self.place)
+        self.most = 7 + 4 * self.middle + 3
         self.n_ffn = self.n_blocks * self.per_block
         self.q_first = self.n_ffn + 2
         self.piece = self.qkv_cols // 3
@@ -262,7 +262,7 @@
 
         steps = self.middle - self.place
 
-        @upto(7 + 3 * steps, 3 + 2 * steps)
+        @upto(7 + 4 * steps, 3 + 2 * steps)
         def _(k):
             @pl.when(jnp.logical_not(at_middle & self.ours(k)))
             def _():
@@ -517,18 +517,21 @@
 
                 for j in range(down_block):
                     to_own(j).start()
+                for j in range(down_block):
+                    to_own(j).wait()
+                line.advance_at(b * 2, 1)
 
                 @pl.loop(0, dp_n)
                 def _(shift):
                     stage[down_block + shift] = contract_rows(n2[:, span(peer(shift), rows)], grads[b]).astype(BF16)
                     to_own(down_block + shift).start()
 
-                @pl.loop(0, per_block)
+                @pl.loop(down_block, per_block)
                 def _(j):
                     to_own(j).wait()
 
 
-                line.advance_at(b * 2, 2)
+                line.advance_at(b * 2 + 1, 1)
 
         pl.run_scoped(blocks, pltpu.VMEM((plane, width), BF16), pltpu.VMEM((plane, width), BF16))
         line.position = n_blocks * 2

time: 674 us -> 665 us (0.987)
  Pallas kernels: 658 us -> 647 us
    pallas_call x1, Pallas kernels: 472 us -> 460 us  [backward(): pl.pallas_call(partial(back_kernel, dims), out_shape=tuple(outs), in_spec...]
where the time goes in v5:
time: 665 us; the launch traced here: 659 us
  Pallas kernels  647 us (97%)
    pallas_call x1, Pallas kernels, backward(): pl.pallas_call(partial(back_kernel, dims), out_shape=tuple(outs), in_spec...  460 us
    pallas_call x1, Pallas kernels, forward(): pl.pallas_call(partial(front_kernel, dims), out_shape=tuple(outs), in_spe...  153 us
    pallas_call x3, Pallas kernels, call(): pl.pallas_call(kernel, grid_spec=pltpu.PrefetchScalarGridSpec(num_scalar_...  34.3 us

profile of v5, /device:TPU:0, one launch (start us, length us, event | category | flops | bytes accessed | tf_op | source)
XLA Modules:
  0.0 658.8 jit_solution(5986076740055284566)
XLA Ops:
  0.7 0.7 broadcast_multiply_fusion
  1.3 0.1 iota_add_fusion
  1.4 0.1 add.44
  1.5 0.1 dynamic_slice.13
  1.5 1.0 compare_select_fusion.refs_7_.refs_15_
  2.5 0.7 convert_bitcast_fusion
  3.2 0.3 multiply_cosine_fusion
  3.5 0.8 pad_maximum_fusion.refs_6_
  4.3 0.7 reshape.182
  5.0 0.7 convert.15
  5.7 0.7 bitcast_convert_fusion.1
  6.3 0.1 scatter.25
  6.5 0.7 bitcast_convert_fusion
  7.1 0.1 scatter.26.refs_5_
  7.2 0.0 copy-start.2
  7.3 0.6 copy-done.2
  7.9 152.6 %forward.1 = (bf16[1024,2048]{1,0:T(8,128)(2,1)}, bf16[1024,2048]{1,0:T(8,128)(2,1)}, bf16[2048,512]{1,0:T(8,128)(2,1)}, f32[128,2048]{1,0:T(8,128)}, bf16[2048,...) custom-call(bf16[128,2048]{1,0:T(8,128)(2,1)} %bitcast.28, ...), custom_call_target="tpu_custom_call" | custom-call | flops 10000000000 | bytes 52428800 | tf_op jit(solution)/shard_map/forward/pallas_call | solution.py:1530
  160.5 459.7 %backward.1 = (bf16[128,2048]{1,0:T(8,128)(2,1)}, bf16[128,2048]{1,0:T(8,128)(2,1)}, f32[8,2048]{1,0:T(8,128)}, bf16[2,29,512,512]{3,2,1,0:T(8,128)(2,1)}, bf16[...) custom-call(bf16[1024,2048]{1,0:T(8,128)(2,1)} %get-tuple-element.84, ...), custom_call_target="tpu_custom_call" | custom-call | flops 38654705664 | bytes 104857600 | tf_op jit(solution)/shard_map/backward/pallas_call | solution.py:1037
  620.2 18.1 %widen_gate_up.1 = (f32[512,8192]{1,0:T(8,128)}, f32[512,8192]{1,0:T(8,128)}) custom-call(s32[1]{0:T(128)} %bitcast.11.place, bf16[2,29,512,512]{3,2,1,0:T(8,128)(2,1)} %get-tuple-element.100.refs_0_.refs_1_.refs_2_.refs_3_.refs_4_, bf16[2,29,512,512]{3,2,1,0:T(8,128)(2,1)} %get-tuple-element.100.refs_0_.refs_1_.refs_2_.refs_3_.refs_4_, ...), custom_call_target="tpu_custom_call" | custom-call | tf_op jit(solution)/shard_map/widen_gate_up/pallas_call | solution.py:1098
  638.3 10.2 %widen_down.1 = f32[2048,2048]{1,0:T(8,128)} custom-call(s32[1]{0:T(128)} %bitcast.11.place, bf16[2,29,512,512]{3,2,1,0:T(8,128)(2,1)} %get-tuple-element.100.refs_0_.refs_1_.refs_2_.refs_3_.refs_4_, bf16[2,29,512,512]{3,2,1,0:T(8,128)(2,1)} %get-tuple-element.100.refs_0_.refs_1_.refs_2_.refs_3_.refs_4_), custom_call_target="tpu_custom_call" | custom-call | tf_op jit(solution)/shard_map/widen_down/pallas_call | solution.py:1098
  648.5 0.0 copy-start.1
  648.5 0.0 copy-start
  648.5 5.9 widen_heads.1
  654.5 0.9 fusion.1
  655.4 0.6 constant_dynamic-slice_fusion
  656.0 1.3 slice_bitcast_fusion
  657.2 0.0 copy-done.1
  657.2 0.8 copy.34
  658.0 0.0 copy-done
  658.0 0.8 copy.35
  (3 shorter events, 0.1 us)
Async XLA Ops:
  7.2 0.6 copy-start.2
  648.5 8.7 %copy-start.1 = (bf16[128,2048]{1,0:T(8,128)(2,1)S(1)}, bf16[128,2048]{1,0:T(8,128)(2,1)}, u32[]{:S(2)}) copy-start(bf16[128,2048]{1,0:T(8,128)(2,1)} %get-tuple-element.97) | copy-start | bytes 1572868
  648.5 9.5 %copy-start = (bf16[128,2048]{1,0:T(8,128)(2,1)S(1)}, bf16[128,2048]{1,0:T(8,128)(2,1)}, u32[]{:S(2)}) copy-start(bf16[128,2048]{1,0:T(8,128)(2,1)} %get-tuple-element.98) | copy-start | bytes 1572868

commit v6 on v5

--- a/solution.py
+++ b/solution.py
@@ -57,8 +57,8 @@
         self.quarter = self.rows // 4
         self.half = self.rows // 2
         self.ahead = 4
-        self.lag = 7 + 4 * (self.middle - self.place)
-        self.most = 7 + 4 * self.middle + 3
+        self.lag = 7 + 6 * (self.middle - self.place)
+        self.most = 7 + 6 * self.middle + 3
         self.n_ffn = self.n_blocks * self.per_block
         self.q_first = self.n_ffn + 2
         self.piece = self.qkv_cols // 3
@@ -262,7 +262,7 @@
 
         steps = self.middle - self.place
 
-        @upto(7 + 4 * steps, 3 + 2 * steps)
+        @upto(7 + 6 * steps, 3 + 2 * steps)
         def _(k):
             @pl.when(jnp.logical_not(at_middle & self.ours(k)))
             def _():

time: 665 us -> 662 us (level)
  no operation moved by 1% of the time
where the time goes in v6:
time: 662 us; the launch traced here: 659 us
  Pallas kernels  647 us (98%)
    pallas_call x1, Pallas kernels, backward(): pl.pallas_call(partial(back_kernel, dims), out_shape=tuple(outs), in_spec...  460 us
    pallas_call x1, Pallas kernels, forward(): pl.pallas_call(partial(front_kernel, dims), out_shape=tuple(outs), in_spe...  153 us
    pallas_call x3, Pallas kernels, call(): pl.pallas_call(kernel, grid_spec=pltpu.PrefetchScalarGridSpec(num_scalar_...  34.3 us

profile of v6, /device:TPU:0, one launch (start us, length us, event | category | flops | bytes accessed | tf_op | source)
XLA Modules:
  0.0 658.8 jit_solution(17359410254520230569)
XLA Ops:
  0.7 0.7 broadcast_multiply_fusion
  1.3 0.1 iota_add_fusion
  1.4 0.1 add.44
  1.5 0.1 dynamic_slice.13
  1.5 1.0 compare_select_fusion.refs_7_.refs_15_
  2.5 0.7 convert_bitcast_fusion
  3.2 0.3 multiply_cosine_fusion
  3.5 0.8 pad_maximum_fusion.refs_6_
  4.3 0.7 reshape.182
  5.0 0.7 convert.15
  5.7 0.7 bitcast_convert_fusion.1
  6.3 0.1 scatter.25
  6.5 0.7 bitcast_convert_fusion
  7.1 0.1 scatter.26.refs_5_
  7.2 0.0 copy-start.2
  7.3 0.6 copy-done.2
  7.9 152.6 %forward.1 = (bf16[1024,2048]{1,0:T(8,128)(2,1)}, bf16[1024,2048]{1,0:T(8,128)(2,1)}, bf16[2048,512]{1,0:T(8,128)(2,1)}, f32[128,2048]{1,0:T(8,128)}, bf16[2048,...) custom-call(bf16[128,2048]{1,0:T(8,128)(2,1)} %bitcast.28, ...), custom_call_target="tpu_custom_call" | custom-call | flops 10000000000 | bytes 52428800 | tf_op jit(solution)/shard_map/forward/pallas_call | solution.py:1530
  160.5 459.7 %backward.1 = (bf16[128,2048]{1,0:T(8,128)(2,1)}, bf16[128,2048]{1,0:T(8,128)(2,1)}, f32[8,2048]{1,0:T(8,128)}, bf16[2,29,512,512]{3,2,1,0:T(8,128)(2,1)}, bf16[...) custom-call(bf16[1024,2048]{1,0:T(8,128)(2,1)} %get-tuple-element.84, ...), custom_call_target="tpu_custom_call" | custom-call | flops 38654705664 | bytes 104857600 | tf_op jit(solution)/shard_map/backward/pallas_call | solution.py:1037
  620.2 18.1 %widen_gate_up.1 = (f32[512,8192]{1,0:T(8,128)}, f32[512,8192]{1,0:T(8,128)}) custom-call(s32[1]{0:T(128)} %bitcast.11.place, bf16[2,29,512,512]{3,2,1,0:T(8,128)(2,1)} %get-tuple-element.100.refs_0_.refs_1_.refs_2_.refs_3_.refs_4_, bf16[2,29,512,512]{3,2,1,0:T(8,128)(2,1)} %get-tuple-element.100.refs_0_.refs_1_.refs_2_.refs_3_.refs_4_, ...), custom_call_target="tpu_custom_call" | custom-call | tf_op jit(solution)/shard_map/widen_gate_up/pallas_call | solution.py:1098
  638.3 10.2 %widen_down.1 = f32[2048,2048]{1,0:T(8,128)} custom-call(s32[1]{0:T(128)} %bitcast.11.place, bf16[2,29,512,512]{3,2,1,0:T(8,128)(2,1)} %get-tuple-element.100.refs_0_.refs_1_.refs_2_.refs_3_.refs_4_, bf16[2,29,512,512]{3,2,1,0:T(8,128)(2,1)} %get-tuple-element.100.refs_0_.refs_1_.refs_2_.refs_3_.refs_4_), custom_call_target="tpu_custom_call" | custom-call | tf_op jit(solution)/shard_map/widen_down/pallas_call | solution.py:1098
  648.5 0.0 copy-start.1
  648.5 0.0 copy-start
  648.5 5.9 widen_heads.1
  654.5 0.9 fusion.1
  655.4 0.6 constant_dynamic-slice_fusion
  656.0 1.3 slice_bitcast_fusion
  657.2 0.0 copy-done.1
  657.2 0.8 copy.34
  658.0 0.0 copy-done
  658.0 0.8 copy.35
  (3 shorter events, 0.1 us)
Async XLA Ops:
  7.2 0.6 copy-start.2
  648.5 8.7 %copy-start.1 = (bf16[128,2048]{1,0:T(8,128)(2,1)S(1)}, bf16[128,2048]{1,0:T(8,128)(2,1)}, u32[]{:S(2)}) copy-start(bf16[128,2048]{1,0:T(8,128)(2,1)} %get-tuple-element.97) | copy-start | bytes 1572868
  648.5 9.5 %copy-start = (bf16[128,2048]{1,0:T(8,128)(2,1)S(1)}, bf16[128,2048]{1,0:T(8,128)(2,1)}, u32[]{:S(2)}) copy-start(bf16[128,2048]{1,0:T(8,128)(2,1)} %get-tuple-element.98) | copy-start | bytes 1572868
